TPU v7x, 32 devices: a whole 2x2x4 slice. The times are simulated.
32 devices in a mesh: gx: 4 (over x, core), gy: 4 (over z), gz: 2 (over y).
Axes of the slice: x: 2, y: 2, z: 4, core: 2. Of those that a mesh axis runs over, the one named last changes fastest.
Arguments:
- offsets: float32 [3, 131072], P(None, ('gx', 'gy', 'gz')), may hold values from -0.5 to 0.5
- velocity: float32 [3, 131072], P(None, ('gx', 'gy', 'gz')), may hold values from -6 to 6
- affine: float32 [9, 131072], P(None, ('gx', 'gy', 'gz')), may hold values from -6 to 6
- volume: float32 [131072], P(('gx', 'gy', 'gz')), may hold values from 0.8 to 1.2
- cot_velocity: float32 [3, 131072], P(None, ('gx', 'gy', 'gz')), may hold values from -6 to 6
- cot_affine: float32 [9, 131072], P(None, ('gx', 'gy', 'gz')), may hold values from -3 to 3
- block_cells: int32 [1024], P(('gx', 'gy', 'gz')), may hold values from 0 to 511
- fill_counts: int32 [32], P(('gx', 'gy', 'gz')), may hold values from 2 to 32, as said below
- baffle_top: int32 [128, 128], P('gx', 'gy'), may hold values from 0 to 16
- drag: float32 [128, 128, 16], P('gx', 'gy', 'gz'), may hold values from 0.2 to 0.9
Outputs:
- grad_velocity: float32 [3, 131072], P(None, ('gx', 'gy', 'gz'))
- grad_affine: float32 [9, 131072], P(None, ('gx', 'gy', 'gz'))
- grad_volume: float32 [131072], P(('gx', 'gy', 'gz'))
- grad_drag: float32 [128, 128, 16], P('gx', 'gy', 'gz')
Inputs may be any that keep to these rules, and one draw needn't show every extreme that they name: Blocks 0 to fill_counts - 1 of a device are live, its other slots are padding; in every draw some device has all 32 blocks live.
All inputs are finite; a program needn't handle non-finite values.
Results may differ from a plain program's by a relative error of at most 0.00011.
Values sent between devices are 32-bit elements; how exact they have to be, the bound alone decides.
No kernel may reach another device: no remote copies, remote signals or barrier semaphores. Data moves between devices by JAX's collectives and lax.ppermute only.
A program may use at most 64 MiB of HBM per device.

v0:
```python
import jax
import jax.numpy as jnp
from jax import lax
from jax.sharding import PartitionSpec as P

stiffness = 2.0
gravity_step = 0.3


def extended_2(block, sides, width):
    for axis, dim in sides:
        count = lax.axis_size(axis)
        forward = [(i, i + 1) for i in range(count - 1)]
        backward = [(target, source) for source, target in forward]
        low = lax.ppermute(
            lax.slice_in_dim(block, block.shape[dim] - width, None, axis=dim), axis, forward
        )
        high = lax.ppermute(lax.slice_in_dim(block, 0, width, axis=dim), axis, backward)
        block = jnp.concatenate([low, block, high], axis=dim)
    return block


def node_window():
    node_ids = jnp.arange(96, dtype=jnp.int32)
    return jnp.stack([node_ids // 24 - 1, node_ids // 6 % 4 - 1, node_ids % 6 - 1])


def local_cells(per_rows):
    cell_ids = jnp.arange(per_rows, dtype=jnp.int32) // 8
    return jnp.stack([cell_ids // 8, cell_ids // 4 % 2, cell_ids % 4])


def axis_weights(frac, local, span):
    spline = jnp.stack([0.5 * (0.5 - frac) ** 2, 0.75 - frac * frac, 0.5 * (0.5 + frac) ** 2])
    window_ids = jnp.arange(span, dtype=jnp.int32)[:, None, None]
    targets = local[None, None, :] + jnp.arange(3, dtype=jnp.int32)[None, :, None]
    hits = (window_ids == targets).astype(jnp.float32)
    return jnp.sum(hits[:, :, None, :] * spline[None], axis=1)


def block_weights(position):
    local = local_cells(position.shape[2])
    weight_x = axis_weights(position[0], local[0], 4)
    weight_y = axis_weights(position[1], local[1], 4)
    weight_z = axis_weights(position[2], local[2], 6)
    product = weight_x[:, None, None] * weight_y[None, :, None] * weight_z[None, None, :]
    return product.reshape((96,) + position.shape[1:])


def shifted(position):
    return position + local_cells(position.shape[2]).astype(jnp.float32)[:, None, :]


def forward_terms(position, speeds, matrices, ratios, alive):
    block_count, per_rows = (position.shape[1], position.shape[2])
    weight = block_weights(position)
    placed = shifted(position)
    alive_rows = alive[:, None]
    identity = jnp.eye(3, dtype=jnp.float32).reshape(9)[:, None, None]
    stress = alive_rows * (matrices - stiffness * (ratios - 1.0) * identity)
    linear = alive_rows * speeds - jnp.sum(
        stress.reshape(3, 3, block_count, per_rows) * placed[None], axis=1
    )
    masses = jnp.broadcast_to(alive_rows[None], (1, block_count, per_rows))
    stacked = jnp.concatenate([masses, linear, stress], axis=0)
    node_sums = jnp.einsum("nkp,ckp->ckn", weight, stacked, precision=lax.Precision.HIGHEST)
    offset_table = node_window().astype(jnp.float32)
    momentum = node_sums[1:4] + jnp.einsum(
        "abkn,bn->akn",
        node_sums[4:].reshape(3, 3, block_count, 96),
        offset_table,
        precision=lax.Precision.HIGHEST,
    )
    return jnp.concatenate([node_sums[:1], momentum], axis=0)


def adjoint_terms(position, cot_speeds, cot_matrices, alive):
    block_count, per_rows = (position.shape[1], position.shape[2])
    weight = block_weights(position)
    placed = shifted(position)
    alive_rows = alive[:, None]
    linear = alive_rows * (
        cot_speeds
        - 4.0 * jnp.sum(cot_matrices.reshape(3, 3, block_count, per_rows) * placed[None], axis=1)
    )
    scaled = 4.0 * alive_rows * cot_matrices
    stacked = jnp.concatenate([linear, scaled], axis=0)
    node_sums = jnp.einsum("nkp,ckp->ckn", weight, stacked, precision=lax.Precision.HIGHEST)
    offset_table = node_window().astype(jnp.float32)
    return node_sums[:3] + jnp.einsum(
        "abkn,bn->akn",
        node_sums[3:].reshape(3, 3, block_count, 96),
        offset_table,
        precision=lax.Precision.HIGHEST,
    )


def pull_back(position, gathered, alive):
    block_count, per_rows = (position.shape[1], position.shape[2])
    weight = block_weights(position)
    placed = shifted(position)
    alive_rows = alive[:, None]
    offset_table = node_window().astype(jnp.float32)
    spread = (gathered[:, None] * offset_table[None, :, None, :]).reshape(9, block_count, 96)
    stacked = jnp.concatenate([gathered, spread], axis=0)
    pulled = jnp.einsum("nkp,ckn->ckp", weight, stacked, precision=lax.Precision.HIGHEST)
    speed_grad = alive_rows * pulled[:3]
    matrix_grad = (
        alive_rows
        * (pulled[3:].reshape(3, 3, block_count, per_rows) - pulled[:3][:, None] * placed[None])
    ).reshape(9, block_count, per_rows)
    ratio_grad = -stiffness * (matrix_grad[0] + matrix_grad[4] + matrix_grad[8])
    return jnp.concatenate([speed_grad, matrix_grad, ratio_grad[None]], axis=0)


def fold_axis(extended, axis):
    inner = extended.shape[axis] - 4
    middle = lax.slice_in_dim(extended, 2, inner + 2, axis=axis)
    lower = lax.slice_in_dim(extended, 0, 1, axis=axis)
    upper = lax.slice_in_dim(extended, inner + 3, inner + 4, axis=axis)
    lower_pads = [(0, 0)] * extended.ndim
    upper_pads = [(0, 0)] * extended.ndim
    lower_pads[axis] = (0, inner - 1)
    upper_pads[axis] = (inner - 1, 0)
    return middle + jnp.pad(lower, lower_pads) + jnp.pad(upper, upper_pads)


def fold_all(extended):
    return fold_axis(fold_axis(fold_axis(extended, 1), 2), 3)


def shards(
    offsets,
    velocity,
    affine,
    volume,
    cot_velocity,
    cot_affine,
    block_cells,
    fill_counts,
    baffle_top,
    drag,
):
    size_x, size_y, size_z = drag.shape
    nblocks = block_cells.shape[0]
    per_block = offsets.shape[1] // nblocks
    pad_x, pad_y, pad_z = (size_x + 2, size_y + 2, size_z + 2)
    node_steps = node_window()
    node_shift = node_steps[0] * (pad_y * pad_z) + node_steps[1] * pad_z + node_steps[2]
    tiles_y = size_y // 2
    tiles_z = size_z // 4
    row_x = 2 * (block_cells // (tiles_y * tiles_z))
    row_y = 2 * (block_cells // tiles_z % tiles_y)
    row_z = 4 * (block_cells % tiles_z)
    center = ((row_x + 1) * pad_y + row_y + 1) * pad_z + row_z + 1
    node_index = center[:, None] + node_shift[None, :]
    live_blocks = (jnp.arange(nblocks, dtype=jnp.int32) < fill_counts[0]).astype(jnp.float32)
    volume_rows = volume[None]

    def block_rows(array, block_count):
        return array.reshape(array.shape[0], block_count, per_block)

    cells_padded = pad_x * pad_y * pad_z
    empty_grid = jnp.zeros((7, cells_padded), jnp.float32)
    node_rows = node_index.reshape(-1)
    alive = live_blocks
    position = block_rows(offsets, nblocks)
    moments = forward_terms(
        position,
        block_rows(velocity, nblocks),
        block_rows(affine, nblocks),
        block_rows(volume_rows, nblocks)[0],
        alive,
    )
    adjoint = adjoint_terms(
        position, block_rows(cot_velocity, nblocks), block_rows(cot_affine, nblocks), alive
    )
    joined_terms = jnp.concatenate([moments, adjoint], axis=0).reshape(7, -1)
    grid_all = empty_grid.at[:, node_rows].add(joined_terms)
    grid_pad = grid_all.reshape(7, pad_x, pad_y, pad_z)
    moments = fold_all(extended_2(grid_pad[:4], (("gx", 1), ("gy", 2), ("gz", 3)), 1))
    node_adjoint = fold_all(extended_2(grid_pad[4:], (("gx", 1), ("gy", 2), ("gz", 3)), 1))
    mass_floor = jnp.maximum(moments[0], 1.0)
    gravity = jnp.array([0.0, 0.0, -gravity_step], dtype=jnp.float32)[:, None, None, None]
    grid_velocity = moments[1:4] / mass_floor[None] + gravity
    depth_index = lax.axis_index("gz") * size_z + jnp.arange(size_z, dtype=jnp.int32)
    baffle = (depth_index[None, None, :] < baffle_top[:, :, None]).astype(jnp.float32)
    grad_drag = -baffle * jnp.sum(node_adjoint * grid_velocity, axis=0)
    node_grad = node_adjoint * (1.0 - baffle * drag)[None] / mass_floor[None]
    beside_all = extended_2(node_grad, (("gx", 1), ("gy", 2), ("gz", 3)), 1).reshape(3, -1)
    node_rows = node_index
    alive = live_blocks
    gathered = beside_all[:, node_rows]
    results = pull_back(block_rows(offsets, nblocks), gathered, alive).reshape(13, -1)
    return (results[:3], results[3:12], results[12], grad_drag)


def solution(mesh):
    in_specs = (
        P(None, ("gx", "gy", "gz")),
        P(None, ("gx", "gy", "gz")),
        P(None, ("gx", "gy", "gz")),
        P(("gx", "gy", "gz")),
        P(None, ("gx", "gy", "gz")),
        P(None, ("gx", "gy", "gz")),
        P(("gx", "gy", "gz")),
        P(("gx", "gy", "gz")),
        P("gx", "gy"),
        P("gx", "gy", "gz"),
    )
    out_specs = (
        P(None, ("gx", "gy", "gz")),
        P(None, ("gx", "gy", "gz")),
        P(("gx", "gy", "gz")),
        P("gx", "gy", "gz"),
    )
    return jax.shard_map(shards, mesh=mesh, in_specs=in_specs, out_specs=out_specs, check_vma=False)
```

profile of v0, /device:TPU:0, one launch (start us, length us, event | category | flops | bytes accessed | tf_op | source)
XLA Modules:
  0.0 194.3 jit_solution(5716723758724008997)
XLA Ops:
  6.6 3.3 %fusion.8 = f32[13,32,96]{2,0,1:T(8,128)S(1)} fusion(f32[96,32,128]{2,1,0:T(8,128)S(1)} %bitcast.87, f32[13,32,128]{2,1,0:T(8,128)S(1)} %pad_maximum_fusion.5), kind=kOutput, calls=%fused_computation.10 | convolution fusion | flops 61341696 | bytes 1945600 | tf_op jit(solution)/shard_map/nkp,ckp->ckn/dot_general | solution.py:66
  10.0 3.3 %fusion.11 = f32[12,32,96]{2,0,1:T(8,128)S(1)} fusion(f32[96,32,128]{2,1,0:T(8,128)S(1)} %bitcast.88, f32[12,32,128]{2,1,0:T(8,128)S(1)} %pad_maximum_fusion.6), kind=kOutput, calls=%fused_computation.11 | convolution fusion | flops 56623104 | bytes 1916928 | tf_op jit(solution)/shard_map/nkp,ckp->ckn/dot_general | solution.py:88
  15.6 19.8 %scatter_custom_fusion = f32[7,11560]{0,1:T(8,128)} fusion(s32[3072]{0:T(1024)S(1)} %bitcast.120, f32[3072,7]{1,0:T(8,128)S(1)} %copy.243, f32[]{:T(128)} %constant.256.clone.1), kind=kCustom, calls=%fused_computation.2 | custom fusion | flops 21504 | bytes 323684 | tf_op jit(solution)/shard_map/scatter-add | solution.py:179
  35.4 5.2 %slice.255 = f32[3,11560]{0,1:T(8,128)} slice(f32[7,11560]{0,1:T(8,128)} %scatter_custom_fusion), slice={[4:7], [0:11560]} | slice | bytes 277440 | tf_op jit(solution)/shard_map/slice | solution.py:182
  40.6 4.4 %copy.244 = f32[3,11560]{1,0:T(4,128)S(1)} copy(f32[3,11560]{0,1:T(8,128)} %slice.255) | data formatting | bytes 277440 | tf_op jit(solution)/shard_map/slice | solution.py:182
  45.0 2.4 %slice.200 = f32[3,34,34,10]{3,2,1,0:T(8,128)} reshape(f32[3,11560]{1,0:T(4,128)S(1)} %copy.244) | data formatting | bytes 277440 | tf_op jit(solution)/shard_map/slice | solution.py:182
  47.4 2.4 %copy.245 = f32[3,34,34,10]{2,3,1,0:T(8,128)S(1)} copy(f32[3,34,34,10]{3,2,1,0:T(8,128)} %slice.200) | data formatting | bytes 277440 | tf_op jit(solution)/shard_map/slice | solution.py:182
  50.5 2.3 %collective-permute-start = (f32[3,1,34,10]{2,3,1,0:T(8,128)}, f32[3,1,34,10]{2,3,1,0:T(8,128)S(1)}, u32[]{:S(2)}, u32[]{:S(2)}) collective-permute-start(f32[3,1,34,10]{2,3,1,0:T(8,128)} %get-tuple-element.44), channel_id=1, source_target_pairs={{0,8},{8,16},{16,24},{1,9},{9,17},{17,25},{2,10},{10,18},{18,26},{... | collective-permute-start | bytes 12248 | tf_op jit(solution)/shard_map/ppermute | solution.py:15
  52.8 1.3 collective-permute-start.1
  54.1 4.4 %copy.254 = f32[4,11560]{1,0:T(4,128)S(1)} copy(f32[4,11560]{0,1:T(8,128)} %bitcast.86) | data formatting | bytes 369920 | tf_op jit(solution)/shard_map/slice | solution.py:181
  58.6 2.9 %slice.217 = f32[4,34,34,10]{3,2,1,0:T(8,128)} reshape(f32[4,11560]{1,0:T(4,128)S(1)} %copy.254) | data formatting | bytes 369920 | tf_op jit(solution)/shard_map/slice | solution.py:181
  61.5 1.6 fusion.79
  63.1 5.8 %collective-permute-start.6 = (f32[4,1,34,10]{3,2,1,0:T(8,128)}, f32[4,1,34,10]{3,2,1,0:T(8,128)}, u32[]{:S(2)}, u32[]{:S(2)}) collective-permute-start(f32[4,1,34,10]{3,2,1,0:T(8,128)} %get-tuple-element.31), channel_id=1, source_target_pairs={{0,8},{8,16},{16,24},{1,9},{9,17},{17,25},{2,10},{10,18},{18,26},{... | collective-permute-start | bytes 16328 | tf_op jit(solution)/shard_map/ppermute | solution.py:15
  68.8 1.3 collective-permute-start.7
  73.3 1.5 copy.248
  74.8 3.5 %collective-permute-start.2 = (f32[3,36,1,10]{1,2,3,0:T(1,128)S(1)}, f32[3,36,1,10]{1,2,3,0:T(1,128)S(1)}, u32[]{:S(2)}, u32[]{:S(2)}) collective-permute-start(f32[3,36,1,10]{1,2,3,0:T(1,128)S(1)} %copy.248), channel_id=1, source_target_pairs={{0,2},{2,4},{4,6},{1,3},{3,5},{5,7},{8,10},{10,12},{12,14},{9,11},... | collective-permute-start | bytes 12968 | tf_op jit(solution)/shard_map/ppermute | solution.py:15
  79.2 1.3 collective-permute-start.3
  81.4 2.0 %constant_dynamic-update-slice_fusion.1 = f32[4,36,34,10]{3,2,1,0:T(8,128)S(1)} fusion(f32[4,36,34,10]{3,2,1,0:T(8,128)S(1)} %constant_dynamic-update-slice_fusion.2, f32[4,34,34,10]{3,2,1,0:T(8,128)} %slice.217), kind=kLoop, calls=%fused_computation.134 | loop fusion | bytes 2970240
  84.3 1.6 copy-done.4
  86.6 3.3 %copy.256 = f32[4,36,34,10]{2,0,3,1:T(4,128)} copy(f32[4,36,34,10]{3,2,1,0:T(8,128)} %copy-done.4) | data formatting | bytes 391680 | tf_op jit(solution)/shard_map/concatenate | solution.py:19
  90.0 5.2 %collective-permute-start.8 = (f32[4,36,1,10]{3,2,1,0:T(1,128)}, f32[4,36,1,10]{3,2,1,0:T(1,128)}, u32[]{:S(2)}, u32[]{:S(2)}) collective-permute-start(f32[4,36,1,10]{3,2,1,0:T(1,128)} %get-tuple-element.28), channel_id=1, source_target_pairs={{0,2},{2,4},{4,6},{1,3},{3,5},{5,7},{8,10},{10,12},{12,14},{9,11},... | collective-permute-start | bytes 17288 | tf_op jit(solution)/shard_map/ppermute | solution.py:15
  95.1 1.3 collective-permute-start.9
  97.0 2.1 %copy.251 = f32[3,36,1,10]{2,3,1,0:T(8,128)} copy(f32[3,36,1,10]{1,2,3,0:T(1,128)} %collective-permute-done.3) | data formatting | bytes 8640 | tf_op jit(solution)/shard_map/ppermute | solution.py:18
  99.1 2.3 %pad_maximum_fusion.15 = (f32[3,36,36,1]{2,3,1,0:T(1,128)}, f32[3,36,36,1]{2,3,1,0:T(1,128)}) fusion(f32[3,36,1,10]{2,3,1,0:T(8,128)} %copy.251, f32[3,36,1,10]{2,3,1,0:T(8,128)S(1)} %copy.250, f32[3,1,34,10]{2,3,1,0:T(8,128)S(1)} %collective-permute-done.1, f32[3,34,34,10]{2,3,1,0:T(8,128)S(1)} %copy.245, f32[3,1,34,10]{2,3,1,0:T(8,128)S(1)} %collective-permute-done), kind=kLoop, calls=%fused_computation.94 | loop fusion | flops 31104 | bytes 186624 | tf_op jit(solution)/shard_map/slice | solution.py:16
  101.4 4.0 %collective-permute-start.4 = (f32[3,36,36,1]{2,3,1,0:T(1,128)}, f32[3,36,36,1]{2,3,1,0:T(1,128)}, u32[]{:S(2)}, u32[]{:S(2)}) collective-permute-start(f32[3,36,36,1]{2,3,1,0:T(1,128)} %get-tuple-element.32), channel_id=1, source_target_pairs={{0,1},{2,3},{4,5},{6,7},{8,9},{10,11},{12,13},{14,15},{16,17},{18,... | collective-permute-start | bytes 46664 | tf_op jit(solution)/shard_map/ppermute | solution.py:15
  106.7 2.7 %copy.255 = f32[4,36,1,10]{2,0,3,1:T(4,128)} copy(f32[4,36,1,10]{3,2,1,0:T(1,128)} %collective-permute-done.8) | data formatting | bytes 11520 | tf_op jit(solution)/shard_map/ppermute | solution.py:15
  109.4 2.7 %copy.257 = f32[4,36,1,10]{2,0,3,1:T(4,128)} copy(f32[4,36,1,10]{3,2,1,0:T(1,128)} %collective-permute-done.9) | data formatting | bytes 11520 | tf_op jit(solution)/shard_map/ppermute | solution.py:18
  112.1 1.4 pad_maximum_fusion.10
  113.5 5.2 %collective-permute-start.10 = (f32[4,36,36,1]{2,0,3,1:T(4,128)S(1)}, f32[4,36,36,1]{2,0,3,1:T(4,128)S(1)}, u32[]{:S(2)}, u32[]{:S(2)}) collective-permute-start(f32[4,36,36,1]{2,0,3,1:T(4,128)S(1)} %get-tuple-element.34), channel_id=1, source_target_pairs={{0,1},{2,3},{4,5},{6,7},{8,9},{10,11},{12,13},{14,15},{16,17},{18,... | collective-permute-start | bytes 62216 | tf_op jit(solution)/shard_map/ppermute | solution.py:15
  118.7 1.5 collective-permute-start.11
  120.2 1.5 pad_maximum_fusion.1
  123.6 1.4 collective-permute-done.11
  128.6 1.3 collective-permute-start.12
  129.9 1.3 collective-permute-start.13
  131.4 5.2 %collective-permute-done.13 = f32[3,1,32,8]{2,3,1,0:T(8,128)S(1)} collective-permute-done((f32[3,1,32,8]{2,3,1,0:T(8,128)S(1)}, f32[3,1,32,8]{2,3,1,0:T(8,128)S(1)}, u32[]{:S(2)}, u32[]{:S(2)}) %collective-permute-start.13) | collective-permute-done | bytes 3104 | tf_op jit(solution)/shard_map/ppermute | solution.py:18
  137.6 4.6 %collective-permute-start.14 = (f32[3,34,1,8]{2,3,1,0:T(8,128)}, f32[3,34,1,8]{2,3,1,0:T(8,128)S(1)}, u32[]{:S(2)}, u32[]{:S(2)}) collective-permute-start(f32[3,34,1,8]{2,3,1,0:T(8,128)} %get-tuple-element.46), channel_id=1, source_target_pairs={{0,2},{2,4},{4,6},{1,3},{3,5},{5,7},{8,10},{10,12},{12,14},{9,11},... | collective-permute-start | bytes 9800 | tf_op jit(solution)/shard_map/ppermute | solution.py:15
  142.2 1.3 collective-permute-start.15
  144.6 6.3 %collective-permute-done.14 = f32[3,34,1,8]{2,3,1,0:T(8,128)S(1)} collective-permute-done((f32[3,34,1,8]{2,3,1,0:T(8,128)}, f32[3,34,1,8]{2,3,1,0:T(8,128)S(1)}, u32[]{:S(2)}, u32[]{:S(2)}) %collective-permute-start.14) | collective-permute-done | bytes 3296 | tf_op jit(solution)/shard_map/ppermute | solution.py:15
  150.9 4.6 %collective-permute-done.15 = f32[3,34,1,8]{2,3,1,0:T(8,128)S(1)} collective-permute-done((f32[3,34,1,8]{2,3,1,0:T(8,128)}, f32[3,34,1,8]{2,3,1,0:T(8,128)S(1)}, u32[]{:S(2)}, u32[]{:S(2)}) %collective-permute-start.15) | collective-permute-done | bytes 3296 | tf_op jit(solution)/shard_map/ppermute | solution.py:18
  156.7 4.5 %collective-permute-start.16 = (f32[3,34,34,1]{2,3,1,0:T(1,128)}, f32[3,34,34,1]{2,3,1,0:T(1,128)}, u32[]{:S(2)}, u32[]{:S(2)}) collective-permute-start(f32[3,34,34,1]{2,3,1,0:T(1,128)} %get-tuple-element.36), channel_id=1, source_target_pairs={{0,1},{2,3},{4,5},{6,7},{8,9},{10,11},{12,13},{14,15},{16,17},{18,... | collective-permute-start | bytes 41624 | tf_op jit(solution)/shard_map/ppermute | solution.py:15
  161.2 1.3 collective-permute-start.17
  163.6 4.3 %collective-permute-done.17 = f32[3,34,34,1]{2,3,1,0:T(1,128)} collective-permute-done((f32[3,34,34,1]{2,3,1,0:T(1,128)}, f32[3,34,34,1]{2,3,1,0:T(1,128)}, u32[]{:S(2)}, u32[]{:S(2)}) %collective-permute-start.17) | collective-permute-done | bytes 13904 | tf_op jit(solution)/shard_map/ppermute | solution.py:18
  167.9 1.5 pad_maximum_fusion.3
  169.4 2.2 %copy.261 = f32[3,34,34,10]{3,2,1,0:T(8,128)} copy(f32[3,34,34,10]{2,3,1,0:T(8,128)S(1)} %pad_maximum_fusion.3) | data formatting | bytes 277440 | tf_op jit(solution)/shard_map/concatenate | solution.py:19
  171.6 2.4 %reshape.870 = f32[3,11560]{1,0:T(4,128)S(1)} reshape(f32[3,34,34,10]{3,2,1,0:T(8,128)} %copy.261) | data formatting | bytes 277440 | tf_op jit(solution)/shard_map/reshape | solution.py:190
  174.0 4.1 %copy.262 = f32[3,11560]{0,1:T(8,128)} copy(f32[3,11560]{1,0:T(4,128)S(1)} %reshape.870) | data formatting | bytes 277440 | tf_op jit(solution)/shard_map/reshape | solution.py:190
  178.1 10.8 %gather_fusion = f32[3072,3]{1,0:T(8,128)S(1)} fusion(f32[3,11560]{0,1:T(8,128)} %copy.262, s32[3072]{0:T(1024)S(1)} %broadcast_clamp_fusion), kind=kCustom, calls=%fused_computation | custom fusion | bytes 86016 | tf_op jit(solution)/shard_map/gather | solution.py:193
  189.6 2.3 %fusion.2 = f32[32,12,128]{2,1,0:T(8,128)S(1)} fusion(f32[96,32,128]{2,1,0:T(8,128)S(1)} %bitcast.89, f32[9,32,96]{2,0,1:T(8,128)S(1)} %copy_multiply_fusion, f32[3,32,96]{2,0,1:T(4,128)S(1)} %bitcast.99), kind=kOutput, calls=%fused_computation.4 | convolution fusion | flops 56659968 | bytes 1916928 | tf_op jit(solution)/shard_map/nkp,ckn->ckp/dot_general | solution.py:106
  (165 shorter events, 29.3 us)
Async XLA Ops:
  1.9 3.9 %copy-start.6 = (f32[3,4096]{1,0:T(4,128)S(1)}, f32[3,4096]{1,0:T(4,128)}, u32[]{:S(2)}) copy-start(f32[3,4096]{1,0:T(4,128)} %param.11) | copy-start | bytes 147460
  2.6 3.9 %copy-start.11 = (f32[32]{0:T(128)}, f32[32]{0:T(128)S(1)}, u32[]{:S(2)}) copy-start(f32[32]{0:T(128)S(1)} %compare_convert_fusion.1) | copy-start | bytes 388
  5.5 0.8 copy-start.9
  5.6 0.9 copy-start.10
  9.9 4.9 %copy-start.17 = (s32[96]{0:T(128)}, s32[96]{0:T(128)S(1)}, u32[]{:S(2)}) copy-start(s32[96]{0:T(128)S(1)} %fusion.57) | copy-start | bytes 1156
  13.3 1.6 copy-start.22
  14.9 0.5 copy-start.19
  50.5 21.5 %collective-permute-start = (f32[3,1,34,10]{2,3,1,0:T(8,128)}, f32[3,1,34,10]{2,3,1,0:T(8,128)S(1)}, u32[]{:S(2)}, u32[]{:S(2)}) collective-permute-start(f32[3,1,34,10]{2,3,1,0:T(8,128)} %get-tuple-element.44), channel_id=1, source_target_pairs={{0,8},{8,16},{16,24},{1,9},{9,17},{17,25},{2,10},{10,18},{18,26},{... | collective-permute-start | bytes 12248 | tf_op jit(solution)/shard_map/ppermute | solution.py:15
  52.8 19.2 %collective-permute-start.1 = (f32[3,1,34,10]{2,3,1,0:T(8,128)}, f32[3,1,34,10]{2,3,1,0:T(8,128)S(1)}, u32[]{:S(2)}, u32[]{:S(2)}) collective-permute-start(f32[3,1,34,10]{2,3,1,0:T(8,128)} %get-tuple-element.45), channel_id=1, source_target_pairs={{8,0},{16,8},{24,16},{9,1},{17,9},{25,17},{10,2},{18,10},{26,18},{... | collective-permute-start | bytes 12248 | tf_op jit(solution)/shard_map/ppermute | solution.py:18
  58.6 12.1 %copy-start.7 = (f32[32,32,8]{1,2,0:T(8,128)S(1)}, f32[32,32,8]{1,2,0:T(8,128)}, u32[]{:S(2)}) copy-start(f32[32,32,8]{1,2,0:T(8,128)} %param.20) | copy-start | bytes 98308
  63.1 17.4 %collective-permute-start.6 = (f32[4,1,34,10]{3,2,1,0:T(8,128)}, f32[4,1,34,10]{3,2,1,0:T(8,128)}, u32[]{:S(2)}, u32[]{:S(2)}) collective-permute-start(f32[4,1,34,10]{3,2,1,0:T(8,128)} %get-tuple-element.31), channel_id=1, source_target_pairs={{0,8},{8,16},{16,24},{1,9},{9,17},{17,25},{2,10},{10,18},{18,26},{... | collective-permute-start | bytes 16328 | tf_op jit(solution)/shard_map/ppermute | solution.py:15
  68.8 14.6 %collective-permute-start.7 = (f32[4,1,34,10]{3,2,1,0:T(8,128)}, f32[4,1,34,10]{3,2,1,0:T(8,128)}, u32[]{:S(2)}, u32[]{:S(2)}) collective-permute-start(f32[4,1,34,10]{3,2,1,0:T(8,128)} %get-tuple-element.30), channel_id=1, source_target_pairs={{8,0},{16,8},{24,16},{9,1},{17,9},{25,17},{10,2},{18,10},{26,18},{... | collective-permute-start | bytes 16328 | tf_op jit(solution)/shard_map/ppermute | solution.py:18
  74.8 21.6 %collective-permute-start.2 = (f32[3,36,1,10]{1,2,3,0:T(1,128)S(1)}, f32[3,36,1,10]{1,2,3,0:T(1,128)S(1)}, u32[]{:S(2)}, u32[]{:S(2)}) collective-permute-start(f32[3,36,1,10]{1,2,3,0:T(1,128)S(1)} %copy.248), channel_id=1, source_target_pairs={{0,2},{2,4},{4,6},{1,3},{3,5},{5,7},{8,10},{10,12},{12,14},{9,11},... | collective-permute-start | bytes 12968 | tf_op jit(solution)/shard_map/ppermute | solution.py:15
  79.2 17.7 %collective-permute-start.3 = (f32[3,36,1,10]{1,2,3,0:T(1,128)}, f32[3,36,1,10]{1,2,3,0:T(1,128)}, u32[]{:S(2)}, u32[]{:S(2)}) collective-permute-start(f32[3,36,1,10]{1,2,3,0:T(1,128)} %copy.249), channel_id=1, source_target_pairs={{2,0},{4,2},{6,4},{3,1},{5,3},{7,5},{10,8},{12,10},{14,12},{11,9},... | collective-permute-start | bytes 12968 | tf_op jit(solution)/shard_map/ppermute | solution.py:18
  84.3 1.6 copy-start.4
  90.0 16.8 %collective-permute-start.8 = (f32[4,36,1,10]{3,2,1,0:T(1,128)}, f32[4,36,1,10]{3,2,1,0:T(1,128)}, u32[]{:S(2)}, u32[]{:S(2)}) collective-permute-start(f32[4,36,1,10]{3,2,1,0:T(1,128)} %get-tuple-element.28), channel_id=1, source_target_pairs={{0,2},{2,4},{4,6},{1,3},{3,5},{5,7},{8,10},{10,12},{12,14},{9,11},... | collective-permute-start | bytes 17288 | tf_op jit(solution)/shard_map/ppermute | solution.py:15
  95.1 14.3 %collective-permute-start.9 = (f32[4,36,1,10]{3,2,1,0:T(1,128)}, f32[4,36,1,10]{3,2,1,0:T(1,128)}, u32[]{:S(2)}, u32[]{:S(2)}) collective-permute-start(f32[4,36,1,10]{3,2,1,0:T(1,128)} %get-tuple-element.29), channel_id=1, source_target_pairs={{2,0},{4,2},{6,4},{3,1},{5,3},{7,5},{10,8},{12,10},{14,12},{11,9},... | collective-permute-start | bytes 17288 | tf_op jit(solution)/shard_map/ppermute | solution.py:18
  101.4 18.8 %collective-permute-start.4 = (f32[3,36,36,1]{2,3,1,0:T(1,128)}, f32[3,36,36,1]{2,3,1,0:T(1,128)}, u32[]{:S(2)}, u32[]{:S(2)}) collective-permute-start(f32[3,36,36,1]{2,3,1,0:T(1,128)} %get-tuple-element.32), channel_id=1, source_target_pairs={{0,1},{2,3},{4,5},{6,7},{8,9},{10,11},{12,13},{14,15},{16,17},{18,... | collective-permute-start | bytes 46664 | tf_op jit(solution)/shard_map/ppermute | solution.py:15
  105.4 14.8 %collective-permute-start.5 = (f32[3,36,36,1]{2,3,1,0:T(1,128)}, f32[3,36,36,1]{2,3,1,0:T(1,128)}, u32[]{:S(2)}, u32[]{:S(2)}) collective-permute-start(f32[3,36,36,1]{2,3,1,0:T(1,128)} %get-tuple-element.33), channel_id=1, source_target_pairs={{1,0},{3,2},{5,4},{7,6},{9,8},{11,10},{13,12},{15,14},{17,16},{19,... | collective-permute-start | bytes 46664 | tf_op jit(solution)/shard_map/ppermute | solution.py:18
  112.1 8.1 %copy-start = (f32[3,36,1,10]{2,3,1,0:T(8,128)S(1)}, f32[3,36,1,10]{2,3,1,0:T(8,128)}, u32[]{:S(2)}) copy-start(f32[3,36,1,10]{2,3,1,0:T(8,128)} %copy.251) | copy-start | bytes 12964
  113.5 8.2 %copy-start.14 = (pred[32]{0:T(512)(128)(4,1)S(1)}, pred[32]{0:T(512)(128)(4,1)}, u32[]{:S(2)}) copy-start(pred[32]{0:T(512)(128)(4,1)} %constant.279.clone.1) | copy-start | bytes 100
  113.5 10.0 %collective-permute-start.10 = (f32[4,36,36,1]{2,0,3,1:T(4,128)S(1)}, f32[4,36,36,1]{2,0,3,1:T(4,128)S(1)}, u32[]{:S(2)}, u32[]{:S(2)}) collective-permute-start(f32[4,36,36,1]{2,0,3,1:T(4,128)S(1)} %get-tuple-element.34), channel_id=1, source_target_pairs={{0,1},{2,3},{4,5},{6,7},{8,9},{10,11},{12,13},{14,15},{16,17},{18,... | collective-permute-start | bytes 62216 | tf_op jit(solution)/shard_map/ppermute | solution.py:15
  118.7 6.2 %collective-permute-start.11 = (f32[4,36,36,1]{2,0,3,1:T(4,128)S(1)}, f32[4,36,36,1]{2,0,3,1:T(4,128)S(1)}, u32[]{:S(2)}, u32[]{:S(2)}) collective-permute-start(f32[4,36,36,1]{2,0,3,1:T(4,128)S(1)} %get-tuple-element.35), channel_id=1, source_target_pairs={{1,0},{3,2},{5,4},{7,6},{9,8},{11,10},{13,12},{15,14},{17,16},{19,... | collective-permute-start | bytes 62216 | tf_op jit(solution)/shard_map/ppermute | solution.py:18
  122.7 2.2 %copy-start.1 = (f32[4,36,34,10]{2,0,3,1:T(4,128)S(1)}, f32[4,36,34,10]{2,0,3,1:T(4,128)}, u32[]{:S(2)}) copy-start(f32[4,36,34,10]{2,0,3,1:T(4,128)} %copy.256) | copy-start | bytes 587524
  122.7 2.2 %copy-start.2 = (f32[4,36,1,10]{2,0,3,1:T(4,128)S(1)}, f32[4,36,1,10]{2,0,3,1:T(4,128)}, u32[]{:S(2)}) copy-start(f32[4,36,1,10]{2,0,3,1:T(4,128)} %copy.255) | copy-start | bytes 17284
  122.8 2.2 %copy-start.3 = (f32[4,36,1,10]{2,0,3,1:T(4,128)S(1)}, f32[4,36,1,10]{2,0,3,1:T(4,128)}, u32[]{:S(2)}) copy-start(f32[4,36,1,10]{2,0,3,1:T(4,128)} %copy.257) | copy-start | bytes 17284
  126.7 0.7 copy-start.15
  126.7 0.9 copy-start.21
  127.3 3.8 %copy-start.18 = (s32[96]{0:T(128)S(1)}, s32[96]{0:T(128)}, u32[]{:S(2)}) copy-start(s32[96]{0:T(128)} %copy-done.17) | copy-start | bytes 1156
  127.4 3.8 %copy-start.20 = (s32[32]{0:T(128)S(1)}, s32[32]{0:T(128)}, u32[]{:S(2)}) copy-start(s32[32]{0:T(128)} %copy-done.19) | copy-start | bytes 388
  127.7 15.8 %copy-start.13 = (f32[3,96]{1,0:T(4,128)S(1)}, f32[3,96]{1,0:T(4,128)}, u32[]{:S(2)}) copy-start(f32[3,96]{1,0:T(4,128)} %get-tuple-element.65) | copy-start | bytes 3460
  128.6 2.8 %collective-permute-start.12 = (f32[3,1,32,8]{2,3,1,0:T(8,128)S(1)}, f32[3,1,32,8]{2,3,1,0:T(8,128)S(1)}, u32[]{:S(2)}, u32[]{:S(2)}) collective-permute-start(f32[3,1,32,8]{2,3,1,0:T(8,128)S(1)} %get-tuple-element.48), channel_id=1, source_target_pairs={{0,8},{8,16},{16,24},{1,9},{9,17},{17,25},{2,10},{10,18},{18,26},{... | collective-permute-start | bytes 9224 | tf_op jit(solution)/shard_map/ppermute | solution.py:15
  129.9 6.6 %collective-permute-start.13 = (f32[3,1,32,8]{2,3,1,0:T(8,128)S(1)}, f32[3,1,32,8]{2,3,1,0:T(8,128)S(1)}, u32[]{:S(2)}, u32[]{:S(2)}) collective-permute-start(f32[3,1,32,8]{2,3,1,0:T(8,128)S(1)} %get-tuple-element.49), channel_id=1, source_target_pairs={{8,0},{16,8},{24,16},{9,1},{17,9},{25,17},{10,2},{18,10},{26,18},{... | collective-permute-start | bytes 9224 | tf_op jit(solution)/shard_map/ppermute | solution.py:18
  131.4 31.2 %copy-start.8 = (s32[32,32]{1,0:T(8,128)S(1)}, s32[32,32]{1,0:T(8,128)}, u32[]{:S(2)}) copy-start(s32[32,32]{1,0:T(8,128)} %param.19) | copy-start | bytes 12292
  131.4 31.2 %copy-start.16 = (s32[8]{0:T(128)S(1)}, s32[8]{0:T(128)}, u32[]{:S(2)}) copy-start(s32[8]{0:T(128)} %iota_add_fusion.3) | copy-start | bytes 100
  137.6 13.3 %collective-permute-start.14 = (f32[3,34,1,8]{2,3,1,0:T(8,128)}, f32[3,34,1,8]{2,3,1,0:T(8,128)S(1)}, u32[]{:S(2)}, u32[]{:S(2)}) collective-permute-start(f32[3,34,1,8]{2,3,1,0:T(8,128)} %get-tuple-element.46), channel_id=1, source_target_pairs={{0,2},{2,4},{4,6},{1,3},{3,5},{5,7},{8,10},{10,12},{12,14},{9,11},... | collective-permute-start | bytes 9800 | tf_op jit(solution)/shard_map/ppermute | solution.py:15
  142.2 13.4 %collective-permute-start.15 = (f32[3,34,1,8]{2,3,1,0:T(8,128)}, f32[3,34,1,8]{2,3,1,0:T(8,128)S(1)}, u32[]{:S(2)}, u32[]{:S(2)}) collective-permute-start(f32[3,34,1,8]{2,3,1,0:T(8,128)} %get-tuple-element.47), channel_id=1, source_target_pairs={{2,0},{4,2},{6,4},{3,1},{5,3},{7,5},{10,8},{12,10},{14,12},{11,9},... | collective-permute-start | bytes 9800 | tf_op jit(solution)/shard_map/ppermute | solution.py:18
  155.6 5.7 %copy-start.5 = (f32[3,34,1,8]{2,3,1,0:T(8,128)}, f32[3,34,1,8]{2,3,1,0:T(8,128)S(1)}, u32[]{:S(2)}) copy-start(f32[3,34,1,8]{2,3,1,0:T(8,128)S(1)} %collective-permute-done.15) | copy-start | bytes 9796
  156.7 6.9 %collective-permute-start.16 = (f32[3,34,34,1]{2,3,1,0:T(1,128)}, f32[3,34,34,1]{2,3,1,0:T(1,128)}, u32[]{:S(2)}, u32[]{:S(2)}) collective-permute-start(f32[3,34,34,1]{2,3,1,0:T(1,128)} %get-tuple-element.36), channel_id=1, source_target_pairs={{0,1},{2,3},{4,5},{6,7},{8,9},{10,11},{12,13},{14,15},{16,17},{18,... | collective-permute-start | bytes 41624 | tf_op jit(solution)/shard_map/ppermute | solution.py:15
  161.2 6.7 %collective-permute-start.17 = (f32[3,34,34,1]{2,3,1,0:T(1,128)}, f32[3,34,34,1]{2,3,1,0:T(1,128)}, u32[]{:S(2)}, u32[]{:S(2)}) collective-permute-start(f32[3,34,34,1]{2,3,1,0:T(1,128)} %get-tuple-element.37), channel_id=1, source_target_pairs={{1,0},{3,2},{5,4},{7,6},{9,8},{11,10},{13,12},{15,14},{17,16},{19,... | collective-permute-start | bytes 41624 | tf_op jit(solution)/shard_map/ppermute | solution.py:18
  188.9 3.0 %copy-start.12 = (f32[32]{0:T(128)S(1)}, f32[32]{0:T(128)}, u32[]{:S(2)}) copy-start(f32[32]{0:T(128)} %copy-done.11) | copy-start | bytes 388
where the time goes:
time: 196 us; the launch traced here: 194 us
  local copies, waits for them, and re-layouts  75.1 us (38%)
  starting transfers between devices  48.1 us (25%)
  other arithmetic  38.1 us (19%)
  waiting for transfers between devices  21.8 us (11%)
  matrix products  8.81 us (4%)
  between operations  2.3 us (1%)
    ppermute x9, starting transfers between devices, extended_2(): lax.ppermute(lax.slice_in_dim(block, block.shape[dim] - width, None, axis...  36.3 us
    scatter-add x1, other arithmetic, shards(): grid_all = empty_grid.at[:, node_rows].add(joined_terms)  19.8 us
    ppermute x9, waiting for transfers between devices, extended_2(): lax.ppermute(lax.slice_in_dim(block, 0, width, axis=dim), axis, backward)  15.5 us
    slice x4, local copies, waits for them, and re-layouts, shards(): grid_pad[4:]  14.5 us
    ppermute x9, starting transfers between devices, extended_2(): lax.ppermute(lax.slice_in_dim(block, 0, width, axis=dim), axis, backward)  11.8 us
    gather x3, local copies, waits for them, and re-layouts, shards(): gathered = beside_all[:, node_rows]  11.3 us
    unnamed x59, local copies, waits for them, and re-layouts  11.1 us
    slice x2, local copies, waits for them, and re-layouts, shards(): grid_pad[:4]  7.32 us
  transfers between devices with their start and end apart: 18, of which 5 were waited for; matrix products, arithmetic and copies ran while one was open for 20% of the time, Pallas kernels for 0%

commit v1 on v0

v1 whole, which is shorter than its diff:
```python
import functools

import jax
import jax.numpy as jnp
from jax import lax
from jax.experimental import pallas as pl
from jax.experimental.pallas import tpu as pltpu
from jax.sharding import PartitionSpec as P

stiffness = 2.0
gravity_step = 0.3

LANES = 128
SLABS = 4
ZROWS = 10
CHANNELS = 8
ROWS = ZROWS * CHANNELS
F32 = jnp.float32
BF16 = jnp.bfloat16


def iota(shape, dim):
    return lax.broadcasted_iota(jnp.int32, shape, dim)


def tile_nodes(tile, rows, brick):
    lane = iota((rows, LANES), 1)
    if tile < 2:
        x, y = lane >> 1, (lane & 1) + tile * brick
        valid = lane < 2 * (brick + 2)
    else:
        x = (lane >> 5) + ((0, brick)[tile - 2] if tile < SLABS else 4 * (tile - SLABS) + 1)
        y = (lane & 31) + 1
        valid = (y >= 2) & (y < brick)
        valid = valid & ((lane < 64) if tile < SLABS else ((x >= 2) & (x < brick)))
    return x, y, valid


def tile_code(tile, rows, brick):
    x, y, valid = tile_nodes(tile, rows, brick)
    return jnp.where(valid, x * 64 + y, -1)


def block_columns(cells_ref, blocks):
    row = iota((blocks, LANES), 0)
    cells = jnp.zeros((blocks, LANES), jnp.int32)
    for b in range(blocks):
        cells = jnp.where(row == b, cells_ref[b], cells)
    code = (cells >> 5) * 128 + ((cells >> 1) & 15) * 2
    return code, cells & 1


def fill_one_hot(hot_ref, code, blocks, tiles, brick):
    for tile in range(tiles):
        lane_code = tile_code(tile, blocks, brick) - code
        for node in range(16):
            hit = lane_code == (node // 4) * 64 + node % 4
            hot_ref[pl.ds(node * blocks, blocks), pl.ds(tile * LANES, LANES)] = jnp.where(hit, 1.0, 0.0).astype(BF16)


def spline(frac):
    return [0.5 * (0.5 - frac) ** 2, 0.75 - frac * frac, 0.5 * (0.5 + frac) ** 2]


def split(value):
    high = value.astype(BF16)
    return high, (value - high.astype(F32)).astype(BF16)


def is_even(axis):
    return lax.rem(lax.axis_index(axis), 2) == 0


def low_high(even, odd, axis):
    here = is_even(axis)
    return jnp.where(here, odd, even), jnp.where(here, even, odd)


def to_rows(flat_ref, first, array_ref, blocks):
    channels = array_ref.shape[0]
    for b in range(blocks):
        flat_ref[pl.ds(first * blocks + b, channels, stride=blocks), :] = array_ref[:, pl.ds(b * LANES, LANES)]


def from_rows(array_ref, flat_ref, first, blocks):
    channels = array_ref.shape[0]
    for b in range(blocks):
        array_ref[:, pl.ds(b * LANES, LANES)] = flat_ref[pl.ds(first * blocks + b, channels, stride=blocks), :]


def corners(low, high):
    lane = iota(low.shape, 1)
    first, last = lane < 4, (lane >= 64) & (lane < 68)
    zero = jnp.zeros_like(low)
    lower = jnp.where(first, pltpu.roll(low, 64, 1), jnp.where(last, high, zero))
    upper = jnp.where(first, pltpu.roll(low, 60, 1), jnp.where(last, pltpu.roll(high, 124, 1), zero))
    return lower, upper


def deposit_kernel(
    cells_ref, count_ref, pos_ref, vel_ref, aff_ref, vol_ref, cvel_ref, caff_ref, top_ref, drag_ref,
    grid_ref, even_ref, odd_ref,
    flat_ref, terms_ref, spread_ref, sums_ref, window_ref, hot_ref, all_ref,
):
    blocks = vol_ref.shape[0]
    brick = drag_ref.shape[0]
    size_z = drag_ref.shape[1]
    tiles = grid_ref.shape[0]
    for first, ref in ((0, pos_ref), (3, vel_ref), (6, aff_ref), (15, cvel_ref), (18, caff_ref)):
        to_rows(flat_ref, first, ref, blocks)

    def channel(c):
        return flat_ref[pl.ds(c * blocks, blocks), :]

    code, upper_tile = block_columns(cells_ref, blocks)
    live = (iota((blocks, LANES), 0) < count_ref[0]).astype(F32)
    frac = [channel(k) for k in range(3)]
    weight = [spline(f) for f in frac]
    stretch = stiffness * (vol_ref[...] - 1.0)
    linear, matrix = [live], [None]
    for a in range(3):
        row = [live * (channel(6 + 3 * a + b) - (stretch if a == b else 0.0)) for b in range(3)]
        matrix.append(row)
        linear.append(live * channel(3 + a) - sum(row[b] * frac[b] for b in range(3)))
    for a in range(3):
        row = [(4.0 * live) * channel(18 + 3 * a + b) for b in range(3)]
        matrix.append(row)
        linear.append(live * channel(15 + a) - sum(row[b] * frac[b] for b in range(3)))

    def put(row, slot, value):
        high, low = split(value)
        lanes = pl.ds(slot * LANES, LANES)
        terms_ref[pl.ds(row * blocks, blocks), lanes] = high
        terms_ref[pl.ds((9 + row) * blocks, blocks), lanes] = low

    for ox in range(3):
        for oy in range(3):
            planar = weight[0][ox] * weight[1][oy]
            weights = [planar * weight[2][oz] for oz in range(3)]
            for c in range(7):
                base = linear[c]
                if c:
                    if ox != 1:
                        base = base + matrix[c][0] if ox else base - matrix[c][0]
                    if oy != 1:
                        base = base + matrix[c][1] if oy else base - matrix[c][1]
                for oz in range(3):
                    value = base
                    if c and oz != 1:
                        value = base + matrix[c][2] if oz else base - matrix[c][2]
                    put(3 * ox + oy, 3 * c + oz, weights[oz] * value)

    particle = iota((LANES, 2 * LANES), 0)
    shift = iota((LANES, 2 * LANES), 1) - ((particle >> 5) * 64 + ((particle >> 3) & 3) * 8)
    for c in range(7):
        for oz in range(3):
            hit = shift == oz * 8 + c
            spread_ref[pl.ds((3 * c + oz) * LANES, LANES), :] = jnp.where(hit, 1.0, 0.0).astype(BF16)
    sums_ref[...] = jnp.dot(terms_ref[...], spread_ref[...], preferred_element_type=F32)

    fill_one_hot(hot_ref, code, blocks, tiles, brick)

    lane = iota((blocks, LANES), 1)
    low_half = lane < 64
    own_half = low_half == (upper_tile == 0)

    def partial(wx, oy):
        total = None
        for cx in range(2):
            ox = wx - cx
            if 0 <= ox < 3:
                lanes = pl.ds(cx * LANES, LANES)
                row = 3 * ox + oy
                piece = sums_ref[pl.ds(row * blocks, blocks), lanes] + sums_ref[pl.ds((9 + row) * blocks, blocks), lanes]
                total = piece if total is None else total + piece
        return total

    for wx in range(4):
        columns = [partial(wx, oy) for oy in range(3)]
        zero = jnp.zeros_like(columns[0])
        for wy in range(4):
            both = jnp.where(low_half, columns[wy] if wy < 3 else zero, columns[wy - 1] if wy else zero)
            node = jnp.where(own_half, both + pltpu.roll(both, 64, 1), 0.0)
            high, low = split(node)
            rows = pl.ds((4 * wx + wy) * blocks, blocks)
            window_ref[rows, pl.ds(0, LANES)] = high
            window_ref[rows, pl.ds(LANES, LANES)] = low

    all_ref[...] = lax.dot_general(
        window_ref[...], hot_ref[...], (((0,), (0,)), ((), ())), preferred_element_type=F32
    )
    for z in range(ZROWS):
        piece = None
        for tz in range(2):
            wz = z - 4 * tz
            if 0 <= wz < 6:
                row = 64 * tz + 8 * wz
                part = all_ref[pl.ds(row, 8), :] + all_ref[pl.ds(128 + row, 8), :]
                piece = part if piece is None else piece + part
        for tile in range(tiles):
            grid_ref[tile, pl.ds(8 * z, 8), :] = piece[:, tile * LANES : (tile + 1) * LANES]

    depth = iota((size_z, brick), 0) + lax.axis_index("gz") * size_z
    lane = iota((size_z, LANES), 1)
    zero = jnp.zeros((size_z, LANES), F32)
    ends = [zero, zero]
    layers = []
    for x in range(brick):
        layer = jnp.where(depth < top_ref[pl.ds(x, 1), :], drag_ref[x], 0.0)
        layers.append(layer)
        ends[0] = jnp.where(lane == 2 * (x + 1) + 1, layer[:, 0:1], ends[0])
        ends[1] = jnp.where(lane == 2 * (x + 1), layer[:, brick - 1 : brick], ends[1])
    blank = jnp.zeros((size_z, 32), F32)
    planes = ends + [
        jnp.concatenate([blank, layers[0], blank, blank], axis=1),
        jnp.concatenate([layers[-1], blank, blank, blank], axis=1),
    ]
    for t in range(brick // 4):
        planes.append(jnp.concatenate(layers[4 * t : 4 * t + 4], axis=1))
    for tile, plane in enumerate(planes):
        grid_ref[tile, pl.ds(8 + 7, size_z, stride=8), :] = plane

    lane = iota((ROWS, LANES), 1)
    slab = [grid_ref[t] for t in range(SLABS)]
    low = jnp.where(lane < 64, slab[2], jnp.where(lane < 68, pltpu.roll(slab[0], 64, 1), pltpu.roll(slab[1], 68, 1)))
    high = jnp.where(lane < 64, slab[3], jnp.where(lane < 68, slab[0], pltpu.roll(slab[1], 4, 1)))
    here = is_even("gx")
    even_ref[...] = jnp.where(here, high, low)
    odd_ref[...] = jnp.where(here, low, high)


def pack_y_kernel(slab_ref, xe_ref, xo_ref, even_ref, odd_ref):
    low, high = low_high(xe_ref[...], xo_ref[...], "gx")
    lower, upper = corners(low, high)
    lower = slab_ref[0] + lower
    upper = slab_ref[1] + upper
    here = is_even("gy")
    even_ref[...] = jnp.where(here, upper, lower)
    odd_ref[...] = jnp.where(here, lower, upper)


def slab_additions(xe, xo, ye, yo):
    low_x, high_x = low_high(xe, xo, "gx")
    low_y, high_y = low_high(ye, yo, "gy")
    lower, upper = corners(low_x, high_x)
    planar = iota(low_x.shape, 1) < 64
    return [low_y + lower, high_y + upper, jnp.where(planar, low_x, 0.0), jnp.where(planar, high_x, 0.0)]


def pack_z_kernel(grid_ref, xe_ref, xo_ref, ye_ref, yo_ref, even_ref, *odd_refs):
    here = is_even("gz")
    ends = []
    for first in (0, ROWS - 16):
        rows = pl.ds(first, 16)
        extra = slab_additions(xe_ref[rows, :], xo_ref[rows, :], ye_ref[rows, :], yo_ref[rows, :])
        ends.append([grid_ref[t, rows, :] + (extra[t] if t < SLABS else 0.0) for t in range(grid_ref.shape[0])])
    for tile, (lower, upper) in enumerate(zip(*ends)):
        even_ref[tile] = jnp.where(here, upper, lower)
        for odd_ref in odd_refs:
            odd_ref[tile] = jnp.where(here, lower, upper)


def collect_kernel(counts, cells_ref, count_ref, pos_ref, top_ref, grid_ref, xe_ref, xo_ref, ye_ref, yo_ref, *refs):
    received_z = refs[: -11]
    gvel_ref, gaff_ref, gvol_ref, gdrag_ref = refs[-11:-7]
    total_ref, push_ref, hot_ref, take_ref, spread_ref, pulled_ref, flat_ref = refs[-7:]
    blocks = gvol_ref.shape[0]
    brick, size_z = gdrag_ref.shape[0], gdrag_ref.shape[1]
    tiles = grid_ref.shape[0]
    to_rows(flat_ref, 0, pos_ref, blocks)
    frac = [flat_ref[pl.ds(k * blocks, blocks), :] for k in range(3)]
    weight = [spline(f) for f in frac]
    code, upper_tile = block_columns(cells_ref, blocks)
    fill_one_hot(hot_ref, code, blocks, tiles, brick)

    here = is_even("gz")
    extra = slab_additions(xe_ref[...], xo_ref[...], ye_ref[...], yo_ref[...])
    for tile in range(tiles):
        even = received_z[0][tile]
        odd = received_z[1][tile] if len(received_z) > 1 else jnp.zeros_like(even)
        total_ref[tile, pl.ds(0, ROWS), :] = grid_ref[tile] + extra[tile] if tile < SLABS else grid_ref[tile]
        total_ref[tile, pl.ds(ROWS, 16), :] = jnp.zeros((16, LANES), F32)
        total_ref[tile, pl.ds(0, 16), :] += jnp.where(here, odd, even)
        total_ref[tile, pl.ds(ROWS - 16, 16), :] += jnp.where(here, even, odd)

    place = [lax.axis_index(axis) for axis in ("gx", "gy", "gz")]
    edges = []
    row = iota((8, LANES), 0)
    blank = jnp.zeros((8, LANES), F32)
    for tile in range(tiles):
        lanes = pl.ds(tile * LANES, LANES)
        node_x, node_y, _ = tile_nodes(tile, 8, brick)
        node_x = node_x + (place[0] * brick - 1)
        node_y = node_y + (place[1] * brick - 1)
        drags = []
        for side in range(2):
            c = [total_ref[tile, pl.ds(32 * side + k, 8, stride=8), :] for k in range(CHANNELS)]
            node_z = row + (4 * side - 1) + place[2] * size_z
            inside = (node_z >= 0) & (node_z < counts[2] * size_z)
            if tile < SLABS:
                inside = inside & (node_x >= 0) & (node_x < counts[0] * brick)
                inside = inside & (node_y >= 0) & (node_y < counts[1] * brick)
            inverse = 1.0 / jnp.maximum(c[0], 1.0)
            scale = jnp.where(inside, (1.0 - c[7]) * inverse, 0.0)
            high, low = split(jnp.concatenate([c[4 + a] * scale for a in range(3)] + [blank], axis=0))
            push_ref[pl.ds(64 * side, 32), lanes] = high
            push_ref[pl.ds(64 * side + 32, 32), lanes] = low
            drags.append(
                c[4] * (c[1] * inverse) + c[5] * (c[2] * inverse) + c[6] * (c[3] * inverse - gravity_step)
            )
        edges.append(jnp.where(row < 7, pltpu.roll(drags[0], 7, 0), pltpu.roll(drags[1], 3, 0)))

    depth = iota((size_z, brick), 0) + place[2] * size_z
    lane = iota((size_z, LANES), 1)
    for x in range(brick):
        if x == 0:
            plane = pltpu.roll(edges[2], 96, 1)
        elif x == brick - 1:
            plane = edges[3]
        else:
            plane = edges[SLABS + x // 4]
            if x % 4:
                plane = pltpu.roll(plane, LANES - 32 * (x % 4), 1)
        at = 2 * (x + 1)
        plane = jnp.where(lane == 0, edges[0][:, at + 1 : at + 2], plane)
        plane = jnp.where(lane == brick - 1, edges[1][:, at : at + 1], plane)
        gdrag_ref[x] = jnp.where(depth < top_ref[pl.ds(x, 1), :], -plane[:, :brick], 0.0)

    gathered = lax.dot_general(hot_ref[...], push_ref[...], (((1,), (1,)), ((), ())), preferred_element_type=F32)
    lane = iota((blocks, LANES), 1)
    low_half = lane < 64
    upper = upper_tile == 1
    lows, highs = [], []
    for node in range(16):
        value = gathered[node * blocks : (node + 1) * blocks]
        rolled = pltpu.roll(value, 64, 1)
        lows.append(jnp.where(upper, rolled, value))
        highs.append(jnp.where(upper, value, rolled))
    for ox in range(3):
        for oy in range(3):
            for cx in range(2):
                value = jnp.where(low_half, lows[4 * (cx + ox) + oy], highs[4 * (cx + ox) + oy + 1])
                take_ref[pl.ds((3 * ox + oy) * blocks, blocks), pl.ds(cx * LANES, LANES)] = value.astype(BF16)

    key = iota((2 * LANES, LANES), 0)
    particle = iota((2 * LANES, LANES), 1)
    shift = jnp.where((key >> 6) == (particle >> 5), (key & 31) - ((particle >> 3) & 3), -64)
    for a in range(3):
        for oz in range(3):
            hit = shift == 8 * a + oz
            spread_ref[:, pl.ds((3 * a + oz) * LANES, LANES)] = jnp.where(hit, 1.0, 0.0).astype(BF16)
    pulled_ref[...] = jnp.dot(take_ref[...], spread_ref[...], preferred_element_type=F32)

    live = (iota((blocks, LANES), 0) < count_ref[0]).astype(F32)
    planar = [[live * weight[0][ox] * weight[1][oy] for oy in range(3)] for ox in range(3)]
    trace = None
    for a in range(3):
        sums_x, sums_y, sums_z = [], [None] * 3, None
        for ox in range(3):
            column = None
            for oy in range(3):
                rows = pl.ds((3 * ox + oy) * blocks, blocks)
                g = [pulled_ref[rows, pl.ds((3 * a + oz) * LANES, LANES)] for oz in range(3)]
                below, above = weight[2][0] * g[0], weight[2][2] * g[2]
                sum_z = planar[ox][oy] * (weight[2][1] * g[1] + (below + above))
                slope = planar[ox][oy] * (above - below)
                column = sum_z if column is None else column + sum_z
                sums_y[oy] = sum_z if sums_y[oy] is None else sums_y[oy] + sum_z
                sums_z = slope if sums_z is None else sums_z + slope
            sums_x.append(column)
        whole = sums_x[0] + sums_x[1] + sums_x[2]
        moments = [sums_x[2] - sums_x[0], sums_y[2] - sums_y[0], sums_z]
        flat_ref[pl.ds((3 + a) * blocks, blocks), :] = whole
        for b in range(3):
            value = moments[b] - frac[b] * whole
            flat_ref[pl.ds((6 + 3 * a + b) * blocks, blocks), :] = value
            if a == b:
                trace = value if trace is None else trace + value
    gvol_ref[...] = -stiffness * trace
    from_rows(gvel_ref, flat_ref, 3, blocks)
    from_rows(gaff_ref, flat_ref, 6, blocks)


def swap(array, axis, first):
    count = lax.axis_size(axis)
    pairs = [(i + k, i + 1 - k) for i in range(first, count - 1, 2) for k in range(2)]
    return lax.ppermute(array, axis, pairs) if pairs else jnp.zeros_like(array)


def shards(
    offsets, velocity, affine, volume, cot_velocity, cot_affine, block_cells, fill_counts, baffle_top, drag
):
    brick, _, size_z = drag.shape
    blocks = block_cells.shape[0]
    counts = tuple(lax.axis_size(axis) for axis in ("gx", "gy", "gz"))
    tiles = SLABS + brick // 4
    width = tiles * LANES
    smem = pl.BlockSpec(memory_space=pltpu.SMEM)
    vmem = pl.BlockSpec(memory_space=pltpu.VMEM)

    def f32(*shape):
        return jax.ShapeDtypeStruct(shape, F32)

    params = pltpu.CompilerParams(vmem_limit_bytes=40 * 1024 * 1024)
    slab = f32(ROWS, LANES)
    grid, send_xe, send_xo = pl.pallas_call(
        deposit_kernel,
        out_shape=(f32(tiles, ROWS, LANES), slab, slab),
        in_specs=[smem, smem] + [vmem] * 8,
        out_specs=(vmem,) * 3,
        scratch_shapes=[
            pltpu.VMEM((27 * blocks, LANES), F32),
            pltpu.VMEM((18 * blocks, 21 * LANES), BF16),
            pltpu.VMEM((21 * LANES, 2 * LANES), BF16),
            pltpu.VMEM((18 * blocks, 2 * LANES), F32),
            pltpu.VMEM((16 * blocks, 2 * LANES), BF16),
            pltpu.VMEM((16 * blocks, width), BF16),
            pltpu.VMEM((2 * LANES, width), F32),
        ],
        compiler_params=params,
        name="deposit",
    )(
        block_cells, fill_counts, offsets, velocity, affine, volume.reshape(blocks, LANES), cot_velocity, cot_affine,
        baffle_top, drag.transpose(0, 2, 1),
    )
    xo = swap(send_xo, "gx", 1)
    xe = swap(send_xe, "gx", 0)
    send_ye, send_yo = pl.pallas_call(
        pack_y_kernel,
        grid=(1,),
        out_shape=(slab, slab),
        in_specs=[pl.BlockSpec((2, ROWS, LANES), lambda i: (0, 0, 0))] + [pl.BlockSpec((ROWS, LANES), lambda i: (0, 0))] * 2,
        out_specs=(pl.BlockSpec((ROWS, LANES), lambda i: (0, 0)),) * 2,
        name="pack_y",
    )(grid, xe, xo)
    yo = swap(send_yo, "gy", 1)
    ye = swap(send_ye, "gy", 0)
    ends_z = 2 if counts[2] > 2 else 1
    send_z = pl.pallas_call(
        pack_z_kernel,
        out_shape=(f32(tiles, 16, LANES),) * ends_z,
        in_specs=[vmem] * 5,
        out_specs=(vmem,) * ends_z,
        name="pack_z",
    )(grid, xe, xo, ye, yo)
    received_z = [swap(array, "gz", first) for first, array in enumerate(send_z)]
    grad_velocity, grad_affine, grad_volume, grad_drag = pl.pallas_call(
        functools.partial(collect_kernel, counts),
        out_shape=(f32(3, blocks * LANES), f32(9, blocks * LANES), f32(blocks, LANES), f32(brick, size_z, brick)),
        in_specs=[smem, smem] + [vmem] * (7 + ends_z),
        out_specs=(vmem,) * 4,
        scratch_shapes=[
            pltpu.VMEM((tiles, ROWS + 16, LANES), F32),
            pltpu.VMEM((LANES, width), BF16),
            pltpu.VMEM((16 * blocks, width), BF16),
            pltpu.VMEM((9 * blocks, 2 * LANES), BF16),
            pltpu.VMEM((2 * LANES, 9 * LANES), BF16),
            pltpu.VMEM((9 * blocks, 9 * LANES), F32),
            pltpu.VMEM((15 * blocks, LANES), F32),
        ],
        compiler_params=params,
        name="collect",
    )(block_cells, fill_counts, offsets, baffle_top, grid, xe, xo, ye, yo, *received_z)
    return grad_velocity, grad_affine, grad_volume.reshape(-1), grad_drag.transpose(0, 2, 1)


def solution(mesh):
    everywhere = ("gx", "gy", "gz")
    rows, flat = P(None, everywhere), P(everywhere)
    in_specs = (rows, rows, rows, flat, rows, rows, flat, flat, P("gx", "gy"), P("gx", "gy", "gz"))
    out_specs = (rows, rows, flat, P("gx", "gy", "gz"))
    return jax.shard_map(shards, mesh=mesh, in_specs=in_specs, out_specs=out_specs, check_vma=False)
```

time: 196 us -> 40.8 us (0.21)
  the two profiles are of different devices: /device:TPU:0 before, /device:TPU:18 now
where the time goes in v1:
time: 40.8 us; the launch traced here: 40.1 us
  local copies, waits for them, and re-layouts  11 us (27%)
  waiting for transfers between devices  10.2 us (25%)
  Pallas kernels  9.86 us (24%)
  starting transfers between devices  7.69 us (19%)
  between operations  1.39 us (3%)
    unnamed x42, local copies, waits for them, and re-layouts  11 us
    ppermute x5, waiting for transfers between devices, swap(): return lax.ppermute(array, axis, pairs) if pairs else jnp.zeros_like(array)  10.2 us
    ppermute x5, starting transfers between devices, swap(): return lax.ppermute(array, axis, pairs) if pairs else jnp.zeros_like(array)  7.69 us
    pallas_call x1, Pallas kernels, shards(): pl.pallas_call(deposit_kernel, out_shape=(f32(tiles, ROWS, LANES), slab,...  3.5 us
    pallas_call x1, Pallas kernels, shards(): pl.pallas_call(functools.partial(collect_kernel, counts), out_shape=(f32(...  2.9 us
    pallas_call x1, Pallas kernels, shards(): pl.pallas_call(pack_z_kernel, out_shape=(f32(tiles, 16, LANES),) * ends_z...  1.81 us
    pallas_call x1, Pallas kernels, shards(): pl.pallas_call(pack_y_kernel, grid=(1,), out_shape=(slab, slab), in_specs...  1.64 us
  transfers between devices with their start and end apart: 5, of which 4 were waited for; matrix products, arithmetic and copies ran while one was open for 0% of the time, Pallas kernels for 0%

profile of v1, /device:TPU:18, one launch (start us, length us, event | category | flops | bytes accessed | tf_op | source)
XLA Modules:
  0.0 40.1 jit_solution(11545342491503156401)
XLA Ops:
  1.3 0.0 copy-start.20
  1.3 0.6 %copy-done.20 = s32[32]{0:T(128)S(1)} copy-done((s32[32]{0:T(128)S(1)}, s32[32]{0:T(128)}, u32[]{:S(2)}) %copy-start.20) | copy-done | bytes 152
  1.9 0.0 copy-start.6
  1.9 0.9 %copy-done.6 = f32[9,4096]{1,0:T(8,128)S(1)} copy-done((f32[9,4096]{1,0:T(8,128)S(1)}, f32[9,4096]{1,0:T(8,128)}, u32[]{:S(2)}) %copy-start.6) | copy-done | bytes 147480
  2.9 0.0 copy-start.7
  2.9 0.9 %copy-done.7 = f32[9,4096]{1,0:T(8,128)S(1)} copy-done((f32[9,4096]{1,0:T(8,128)S(1)}, f32[9,4096]{1,0:T(8,128)}, u32[]{:S(2)}) %copy-start.7) | copy-done | bytes 147480
  3.8 0.0 copy-start.8
  3.8 0.8 %copy-done.8 = f32[3,4096]{1,0:T(4,128)S(1)} copy-done((f32[3,4096]{1,0:T(4,128)S(1)}, f32[3,4096]{1,0:T(4,128)}, u32[]{:S(2)}) %copy-start.8) | copy-done | bytes 49176
  4.7 0.0 copy-start.14
  4.7 0.9 %copy-done.14 = f32[32,32,8]{1,2,0:T(8,128)S(1)} copy-done((f32[32,32,8]{1,2,0:T(8,128)S(1)}, f32[32,32,8]{1,2,0:T(8,128)}, u32[]{:S(2)}) %copy-start.14) | copy-done | bytes 32792
  5.6 0.0 copy-start.15
  5.6 0.7 %copy-done.15 = s32[32,32]{1,0:T(8,128)S(1)} copy-done((s32[32,32]{1,0:T(8,128)S(1)}, s32[32,32]{1,0:T(8,128)}, u32[]{:S(2)}) %copy-start.15) | copy-done | bytes 4120
  6.3 0.0 copy-start.17
  6.3 0.8 %copy-done.17 = f32[3,4096]{1,0:T(4,128)S(1)} copy-done((f32[3,4096]{1,0:T(4,128)S(1)}, f32[3,4096]{1,0:T(4,128)}, u32[]{:S(2)}) %copy-start.17) | copy-done | bytes 49176
  7.1 0.0 copy-start.18
  7.1 0.8 %copy-done.18 = f32[3,4096]{1,0:T(4,128)S(1)} copy-done((f32[3,4096]{1,0:T(4,128)S(1)}, f32[3,4096]{1,0:T(4,128)}, u32[]{:S(2)}) %copy-start.18) | copy-done | bytes 49176
  8.0 0.0 copy-start.19
  8.0 0.7 %copy-done.19 = f32[4096]{0:T(1024)S(1)} copy-done((f32[4096]{0:T(1024)S(1)}, f32[4096]{0:T(1024)}, u32[]{:S(2)}) %copy-start.19) | copy-done | bytes 16408
  8.7 3.5 %deposit.1 = (f32[12,80,128]{2,1,0:T(8,128)S(1)}, f32[80,128]{1,0:T(8,128)S(1)}, f32[80,128]{1,0:T(8,128)S(1)}) custom-call(s32[32]{0:T(128)S(1)} %copy-done.20, s32[1]{0:T(128)S(6)} %copy.14.count_ref, f32[3,4096]{1,0:T(4,128)S(1)} %copy-done.8, f32[3,4096]{1,0:T(4,128)S(1)} %copy-done.17, f32[9,4096]{1,0:T(8,128)S(1)} %copy-done.6, f32[32,128]{1,0:T(8,128)S(1)} %bitcast.5, ...), custom_call_target="tpu_custom_call" | custom-call | tf_op jit(solution)/shard_map/deposit/pallas_call | solution.py:406
  12.2 0.0 copy-start
  12.2 0.8 %copy-done = f32[12,80,128]{2,1,0:T(8,128)} copy-done((f32[12,80,128]{2,1,0:T(8,128)}, f32[12,80,128]{2,1,0:T(8,128)S(1)}, u32[]{:S(2)}) %copy-start) | copy-done | bytes 491544
  13.0 0.0 collective-permute-start
  13.0 2.5 %collective-permute-start.1 = (f32[80,128]{1,0:T(8,128)S(1)}, f32[80,128]{1,0:T(8,128)S(1)}, u32[]{:S(2)}, u32[]{:S(2)}) collective-permute-start(f32[80,128]{1,0:T(8,128)S(1)} %get-tuple-element.15), channel_id=1, source_target_pairs={{8,16},{16,8},{9,17},{17,9},{10,18},{18,10},{11,19},{19,11},{12,20... | collective-permute-start | bytes 122888 | tf_op jit(solution)/shard_map/ppermute | solution.py:387
  15.6 0.0 collective-permute-done.xe_ref
  15.6 0.0 copy-start.2
  15.6 2.7 %collective-permute-done.1.xo_ref = f32[80,128]{1,0:T(8,128)S(1)} collective-permute-done((f32[80,128]{1,0:T(8,128)S(1)}, f32[80,128]{1,0:T(8,128)S(1)}, u32[]{:S(2)}, u32[]{:S(2)}) %collective-permute-start.1) | collective-permute-done | bytes 40992 | tf_op jit(solution)/shard_map/ppermute | solution.py:387
  18.3 0.0 copy-start.4
  18.3 0.0 copy-done.2
  18.3 0.6 %copy-done.4 = f32[80,128]{1,0:T(8,128)} copy-done((f32[80,128]{1,0:T(8,128)}, f32[80,128]{1,0:T(8,128)S(1)}, u32[]{:S(2)}) %copy-start.4) | copy-done | bytes 40984
  18.9 1.6 %pack_y.1 = (f32[80,128]{1,0:T(8,128)}, f32[80,128]{1,0:T(8,128)}) custom-call(f32[12,80,128]{2,1,0:T(8,128)} %copy-done, f32[80,128]{1,0:T(8,128)} %copy-done.2, f32[80,128]{1,0:T(8,128)} %copy-done.4), custom_call_target="tpu_custom_call" | custom-call | tf_op jit(solution)/shard_map/pack_y/pallas_call | solution.py:428
  20.6 1.6 %collective-permute-start.2 = (f32[80,128]{1,0:T(8,128)}, f32[80,128]{1,0:T(8,128)S(1)}, u32[]{:S(2)}, u32[]{:S(2)}) collective-permute-start(f32[80,128]{1,0:T(8,128)} %get-tuple-element.16), channel_id=1, source_target_pairs={{0,2},{2,0},{4,6},{6,4},{1,3},{3,1},{5,7},{7,5},{8,10},{10,8},{12,... | collective-permute-start | bytes 122888 | tf_op jit(solution)/shard_map/ppermute | solution.py:387
  22.2 2.1 %collective-permute-start.3 = (f32[80,128]{1,0:T(8,128)}, f32[80,128]{1,0:T(8,128)S(1)}, u32[]{:S(2)}, u32[]{:S(2)}) collective-permute-start(f32[80,128]{1,0:T(8,128)} %get-tuple-element.17), channel_id=1, source_target_pairs={{2,4},{4,2},{3,5},{5,3},{10,12},{12,10},{11,13},{13,11},{18,20},{2... | collective-permute-start | bytes 122888 | tf_op jit(solution)/shard_map/ppermute | solution.py:387
  24.2 0.6 %collective-permute-done.2.ye_ref = f32[80,128]{1,0:T(8,128)S(1)} collective-permute-done((f32[80,128]{1,0:T(8,128)}, f32[80,128]{1,0:T(8,128)S(1)}, u32[]{:S(2)}, u32[]{:S(2)}) %collective-permute-start.2) | collective-permute-done | bytes 40992 | tf_op jit(solution)/shard_map/ppermute | solution.py:387
  24.8 3.6 %collective-permute-done.3.yo_ref = f32[80,128]{1,0:T(8,128)S(1)} collective-permute-done((f32[80,128]{1,0:T(8,128)}, f32[80,128]{1,0:T(8,128)S(1)}, u32[]{:S(2)}, u32[]{:S(2)}) %collective-permute-start.3) | collective-permute-done | bytes 40992 | tf_op jit(solution)/shard_map/ppermute | solution.py:387
  28.4 0.0 copy-done.10
  28.4 0.6 %copy-done.12 = f32[80,128]{1,0:T(8,128)} copy-done((f32[80,128]{1,0:T(8,128)}, f32[80,128]{1,0:T(8,128)S(1)}, u32[]{:S(2)}) %copy-start.12) | copy-done | bytes 40984
  29.0 1.8 %pack_z.1 = f32[12,16,128]{2,1,0:T(8,128)} custom-call(f32[12,80,128]{2,1,0:T(8,128)} %copy-done, f32[80,128]{1,0:T(8,128)} %copy-done.2, f32[80,128]{1,0:T(8,128)} %copy-done.4, f32[80,128]{1,0:T(8,128)} %copy-done.10, f32[80,128]{1,0:T(8,128)} %copy-done.12), custom_call_target="tpu_custom_call" | custom-call | tf_op jit(solution)/shard_map/pack_z/pallas_call | solution.py:439
  30.8 1.5 %collective-permute-start.4 = (f32[12,16,128]{2,1,0:T(8,128)}, f32[12,16,128]{2,1,0:T(8,128)S(1)}, u32[]{:S(2)}, u32[]{:S(2)}) collective-permute-start(f32[12,16,128]{2,1,0:T(8,128)} %pack_z.1), channel_id=1, source_target_pairs={{0,1},{1,0},{2,3},{3,2},{4,5},{5,4},{6,7},{7,6},{8,9},{9,8},{10,11... | collective-permute-start | bytes 294920 | tf_op jit(solution)/shard_map/ppermute | solution.py:387
  32.3 3.3 %collective-permute-done.4.refs_0_ = f32[12,16,128]{2,1,0:T(8,128)S(1)} collective-permute-done((f32[12,16,128]{2,1,0:T(8,128)}, f32[12,16,128]{2,1,0:T(8,128)S(1)}, u32[]{:S(2)}, u32[]{:S(2)}) %collective-permute-start.4) | collective-permute-done | bytes 98336 | tf_op jit(solution)/shard_map/ppermute | solution.py:387
  35.7 0.0 copy-done.1
  35.7 0.0 copy-done.3
  35.7 0.0 copy-done.5
  35.7 0.0 copy-done.9
  35.7 0.0 copy-done.16
  35.7 0.0 copy-start.11
  35.7 0.8 %copy-done.11 = f32[80,128]{1,0:T(8,128)S(1)} copy-done((f32[80,128]{1,0:T(8,128)S(1)}, f32[80,128]{1,0:T(8,128)}, u32[]{:S(2)}) %copy-start.11) | copy-done | bytes 40984
  36.5 0.8 %copy-done.13 = f32[80,128]{1,0:T(8,128)S(1)} copy-done((f32[80,128]{1,0:T(8,128)S(1)}, f32[80,128]{1,0:T(8,128)}, u32[]{:S(2)}) %copy-start.13) | copy-done | bytes 40984
  37.2 2.9 %collect.1 = (f32[3,4096]{1,0:T(4,128)}, f32[9,4096]{1,0:T(8,128)}, f32[32,128]{1,0:T(8,128)}, f32[32,8,32]{2,1,0:T(8,128)}) custom-call(s32[32]{0:T(128)S(1)} %copy-done.20, s32[1]{0:T(128)S(6)} %copy.14.count_ref, f32[3,4096]{1,0:T(4,128)S(1)} %copy-done.9, s32[32,32]{1,0:T(8,128)S(1)} %copy-done.16, f32[12,80,128]{2,1,0:T(8,128)S(1)} %copy-done.1, ...), custom_call_target="tpu_custom_call" | custom-call | tf_op jit(solution)/shard_map/collect/pallas_call | solution.py:447
  (8 shorter events, 0.0 us)
Async XLA Ops:
  1.3 0.7 %copy-start.20 = (s32[32]{0:T(128)S(1)}, s32[32]{0:T(128)}, u32[]{:S(2)}) copy-start(s32[32]{0:T(128)} %cells_ref.3) | copy-start | bytes 388
  1.9 0.9 %copy-start.6 = (f32[9,4096]{1,0:T(8,128)S(1)}, f32[9,4096]{1,0:T(8,128)}, u32[]{:S(2)}) copy-start(f32[9,4096]{1,0:T(8,128)} %aff_ref.1) | copy-start | bytes 442372
  2.9 0.9 %copy-start.7 = (f32[9,4096]{1,0:T(8,128)S(1)}, f32[9,4096]{1,0:T(8,128)}, u32[]{:S(2)}) copy-start(f32[9,4096]{1,0:T(8,128)} %caff_ref.1) | copy-start | bytes 442372
  3.8 0.8 %copy-start.8 = (f32[3,4096]{1,0:T(4,128)S(1)}, f32[3,4096]{1,0:T(4,128)}, u32[]{:S(2)}) copy-start(f32[3,4096]{1,0:T(4,128)} %pos_ref.3) | copy-start | bytes 147460
  4.7 0.9 %copy-start.14 = (f32[32,32,8]{1,2,0:T(8,128)S(1)}, f32[32,32,8]{1,2,0:T(8,128)}, u32[]{:S(2)}) copy-start(f32[32,32,8]{1,2,0:T(8,128)} %param.19) | copy-start | bytes 98308
  5.6 0.7 %copy-start.15 = (s32[32,32]{1,0:T(8,128)S(1)}, s32[32,32]{1,0:T(8,128)}, u32[]{:S(2)}) copy-start(s32[32,32]{1,0:T(8,128)} %top_ref.3) | copy-start | bytes 12292
  6.3 0.8 %copy-start.17 = (f32[3,4096]{1,0:T(4,128)S(1)}, f32[3,4096]{1,0:T(4,128)}, u32[]{:S(2)}) copy-start(f32[3,4096]{1,0:T(4,128)} %vel_ref.1) | copy-start | bytes 147460
  7.1 0.8 %copy-start.18 = (f32[3,4096]{1,0:T(4,128)S(1)}, f32[3,4096]{1,0:T(4,128)}, u32[]{:S(2)}) copy-start(f32[3,4096]{1,0:T(4,128)} %cvel_ref.1) | copy-start | bytes 147460
  8.0 0.7 %copy-start.19 = (f32[4096]{0:T(1024)S(1)}, f32[4096]{0:T(1024)}, u32[]{:S(2)}) copy-start(f32[4096]{0:T(1024)} %param.13) | copy-start | bytes 49156
  12.2 0.8 %copy-start = (f32[12,80,128]{2,1,0:T(8,128)}, f32[12,80,128]{2,1,0:T(8,128)S(1)}, u32[]{:S(2)}) copy-start(f32[12,80,128]{2,1,0:T(8,128)S(1)} %get-tuple-element.13.slab_ref.grid_ref) | copy-start | bytes 1474564
  13.0 2.6 %collective-permute-start = (f32[80,128]{1,0:T(8,128)S(1)}, f32[80,128]{1,0:T(8,128)S(1)}, u32[]{:S(2)}, u32[]{:S(2)}) collective-permute-start(f32[80,128]{1,0:T(8,128)S(1)} %get-tuple-element.14), channel_id=1, source_target_pairs={{0,8},{8,0},{16,24},{24,16},{1,9},{9,1},{17,25},{25,17},{2,10},{10... | collective-permute-start | bytes 122888 | tf_op jit(solution)/shard_map/ppermute | solution.py:387
  13.0 5.3 %collective-permute-start.1 = (f32[80,128]{1,0:T(8,128)S(1)}, f32[80,128]{1,0:T(8,128)S(1)}, u32[]{:S(2)}, u32[]{:S(2)}) collective-permute-start(f32[80,128]{1,0:T(8,128)S(1)} %get-tuple-element.15), channel_id=1, source_target_pairs={{8,16},{16,8},{9,17},{17,9},{10,18},{18,10},{11,19},{19,11},{12,20... | collective-permute-start | bytes 122888 | tf_op jit(solution)/shard_map/ppermute | solution.py:387
  15.6 2.8 %copy-start.2 = (f32[80,128]{1,0:T(8,128)}, f32[80,128]{1,0:T(8,128)S(1)}, u32[]{:S(2)}) copy-start(f32[80,128]{1,0:T(8,128)S(1)} %collective-permute-done.xe_ref) | copy-start | bytes 122884
  18.3 0.6 %copy-start.4 = (f32[80,128]{1,0:T(8,128)}, f32[80,128]{1,0:T(8,128)S(1)}, u32[]{:S(2)}) copy-start(f32[80,128]{1,0:T(8,128)S(1)} %collective-permute-done.1.xo_ref) | copy-start | bytes 122884
  20.6 15.1 %copy-start.1 = (f32[12,80,128]{2,1,0:T(8,128)S(1)}, f32[12,80,128]{2,1,0:T(8,128)}, u32[]{:S(2)}) copy-start(f32[12,80,128]{2,1,0:T(8,128)} %copy-done) | copy-start | bytes 1474564
  20.6 4.2 %collective-permute-start.2 = (f32[80,128]{1,0:T(8,128)}, f32[80,128]{1,0:T(8,128)S(1)}, u32[]{:S(2)}, u32[]{:S(2)}) collective-permute-start(f32[80,128]{1,0:T(8,128)} %get-tuple-element.16), channel_id=1, source_target_pairs={{0,2},{2,0},{4,6},{6,4},{1,3},{3,1},{5,7},{7,5},{8,10},{10,8},{12,... | collective-permute-start | bytes 122888 | tf_op jit(solution)/shard_map/ppermute | solution.py:387
  22.2 13.5 %copy-start.3 = (f32[80,128]{1,0:T(8,128)S(1)}, f32[80,128]{1,0:T(8,128)}, u32[]{:S(2)}) copy-start(f32[80,128]{1,0:T(8,128)} %copy-done.2) | copy-start | bytes 122884
  22.2 13.5 %copy-start.5 = (f32[80,128]{1,0:T(8,128)S(1)}, f32[80,128]{1,0:T(8,128)}, u32[]{:S(2)}) copy-start(f32[80,128]{1,0:T(8,128)} %copy-done.4) | copy-start | bytes 122884
  22.2 13.5 %copy-start.9 = (f32[3,4096]{1,0:T(4,128)S(1)}, f32[3,4096]{1,0:T(4,128)}, u32[]{:S(2)}) copy-start(f32[3,4096]{1,0:T(4,128)} %pos_ref.3) | copy-start | bytes 147460
  22.2 13.5 %copy-start.16 = (s32[32,32]{1,0:T(8,128)S(1)}, s32[32,32]{1,0:T(8,128)}, u32[]{:S(2)}) copy-start(s32[32,32]{1,0:T(8,128)} %top_ref.3) | copy-start | bytes 12292
  22.2 6.2 %collective-permute-start.3 = (f32[80,128]{1,0:T(8,128)}, f32[80,128]{1,0:T(8,128)S(1)}, u32[]{:S(2)}, u32[]{:S(2)}) collective-permute-start(f32[80,128]{1,0:T(8,128)} %get-tuple-element.17), channel_id=1, source_target_pairs={{2,4},{4,2},{3,5},{5,3},{10,12},{12,10},{11,13},{13,11},{18,20},{2... | collective-permute-start | bytes 122888 | tf_op jit(solution)/shard_map/ppermute | solution.py:387
  24.8 3.6 %copy-start.10 = (f32[80,128]{1,0:T(8,128)}, f32[80,128]{1,0:T(8,128)S(1)}, u32[]{:S(2)}) copy-start(f32[80,128]{1,0:T(8,128)S(1)} %collective-permute-done.2.ye_ref) | copy-start | bytes 122884
  28.4 0.6 %copy-start.12 = (f32[80,128]{1,0:T(8,128)}, f32[80,128]{1,0:T(8,128)S(1)}, u32[]{:S(2)}) copy-start(f32[80,128]{1,0:T(8,128)S(1)} %collective-permute-done.3.yo_ref) | copy-start | bytes 122884
  30.8 4.8 %collective-permute-start.4 = (f32[12,16,128]{2,1,0:T(8,128)}, f32[12,16,128]{2,1,0:T(8,128)S(1)}, u32[]{:S(2)}, u32[]{:S(2)}) collective-permute-start(f32[12,16,128]{2,1,0:T(8,128)} %pack_z.1), channel_id=1, source_target_pairs={{0,1},{1,0},{2,3},{3,2},{4,5},{5,4},{6,7},{7,6},{8,9},{9,8},{10,11... | collective-permute-start | bytes 294920 | tf_op jit(solution)/shard_map/ppermute | solution.py:387
  35.7 0.8 %copy-start.11 = (f32[80,128]{1,0:T(8,128)S(1)}, f32[80,128]{1,0:T(8,128)}, u32[]{:S(2)}) copy-start(f32[80,128]{1,0:T(8,128)} %copy-done.10) | copy-start | bytes 122884
  36.5 0.8 %copy-start.13 = (f32[80,128]{1,0:T(8,128)S(1)}, f32[80,128]{1,0:T(8,128)}, u32[]{:S(2)}) copy-start(f32[80,128]{1,0:T(8,128)} %copy-done.12) | copy-start | bytes 122884

commit v2 on v1

v2 whole, which is shorter than its diff:
```python
import functools

import jax
import jax.numpy as jnp
from jax import lax
from jax.experimental import pallas as pl
from jax.experimental.pallas import tpu as pltpu
from jax.sharding import PartitionSpec as P

stiffness = 2.0
gravity_step = 0.3

LANES = 128
SLABS = 4
ZROWS = 10
CHANNELS = 8
ROWS = ZROWS * CHANNELS
F32 = jnp.float32
BF16 = jnp.bfloat16


def iota(shape, dim):
    return lax.broadcasted_iota(jnp.int32, shape, dim)


def tile_nodes(tile, rows, brick):
    lane = iota((rows, LANES), 1)
    if tile < 2:
        x, y = lane >> 1, (lane & 1) + tile * brick
        valid = lane < 2 * (brick + 2)
    else:
        x = (lane >> 5) + ((0, brick)[tile - 2] if tile < SLABS else 4 * (tile - SLABS) + 1)
        y = (lane & 31) + 1
        valid = (y >= 2) & (y < brick)
        valid = valid & ((lane < 64) if tile < SLABS else ((x >= 2) & (x < brick)))
    return x, y, valid


def tile_code(tile, rows, brick):
    x, y, valid = tile_nodes(tile, rows, brick)
    return jnp.where(valid, x * 64 + y, -1)


def block_columns(cells_ref, blocks):
    row = iota((blocks, LANES), 0)
    cells = jnp.zeros((blocks, LANES), jnp.int32)
    for b in range(blocks):
        cells = jnp.where(row == b, cells_ref[b], cells)
    code = (cells >> 5) * 128 + ((cells >> 1) & 15) * 2
    return code, cells & 1


def fill_one_hot(hot_ref, code, first_tile, brick):
    blocks = code.shape[0]
    for at in range(hot_ref.shape[1] // LANES):
        lane_code = tile_code(first_tile + at, blocks, brick) - code
        for node in range(16):
            hit = lane_code == (node // 4) * 64 + node % 4
            hot_ref[pl.ds(node * blocks, blocks), pl.ds(at * LANES, LANES)] = jnp.where(hit, 1.0, 0.0).astype(BF16)


def deposit_windows(grid_ref, window_ref, hot_ref, all_ref):
    all_ref[...] = lax.dot_general(
        window_ref[...], hot_ref[...], (((0,), (0,)), ((), ())), preferred_element_type=F32
    )
    for z in range(ZROWS):
        piece = None
        for tz in range(2):
            wz = z - 4 * tz
            if 0 <= wz < 6:
                row = 64 * tz + 8 * wz
                part = all_ref[pl.ds(row, 8), :] + all_ref[pl.ds(128 + row, 8), :]
                piece = part if piece is None else piece + part
        for tile in range(grid_ref.shape[0]):
            grid_ref[tile, pl.ds(8 * z, 8), :] = piece[:, tile * LANES : (tile + 1) * LANES]


def spline(frac):
    return [0.5 * (0.5 - frac) ** 2, 0.75 - frac * frac, 0.5 * (0.5 + frac) ** 2]


def split(value):
    high = value.astype(BF16)
    return high, (value - high.astype(F32)).astype(BF16)


def is_even(axis):
    return lax.rem(lax.axis_index(axis), 2) == 0


def low_high(even, odd, axis):
    here = is_even(axis)
    place = lax.axis_index(axis)
    low, high = jnp.where(here, odd, even), jnp.where(here, even, odd)
    return jnp.where(place > 0, low, 0.0), jnp.where(place < lax.axis_size(axis) - 1, high, 0.0)


def diagonal_rows(ends):
    even = ends[0]
    low, high = low_high(even, ends[1] if len(ends) > 1 else jnp.zeros_like(even), "gz")
    return jnp.concatenate([low, jnp.zeros((ROWS - 32, LANES), F32), high], axis=0)


def to_rows(flat_ref, first, array_ref, blocks):
    channels = array_ref.shape[0]
    for b in range(blocks):
        flat_ref[pl.ds(first * blocks + b, channels, stride=blocks), :] = array_ref[:, pl.ds(b * LANES, LANES)]


def from_rows(array_ref, flat_ref, first, blocks):
    channels = array_ref.shape[0]
    for b in range(blocks):
        array_ref[:, pl.ds(b * LANES, LANES)] = flat_ref[pl.ds(first * blocks + b, channels, stride=blocks), :]


def corners(low, high):
    lane = iota(low.shape, 1)
    first, last = lane < 4, (lane >= 64) & (lane < 68)
    zero = jnp.zeros_like(low)
    lower = jnp.where(first, pltpu.roll(low, 64, 1), jnp.where(last, high, zero))
    upper = jnp.where(first, pltpu.roll(low, 60, 1), jnp.where(last, pltpu.roll(high, 124, 1), zero))
    return lower, upper


def spread_kernel(spread_ref, take_ref):
    particle = iota((LANES, 2 * LANES), 0)
    shift = iota((LANES, 2 * LANES), 1) - ((particle >> 5) * 64 + ((particle >> 3) & 3) * 8)
    for c in range(7):
        for oz in range(3):
            hit = shift == oz * 8 + c
            spread_ref[pl.ds((3 * c + oz) * LANES, LANES), :] = jnp.where(hit, 1.0, 0.0).astype(BF16)
    key = iota((2 * LANES, LANES), 0)
    particle = iota((2 * LANES, LANES), 1)
    shift = jnp.where((key >> 6) == (particle >> 5), (key & 31) - ((particle >> 3) & 3), -64)
    for a in range(3):
        for oz in range(3):
            hit = shift == 8 * a + oz
            take_ref[:, pl.ds((3 * a + oz) * LANES, LANES)] = jnp.where(hit, 1.0, 0.0).astype(BF16)


def deposit_kernel(*refs):
    cells_ref, count_ref, pos_ref, vel_ref, aff_ref, vol_ref, cvel_ref, caff_ref, top_ref, drag_ref = refs[:10]
    spread_ref, refs = refs[10], refs[11:]
    grid_ref, even_ref, odd_ref, diagonal_ref, meta_ref, shape_ref, window_ref, hot_ref, planes_ref = refs[:9]
    flat_ref, terms_ref, sums_ref, all_ref = refs[9:]
    blocks = vol_ref.shape[0]
    brick = drag_ref.shape[0]
    size_z = drag_ref.shape[1]
    code, upper_tile = block_columns(cells_ref, blocks)
    live_rows = iota((blocks, LANES), 0) < count_ref[0]
    meta_ref[0], meta_ref[1], meta_ref[2] = code, upper_tile, live_rows.astype(jnp.int32)
    fill_one_hot(hot_ref, code, 0, brick)
    for first, ref in ((0, pos_ref), (3, vel_ref), (6, aff_ref), (15, cvel_ref), (18, caff_ref)):
        to_rows(flat_ref, first, ref, blocks)

    def channel(c):
        return flat_ref[pl.ds(c * blocks, blocks), :]

    live = live_rows.astype(F32)
    frac = [channel(k) for k in range(3)]
    weight = [spline(f) for f in frac]
    for k, value in enumerate(weight[0] + weight[1] + weight[2] + frac):
        shape_ref[pl.ds(k * blocks, blocks), :] = value
    stretch = stiffness * (vol_ref[...] - 1.0)
    linear, matrix = [live], [None]
    for a in range(3):
        row = [live * (channel(6 + 3 * a + b) - (stretch if a == b else 0.0)) for b in range(3)]
        matrix.append(row)
        linear.append(live * channel(3 + a) - sum(row[b] * frac[b] for b in range(3)))
    for a in range(3):
        row = [(4.0 * live) * channel(18 + 3 * a + b) for b in range(3)]
        matrix.append(row)
        linear.append(live * channel(15 + a) - sum(row[b] * frac[b] for b in range(3)))

    def put(row, slot, value):
        high, low = split(value)
        lanes = pl.ds(slot * LANES, LANES)
        terms_ref[pl.ds(row * blocks, blocks), lanes] = high
        terms_ref[pl.ds((9 + row) * blocks, blocks), lanes] = low

    for ox in range(3):
        for oy in range(3):
            planar = weight[0][ox] * weight[1][oy]
            weights = [planar * weight[2][oz] for oz in range(3)]
            for c in range(7):
                base = linear[c]
                if c:
                    if ox != 1:
                        base = base + matrix[c][0] if ox else base - matrix[c][0]
                    if oy != 1:
                        base = base + matrix[c][1] if oy else base - matrix[c][1]
                for oz in range(3):
                    value = base
                    if c and oz != 1:
                        value = base + matrix[c][2] if oz else base - matrix[c][2]
                    put(3 * ox + oy, 3 * c + oz, weights[oz] * value)

    sums_ref[...] = jnp.dot(terms_ref[...], spread_ref[...], preferred_element_type=F32)

    lane = iota((blocks, LANES), 1)
    low_half = lane < 64
    own_half = low_half == (upper_tile == 0)

    def partial(wx, oy):
        total = None
        for cx in range(2):
            ox = wx - cx
            if 0 <= ox < 3:
                lanes = pl.ds(cx * LANES, LANES)
                row = 3 * ox + oy
                piece = sums_ref[pl.ds(row * blocks, blocks), lanes] + sums_ref[pl.ds((9 + row) * blocks, blocks), lanes]
                total = piece if total is None else total + piece
        return total

    for wx in range(4):
        columns = [partial(wx, oy) for oy in range(3)]
        zero = jnp.zeros_like(columns[0])
        for wy in range(4):
            both = jnp.where(low_half, columns[wy] if wy < 3 else zero, columns[wy - 1] if wy else zero)
            node = jnp.where(own_half, both + pltpu.roll(both, 64, 1), 0.0)
            high, low = split(node)
            rows = pl.ds((4 * wx + wy) * blocks, blocks)
            window_ref[rows, pl.ds(0, LANES)] = high
            window_ref[rows, pl.ds(LANES, LANES)] = low

    deposit_windows(grid_ref, window_ref, hot_ref, all_ref)

    depth = iota((size_z, brick), 0) + lax.axis_index("gz") * size_z
    lane = iota((size_z, LANES), 1)
    zero = jnp.zeros((size_z, LANES), F32)
    ends = [zero, zero]
    layers = []
    for x in range(brick):
        layer = jnp.where(depth < top_ref[pl.ds(x, 1), :], drag_ref[x], 0.0)
        layers.append(layer)
        ends[0] = jnp.where(lane == 2 * (x + 1) + 1, layer[:, 0:1], ends[0])
        ends[1] = jnp.where(lane == 2 * (x + 1), layer[:, brick - 1 : brick], ends[1])
    blank = jnp.zeros((size_z, 32), F32)
    planes = ends + [
        jnp.concatenate([blank, layers[0], blank, blank], axis=1),
        jnp.concatenate([layers[-1], blank, blank, blank], axis=1),
    ]
    for t in range(brick // 4):
        planes_ref[t] = jnp.concatenate(layers[4 * t : 4 * t + 4], axis=1)
    for tile, plane in enumerate(planes):
        grid_ref[tile, pl.ds(8 + 7, size_z, stride=8), :] = plane

    lane = iota((ROWS, LANES), 1)
    slab = [grid_ref[t] for t in range(SLABS)]
    low = jnp.where(lane < 64, slab[2], jnp.where(lane < 68, pltpu.roll(slab[0], 64, 1), pltpu.roll(slab[1], 68, 1)))
    high = jnp.where(lane < 64, slab[3], jnp.where(lane < 68, slab[0], pltpu.roll(slab[1], 4, 1)))
    here = is_even("gx")
    even_ref[...] = jnp.where(here, high, low)
    odd_ref[...] = jnp.where(here, low, high)
    here = is_even("gz")
    lower, upper = odd_ref[pl.ds(0, 16), :], odd_ref[pl.ds(ROWS - 16, 16), :]
    diagonal_ref[0] = jnp.where(here, upper, lower)
    if diagonal_ref.shape[0] > 1:
        diagonal_ref[1] = jnp.where(here, lower, upper)


def interior_kernel(brick, window_ref, meta_ref, planes_ref, grid_ref, hot_ref, all_ref):
    fill_one_hot(hot_ref, meta_ref[0], SLABS, brick)
    deposit_windows(grid_ref, window_ref, hot_ref, all_ref)
    for tile in range(grid_ref.shape[0]):
        grid_ref[tile, pl.ds(8 + 7, planes_ref.shape[1], stride=8), :] = planes_ref[tile]


def pack_z_kernel(slab_ref, grid_ref, xe_ref, even_ref, *odd_refs):
    here = is_even("gz")
    ends = []
    for first in (0, ROWS - 16):
        rows = pl.ds(first, 16)
        received = xe_ref[rows, :]
        extra = x_additions(*low_high(received, jnp.zeros_like(received), "gx"))
        ends.append([slab_ref[t, rows, :] + extra[t] for t in range(SLABS)])
        ends[-1] += [grid_ref[t, rows, :] for t in range(grid_ref.shape[0])]
    for tile, (lower, upper) in enumerate(zip(*ends)):
        even_ref[tile] = jnp.where(here, upper, lower)
        for odd_ref in odd_refs:
            odd_ref[tile] = jnp.where(here, lower, upper)


def x_additions(low, high):
    lower, upper = corners(low, high)
    planar = iota(low.shape, 1) < 64
    return [lower, upper, jnp.where(planar, low, 0.0), jnp.where(planar, high, 0.0)]


def xz_additions(xe_ref, xo_ref, diagonals, layers, tiles):
    odd = xo_ref[...] + diagonal_rows([ref[...] for ref in diagonals])
    extra = x_additions(*low_high(xe_ref[...], odd, "gx"))
    return [extra[t] + diagonal_rows([ref[t] for ref in layers]) for t in range(tiles)]


def pack_y_kernel(ends, *refs):
    slab_ref, xe_ref, xo_ref, *received = refs[:-2]
    even_ref, odd_ref = refs[-2:]
    extra = xz_additions(xe_ref, xo_ref, received[:ends], received[ends:], 2)
    lower, upper = slab_ref[0] + extra[0], slab_ref[1] + extra[1]
    here = is_even("gy")
    even_ref[...] = jnp.where(here, upper, lower)
    odd_ref[...] = jnp.where(here, lower, upper)


def collect_kernel(counts, ends, *refs):
    inputs, refs = refs[:-10], refs[-10:]
    meta_ref, shape_ref, hot_slab_ref, hot_ref, spread_ref, top_ref, slab_ref, grid_ref = inputs[:8]
    xe_ref, xo_ref, ye_ref, yo_ref, *received = inputs[8:]
    gvel_ref, gaff_ref, gvol_ref, gdrag_ref = refs[:4]
    total_ref, push_slab_ref, push_ref, take_ref, pulled_ref, flat_ref = refs[4:]
    blocks = gvol_ref.shape[0]
    brick, size_z = gdrag_ref.shape[0], gdrag_ref.shape[1]
    tiles = SLABS + grid_ref.shape[0]
    saved = [shape_ref[pl.ds(k * blocks, blocks), :] for k in range(12)]
    weight, frac = [saved[3 * k : 3 * k + 3] for k in range(3)], saved[9:]

    extra = xz_additions(xe_ref, xo_ref, received[:ends], received[ends:], SLABS)
    low, high = low_high(ye_ref[...], yo_ref[...], "gy")
    extra[0], extra[1] = extra[0] + low, extra[1] + high
    for tile in range(tiles):
        if tile < SLABS:
            total_ref[tile, pl.ds(0, ROWS), :] = slab_ref[tile] + extra[tile]
        else:
            more = diagonal_rows([ref[tile] for ref in received[ends:]])
            total_ref[tile, pl.ds(0, ROWS), :] = grid_ref[tile - SLABS] + more
        total_ref[tile, pl.ds(ROWS, 16), :] = jnp.zeros((16, LANES), F32)

    place = [lax.axis_index(axis) for axis in ("gx", "gy", "gz")]
    edges = []
    row = iota((8, LANES), 0)
    blank = jnp.zeros((8, LANES), F32)
    for tile in range(tiles):
        at = tile if tile < SLABS else tile - SLABS
        lanes = pl.ds(at * LANES, LANES)
        target_ref = push_slab_ref if tile < SLABS else push_ref
        node_x, node_y, _ = tile_nodes(tile, 8, brick)
        node_x = node_x + (place[0] * brick - 1)
        node_y = node_y + (place[1] * brick - 1)
        drags = []
        for side in range(2):
            c = [total_ref[tile, pl.ds(32 * side + k, 8, stride=8), :] for k in range(CHANNELS)]
            node_z = row + (4 * side - 1) + place[2] * size_z
            inside = (node_z >= 0) & (node_z < counts[2] * size_z)
            if tile < SLABS:
                inside = inside & (node_x >= 0) & (node_x < counts[0] * brick)
                inside = inside & (node_y >= 0) & (node_y < counts[1] * brick)
            inverse = 1.0 / jnp.maximum(c[0], 1.0)
            scale = jnp.where(inside, (1.0 - c[7]) * inverse, 0.0)
            high, low = split(jnp.concatenate([c[4 + a] * scale for a in range(3)] + [blank], axis=0))
            target_ref[pl.ds(64 * side, 32), lanes] = high
            target_ref[pl.ds(64 * side + 32, 32), lanes] = low
            drags.append(
                c[4] * (c[1] * inverse) + c[5] * (c[2] * inverse) + c[6] * (c[3] * inverse - gravity_step)
            )
        edges.append(jnp.where(row < 7, pltpu.roll(drags[0], 7, 0), pltpu.roll(drags[1], 3, 0)))

    depth = iota((size_z, brick), 0) + place[2] * size_z
    lane = iota((size_z, LANES), 1)
    for x in range(brick):
        if x == 0:
            plane = pltpu.roll(edges[2], 96, 1)
        elif x == brick - 1:
            plane = edges[3]
        else:
            plane = edges[SLABS + x // 4]
            if x % 4:
                plane = pltpu.roll(plane, LANES - 32 * (x % 4), 1)
        at = 2 * (x + 1)
        plane = jnp.where(lane == 0, edges[0][:, at + 1 : at + 2], plane)
        plane = jnp.where(lane == brick - 1, edges[1][:, at : at + 1], plane)
        gdrag_ref[x] = jnp.where(depth < top_ref[pl.ds(x, 1), :], -plane[:, :brick], 0.0)

    gathered = sum(
        lax.dot_general(hot[...], push[...], (((1,), (1,)), ((), ())), preferred_element_type=F32)
        for hot, push in ((hot_slab_ref, push_slab_ref), (hot_ref, push_ref))
    )
    lane = iota((blocks, LANES), 1)
    low_half = lane < 64
    upper = meta_ref[1] == 1
    lows, highs = [], []
    for node in range(16):
        value = gathered[node * blocks : (node + 1) * blocks]
        rolled = pltpu.roll(value, 64, 1)
        lows.append(jnp.where(upper, rolled, value))
        highs.append(jnp.where(upper, value, rolled))
    for ox in range(3):
        for oy in range(3):
            for cx in range(2):
                value = jnp.where(low_half, lows[4 * (cx + ox) + oy], highs[4 * (cx + ox) + oy + 1])
                take_ref[pl.ds((3 * ox + oy) * blocks, blocks), pl.ds(cx * LANES, LANES)] = value.astype(BF16)

    pulled_ref[...] = jnp.dot(take_ref[...], spread_ref[...], preferred_element_type=F32)

    live = meta_ref[2].astype(F32)
    planar = [[live * weight[0][ox] * weight[1][oy] for oy in range(3)] for ox in range(3)]
    trace = None
    for a in range(3):
        sums_x, sums_y, sums_z = [], [None] * 3, None
        for ox in range(3):
            column = None
            for oy in range(3):
                rows = pl.ds((3 * ox + oy) * blocks, blocks)
                g = [pulled_ref[rows, pl.ds((3 * a + oz) * LANES, LANES)] for oz in range(3)]
                below, above = weight[2][0] * g[0], weight[2][2] * g[2]
                sum_z = planar[ox][oy] * (weight[2][1] * g[1] + (below + above))
                slope = planar[ox][oy] * (above - below)
                column = sum_z if column is None else column + sum_z
                sums_y[oy] = sum_z if sums_y[oy] is None else sums_y[oy] + sum_z
                sums_z = slope if sums_z is None else sums_z + slope
            sums_x.append(column)
        whole = sums_x[0] + sums_x[1] + sums_x[2]
        moments = [sums_x[2] - sums_x[0], sums_y[2] - sums_y[0], sums_z]
        flat_ref[pl.ds(a * blocks, blocks), :] = whole
        for b in range(3):
            value = moments[b] - frac[b] * whole
            flat_ref[pl.ds((3 + 3 * a + b) * blocks, blocks), :] = value
            if a == b:
                trace = value if trace is None else trace + value
    gvol_ref[...] = -stiffness * trace
    from_rows(gvel_ref, flat_ref, 0, blocks)
    from_rows(gaff_ref, flat_ref, 3, blocks)


def paired(index, count, first):
    partner = index + 1 if (index - first) % 2 == 0 else index - 1
    return partner if 0 <= partner < count else None


def exchange(array, counts, pair):
    names = ("gx", "gy", "gz")
    links = []
    for x in range(counts[0]):
        for y in range(counts[1]):
            for z in range(counts[2]):
                target = pair(x, y, z)
                if None not in target:
                    links.append(((x * counts[1] + y) * counts[2] + z, (target[0] * counts[1] + target[1]) * counts[2] + target[2]))
    return lax.ppermute(array, names, links) if links else jnp.zeros_like(array)


def shards(
    offsets, velocity, affine, volume, cot_velocity, cot_affine, block_cells, fill_counts, baffle_top, drag
):
    brick, _, size_z = drag.shape
    blocks = block_cells.shape[0]
    counts = tuple(lax.axis_size(axis) for axis in ("gx", "gy", "gz"))
    interior = brick // 4
    smem = pl.BlockSpec(memory_space=pltpu.SMEM)
    vmem = pl.BlockSpec(memory_space=pltpu.VMEM)

    def f32(*shape):
        return jax.ShapeDtypeStruct(shape, F32)

    def bf16(*shape):
        return jax.ShapeDtypeStruct(shape, BF16)

    def call(kernel, name, out_shape, operands, in_specs=None, scratch=(), megabytes=4, flops=0):
        return pl.pallas_call(
            kernel,
            out_shape=out_shape,
            in_specs=in_specs or [vmem] * len(operands),
            out_specs=(vmem,) * len(out_shape),
            scratch_shapes=scratch,
            compiler_params=pltpu.CompilerParams(vmem_limit_bytes=megabytes * 1024 * 1024),
            cost_estimate=pl.CostEstimate(flops=flops, bytes_accessed=1024, transcendentals=0),
            name=name,
        )(*operands)

    operands = (
        block_cells, fill_counts, offsets, velocity, affine, volume.reshape(blocks, LANES), cot_velocity, cot_affine,
        baffle_top, drag.transpose(0, 2, 1),
    )
    slab = f32(ROWS, LANES)
    ends = 2 if counts[2] > 2 else 1
    spread, take = call(
        spread_kernel, "spread", (bf16(21 * LANES, 2 * LANES), bf16(2 * LANES, 9 * LANES)), (), flops=20_000_000_000
    )
    edge, send_xe, send_xo, send_xz, meta, shape, window, hot_edge, planes = call(
        deposit_kernel,
        "deposit",
        (
            f32(SLABS, ROWS, LANES), slab, slab, f32(ends, 16, LANES),
            jax.ShapeDtypeStruct((3, blocks, LANES), jnp.int32), f32(12 * blocks, LANES),
            bf16(16 * blocks, 2 * LANES), bf16(16 * blocks, SLABS * LANES), f32(interior, size_z, LANES),
        ),
        operands + (spread,),
        in_specs=[smem, smem] + [vmem] * 9,
        scratch=[
            pltpu.VMEM((27 * blocks, LANES), F32),
            pltpu.VMEM((18 * blocks, 21 * LANES), BF16),
            pltpu.VMEM((18 * blocks, 2 * LANES), F32),
            pltpu.VMEM((2 * LANES, SLABS * LANES), F32),
        ],
        megabytes=16,
    )

    def even_x(x):
        return paired(x, counts[0], 0)

    def odd_x(x):
        partner = paired(x, counts[0], 1)
        return counts[0] - 1 - x if partner is None and counts[0] % 2 == 0 else partner

    def odd_y(x, y, z):
        partner = paired(y, counts[1], 1)
        return (even_x(x), y, z) if partner is None else (x, partner, z)

    xe = exchange(send_xe, counts, lambda x, y, z: (even_x(x), y, z))
    xo = exchange(send_xo, counts, lambda x, y, z: (odd_x(x), y, z))
    xz = [
        exchange(send_xz[first], counts, lambda x, y, z: (odd_x(x), y, paired(z, counts[2], first)))
        for first in range(ends)
    ]
    grid, hot = call(
        functools.partial(interior_kernel, brick),
        "interior",
        (f32(interior, ROWS, LANES), bf16(16 * blocks, interior * LANES)),
        (window, meta, planes),
        scratch=[pltpu.VMEM((2 * LANES, interior * LANES), F32)],
        megabytes=8,
        flops=1_000_000_000,
    )
    send_z = call(pack_z_kernel, "pack_z", (f32(SLABS + interior, 16, LANES),) * ends, (edge, grid, xe))
    layers = [
        exchange(array, counts, lambda x, y, z: (x, y, paired(z, counts[2], first)))
        for first, array in enumerate(send_z)
    ]
    send_ye, send_yo = call(
        functools.partial(pack_y_kernel, ends), "pack_y", (slab, slab), (edge, xe, xo, *xz, *layers)
    )
    yo = exchange(send_yo, counts, odd_y)
    ye = exchange(send_ye, counts, lambda x, y, z: (x, paired(y, counts[1], 0), z))
    grad_velocity, grad_affine, grad_volume, grad_drag = call(
        functools.partial(collect_kernel, counts, ends),
        "collect",
        (f32(3, blocks * LANES), f32(9, blocks * LANES), f32(blocks, LANES), f32(brick, size_z, brick)),
        (meta, shape, hot_edge, hot, take, baffle_top, edge, grid, xe, xo, ye, yo, *xz, *layers),
        scratch=[
            pltpu.VMEM((SLABS + interior, ROWS + 16, LANES), F32),
            pltpu.VMEM((LANES, SLABS * LANES), BF16),
            pltpu.VMEM((LANES, interior * LANES), BF16),
            pltpu.VMEM((9 * blocks, 2 * LANES), BF16),
            pltpu.VMEM((9 * blocks, 9 * LANES), F32),
            pltpu.VMEM((12 * blocks, LANES), F32),
        ],
        megabytes=16,
    )
    return grad_velocity, grad_affine, grad_volume.reshape(-1), grad_drag.transpose(0, 2, 1)


def solution(mesh):
    everywhere = ("gx", "gy", "gz")
    rows, flat = P(None, everywhere), P(everywhere)
    in_specs = (rows, rows, rows, flat, rows, rows, flat, flat, P("gx", "gy"), P("gx", "gy", "gz"))
    out_specs = (rows, rows, flat, P("gx", "gy", "gz"))
    return jax.shard_map(shards, mesh=mesh, in_specs=in_specs, out_specs=out_specs, check_vma=False)
```

time: 40.8 us -> 20.6 us (0.50)
  the two profiles are of different devices: /device:TPU:18 before, /device:TPU:0 now
where the time goes in v2:
time: 20.6 us; the launch traced here: 20.5 us
  starting transfers between devices  6.7 us (33%)
  waiting for transfers between devices  6.15 us (30%)
  Pallas kernels  6.12 us (30%)
  between operations  1.46 us (7%)
    ppermute x6, starting transfers between devices, exchange(): return lax.ppermute(array, names, links) if links else jnp.zeros_like(array)  6.7 us
    ppermute x6, waiting for transfers between devices, exchange(): return lax.ppermute(array, names, links) if links else jnp.zeros_like(array)  6.15 us
    pallas_call x6, Pallas kernels, call(): pl.pallas_call(kernel, out_shape=out_shape, in_specs=in_specs or [vmem] *...  6.12 us
  transfers between devices with their start and end apart: 6, of which 3 were waited for; matrix products, arithmetic and copies ran while one was open for 0% of the time, Pallas kernels for 3%

profile of v2, /device:TPU:0, one launch (start us, length us, event | category | flops | bytes accessed | tf_op | source)
XLA Modules:
  0.0 20.5 jit_solution(8022570436570038546)
XLA Ops:
  0.6 0.0 copy-start.3
  0.6 0.0 copy-start.2
  0.7 0.0 copy-start.8
  0.7 0.0 copy-start.1
  0.7 0.0 copy-start.6
  0.7 0.0 copy-start.7
  0.7 0.0 copy-start
  0.7 0.0 copy-start.5
  0.7 0.0 copy-start.4
  0.7 0.4 %spread.1 = (bf16[2688,256]{1,0:T(8,128)(2,1)S(1)}, bf16[256,1152]{1,0:T(8,128)(2,1)S(1)}) custom-call(), custom_call_target="tpu_custom_call" | custom-call | flops 20000000000 | bytes 1024 | tf_op jit(solution)/shard_map/spread/pallas_call | solution.py:459
  1.8 0.0 copy-done.3
  1.8 0.0 copy-done.2
  1.8 0.0 copy-done.8
  1.8 0.0 copy-done.1
  1.8 0.0 copy-done.6
  1.8 0.0 copy-done.7
  1.8 0.0 copy-done
  1.8 0.0 copy-done.5
  1.9 0.0 copy-done.4
  1.9 2.7 %deposit.1 = (f32[4,80,128]{2,1,0:T(8,128)S(1)}, f32[80,128]{1,0:T(8,128)S(1)}, f32[80,128]{1,0:T(8,128)S(1)}, f32[1,16,128]{2,1,0:T(8,128)S(1)}, s32[3,32,128]{...) custom-call(s32[32]{0:T(128)S(1)} %copy-done.8, ...), custom_call_target="tpu_custom_call" | custom-call | bytes 1024 | tf_op jit(solution)/shard_map/deposit/pallas_call | solution.py:459
  4.5 0.5 %collective-permute-start = (f32[80,128]{1,0:T(8,128)S(1)}, f32[80,128]{1,0:T(8,128)S(1)}, u32[]{:S(2)}, u32[]{:S(2)}) collective-permute-start(f32[80,128]{1,0:T(8,128)S(1)} %get-tuple-element.33), channel_id=1, source_target_pairs={{0,8},{1,9},{2,10},{3,11},{4,12},{5,13},{6,14},{7,15},{8,0},{9,1},... | collective-permute-start | bytes 122888 | tf_op jit(solution)/shard_map/ppermute | solution.py:439
  5.1 0.6 %interior.1 = (f32[8,80,128]{2,1,0:T(8,128)S(1)}, bf16[512,1024]{1,0:T(8,128)(2,1)S(1)}) custom-call(bf16[512,256]{1,0:T(8,128)(2,1)S(1)} %get-tuple-element.27.window_ref, s32[3,32,128]{2,1,0:T(8,128)S(1)} %get-tuple-element.24.meta_ref.refs_0_, f32[8,8,128]{2,1,0:T(8,128)S(1)} %get-tuple-element.28.planes_ref), custom_call_target="tpu_custom_call" | custom-call | flops 1000000000 | bytes 1024 | tf_op jit(solution)/shard_map/interior/pallas_call | solution.py:459
  5.7 0.3 %collective-permute-done.xe_ref.refs_1_.refs_8_ = f32[80,128]{1,0:T(8,128)S(1)} collective-permute-done((f32[80,128]{1,0:T(8,128)S(1)}, f32[80,128]{1,0:T(8,128)S(1)}, u32[]{:S(2)}, u32[]{:S(2)}) %collective-permute-start) | collective-permute-done | bytes 40992 | tf_op jit(solution)/shard_map/ppermute | solution.py:439
  5.9 0.1 pack_z.1
  6.0 2.9 %collective-permute-start.3 = (f32[12,16,128]{2,1,0:T(8,128)S(1)}, f32[12,16,128]{2,1,0:T(8,128)S(1)}, u32[]{:S(2)}, u32[]{:S(2)}) collective-permute-start(f32[12,16,128]{2,1,0:T(8,128)S(1)} %pack_z.1), channel_id=1, source_target_pairs={{0,1},{1,0},{2,3},{3,2},{4,5},{5,4},{6,7},{7,6},{8,9},{9,8},{10,11... | collective-permute-start | bytes 294920 | tf_op jit(solution)/shard_map/ppermute | solution.py:439
  9.0 1.0 %collective-permute-start.1 = (f32[80,128]{1,0:T(8,128)S(1)}, f32[80,128]{1,0:T(8,128)S(1)}, u32[]{:S(2)}, u32[]{:S(2)}) collective-permute-start(f32[80,128]{1,0:T(8,128)S(1)} %get-tuple-element.34), channel_id=1, source_target_pairs={{0,24},{1,25},{2,26},{3,27},{4,28},{5,29},{6,30},{7,31},{8,16},{9,... | collective-permute-start | bytes 122888 | tf_op jit(solution)/shard_map/ppermute | solution.py:439
  9.9 0.3 %collective-permute-start.2 = (f32[16,128]{1,0:T(8,128)S(1)}, f32[16,128]{1,0:T(8,128)S(1)}, u32[]{:S(2)}, u32[]{:S(2)}) collective-permute-start(f32[16,128]{1,0:T(8,128)S(1)} %bitcast.7), channel_id=1, source_target_pairs={{0,25},{1,24},{2,27},{3,26},{4,29},{5,28},{6,31},{7,30},{8,17},{9,... | collective-permute-start | bytes 24584 | tf_op jit(solution)/shard_map/ppermute | solution.py:439
  10.2 3.7 %collective-permute-done.2.refs_3_.refs_12_ = f32[16,128]{1,0:T(8,128)S(1)} collective-permute-done((f32[16,128]{1,0:T(8,128)S(1)}, f32[16,128]{1,0:T(8,128)S(1)}, u32[]{:S(2)}, u32[]{:S(2)}) %collective-permute-start.2) | collective-permute-done | bytes 8224 | tf_op jit(solution)/shard_map/ppermute | solution.py:439
  13.9 0.0 collective-permute-done.1.refs_2_.refs_9_
  13.9 0.0 collective-permute-done.3.refs_4_.refs_13_
  13.9 0.1 pack_y.1
  14.0 1.6 %collective-permute-start.4 = (f32[80,128]{1,0:T(8,128)S(1)}, f32[80,128]{1,0:T(8,128)S(1)}, u32[]{:S(2)}, u32[]{:S(2)}) collective-permute-start(f32[80,128]{1,0:T(8,128)S(1)} %get-tuple-element.36), channel_id=1, source_target_pairs={{0,2},{1,3},{2,0},{3,1},{4,6},{5,7},{6,4},{7,5},{8,10},{9,11},{10,... | collective-permute-start | bytes 122888 | tf_op jit(solution)/shard_map/ppermute | solution.py:439
  15.7 0.3 %collective-permute-start.5 = (f32[80,128]{1,0:T(8,128)S(1)}, f32[80,128]{1,0:T(8,128)S(1)}, u32[]{:S(2)}, u32[]{:S(2)}) collective-permute-start(f32[80,128]{1,0:T(8,128)S(1)} %get-tuple-element.37), channel_id=1, source_target_pairs={{0,8},{1,9},{2,4},{3,5},{4,2},{5,3},{6,14},{7,15},{8,0},{9,1},{10,... | collective-permute-start | bytes 122888 | tf_op jit(solution)/shard_map/ppermute | solution.py:439
  16.0 2.2 %collective-permute-done.4.refs_10_ = f32[80,128]{1,0:T(8,128)S(1)} collective-permute-done((f32[80,128]{1,0:T(8,128)S(1)}, f32[80,128]{1,0:T(8,128)S(1)}, u32[]{:S(2)}, u32[]{:S(2)}) %collective-permute-start.4) | collective-permute-done | bytes 40992 | tf_op jit(solution)/shard_map/ppermute | solution.py:439
  18.2 0.0 collective-permute-done.5.refs_11_
  18.2 2.3 %collect.1 = (f32[3,4096]{1,0:T(4,128)}, f32[9,4096]{1,0:T(8,128)}, f32[32,128]{1,0:T(8,128)}, f32[32,8,32]{2,1,0:T(8,128)}) custom-call(s32[3,32,128]{2,1,0:T(8,128)S(1)} %get-tuple-element.24.meta_ref.refs_0_, f32[384,128]{1,0:T(8,128)S(1)} %get-tuple-element.25.refs_1_, bf16[512,512]{1,0:T(8,128)(2,1)S(1)} %get-tuple-element.26.refs_2_, ...), custom_call_target="tpu_custom_call" | custom-call | bytes 1024 | tf_op jit(solution)/shard_map/collect/pallas_call | solution.py:459
Async XLA Ops:
  0.6 1.1 %copy-start.3 = (s32[32,32]{1,0:T(8,128)S(1)}, s32[32,32]{1,0:T(8,128)}, u32[]{:S(2)}) copy-start(s32[32,32]{1,0:T(8,128)} %refs_5_.1) | copy-start | bytes 12292
  0.6 1.1 %copy-start.2 = (f32[32,32,8]{1,2,0:T(8,128)S(1)}, f32[32,32,8]{1,2,0:T(8,128)}, u32[]{:S(2)}) copy-start(f32[32,32,8]{1,2,0:T(8,128)} %param.19) | copy-start | bytes 98308
  0.7 1.1 %copy-start.8 = (s32[32]{0:T(128)S(1)}, s32[32]{0:T(128)}, u32[]{:S(2)}) copy-start(s32[32]{0:T(128)} %refs_0_.1) | copy-start | bytes 388
  0.7 1.1 %copy-start.1 = (f32[9,4096]{1,0:T(8,128)S(1)}, f32[9,4096]{1,0:T(8,128)}, u32[]{:S(2)}) copy-start(f32[9,4096]{1,0:T(8,128)} %refs_7_.1) | copy-start | bytes 442372
  0.7 1.1 %copy-start.6 = (f32[3,4096]{1,0:T(4,128)S(1)}, f32[3,4096]{1,0:T(4,128)}, u32[]{:S(2)}) copy-start(f32[3,4096]{1,0:T(4,128)} %refs_6_.1) | copy-start | bytes 147460
  0.7 1.1 %copy-start.7 = (f32[4096]{0:T(1024)S(1)}, f32[4096]{0:T(1024)}, u32[]{:S(2)}) copy-start(f32[4096]{0:T(1024)} %param.13) | copy-start | bytes 49156
  0.7 1.1 %copy-start = (f32[9,4096]{1,0:T(8,128)S(1)}, f32[9,4096]{1,0:T(8,128)}, u32[]{:S(2)}) copy-start(f32[9,4096]{1,0:T(8,128)} %refs_4_.1) | copy-start | bytes 442372
  0.7 1.1 %copy-start.5 = (f32[3,4096]{1,0:T(4,128)S(1)}, f32[3,4096]{1,0:T(4,128)}, u32[]{:S(2)}) copy-start(f32[3,4096]{1,0:T(4,128)} %refs_3_.1) | copy-start | bytes 147460
  0.7 1.1 %copy-start.4 = (f32[3,4096]{1,0:T(4,128)S(1)}, f32[3,4096]{1,0:T(4,128)}, u32[]{:S(2)}) copy-start(f32[3,4096]{1,0:T(4,128)} %refs_2_.1) | copy-start | bytes 147460
  4.5 1.4 %collective-permute-start = (f32[80,128]{1,0:T(8,128)S(1)}, f32[80,128]{1,0:T(8,128)S(1)}, u32[]{:S(2)}, u32[]{:S(2)}) collective-permute-start(f32[80,128]{1,0:T(8,128)S(1)} %get-tuple-element.33), channel_id=1, source_target_pairs={{0,8},{1,9},{2,10},{3,11},{4,12},{5,13},{6,14},{7,15},{8,0},{9,1},... | collective-permute-start | bytes 122888 | tf_op jit(solution)/shard_map/ppermute | solution.py:439
  6.0 7.9 %collective-permute-start.3 = (f32[12,16,128]{2,1,0:T(8,128)S(1)}, f32[12,16,128]{2,1,0:T(8,128)S(1)}, u32[]{:S(2)}, u32[]{:S(2)}) collective-permute-start(f32[12,16,128]{2,1,0:T(8,128)S(1)} %pack_z.1), channel_id=1, source_target_pairs={{0,1},{1,0},{2,3},{3,2},{4,5},{5,4},{6,7},{7,6},{8,9},{9,8},{10,11... | collective-permute-start | bytes 294920 | tf_op jit(solution)/shard_map/ppermute | solution.py:439
  9.0 5.0 %collective-permute-start.1 = (f32[80,128]{1,0:T(8,128)S(1)}, f32[80,128]{1,0:T(8,128)S(1)}, u32[]{:S(2)}, u32[]{:S(2)}) collective-permute-start(f32[80,128]{1,0:T(8,128)S(1)} %get-tuple-element.34), channel_id=1, source_target_pairs={{0,24},{1,25},{2,26},{3,27},{4,28},{5,29},{6,30},{7,31},{8,16},{9,... | collective-permute-start | bytes 122888 | tf_op jit(solution)/shard_map/ppermute | solution.py:439
  9.9 4.0 %collective-permute-start.2 = (f32[16,128]{1,0:T(8,128)S(1)}, f32[16,128]{1,0:T(8,128)S(1)}, u32[]{:S(2)}, u32[]{:S(2)}) collective-permute-start(f32[16,128]{1,0:T(8,128)S(1)} %bitcast.7), channel_id=1, source_target_pairs={{0,25},{1,24},{2,27},{3,26},{4,29},{5,28},{6,31},{7,30},{8,17},{9,... | collective-permute-start | bytes 24584 | tf_op jit(solution)/shard_map/ppermute | solution.py:439
  14.0 4.2 %collective-permute-start.4 = (f32[80,128]{1,0:T(8,128)S(1)}, f32[80,128]{1,0:T(8,128)S(1)}, u32[]{:S(2)}, u32[]{:S(2)}) collective-permute-start(f32[80,128]{1,0:T(8,128)S(1)} %get-tuple-element.36), channel_id=1, source_target_pairs={{0,2},{1,3},{2,0},{3,1},{4,6},{5,7},{6,4},{7,5},{8,10},{9,11},{10,... | collective-permute-start | bytes 122888 | tf_op jit(solution)/shard_map/ppermute | solution.py:439
  15.7 2.5 %collective-permute-start.5 = (f32[80,128]{1,0:T(8,128)S(1)}, f32[80,128]{1,0:T(8,128)S(1)}, u32[]{:S(2)}, u32[]{:S(2)}) collective-permute-start(f32[80,128]{1,0:T(8,128)S(1)} %get-tuple-element.37), channel_id=1, source_target_pairs={{0,8},{1,9},{2,4},{3,5},{4,2},{5,3},{6,14},{7,15},{8,0},{9,1},{10,... | collective-permute-start | bytes 122888 | tf_op jit(solution)/shard_map/ppermute | solution.py:439

commit v3 on v2

--- a/solution.py
+++ b/solution.py
@@ -41,13 +41,12 @@
     return jnp.where(valid, x * 64 + y, -1)
 
 
-def block_columns(cells_ref, blocks):
-    row = iota((blocks, LANES), 0)
-    cells = jnp.zeros((blocks, LANES), jnp.int32)
-    for b in range(blocks):
-        cells = jnp.where(row == b, cells_ref[b], cells)
-    code = (cells >> 5) * 128 + ((cells >> 1) & 15) * 2
-    return code, cells & 1
+def block_columns(cells_ref):
+    blocks = cells_ref.shape[1]
+    same = iota((blocks, blocks), 0) == iota((blocks, blocks), 1)
+    column = jnp.sum(jnp.where(same, cells_ref[...].astype(F32), 0.0), axis=1, keepdims=True)
+    cells = jnp.broadcast_to(column, (blocks, LANES)).astype(jnp.int32)
+    return (cells >> 5) * 128 + ((cells >> 1) & 15) * 2, cells & 1
 
 
 def fill_one_hot(hot_ref, code, first_tile, brick):
@@ -146,8 +145,8 @@
     blocks = vol_ref.shape[0]
     brick = drag_ref.shape[0]
     size_z = drag_ref.shape[1]
-    code, upper_tile = block_columns(cells_ref, blocks)
-    live_rows = iota((blocks, LANES), 0) < count_ref[0]
+    code, upper_tile = block_columns(cells_ref)
+    live_rows = iota((blocks, LANES), 0) < count_ref[...]
     meta_ref[0], meta_ref[1], meta_ref[2] = code, upper_tile, live_rows.astype(jnp.int32)
     fill_one_hot(hot_ref, code, 0, brick)
     for first, ref in ((0, pos_ref), (3, vel_ref), (6, aff_ref), (15, cvel_ref), (18, caff_ref)):
@@ -303,43 +302,20 @@
     odd_ref[...] = jnp.where(here, lower, upper)
 
 
-def collect_kernel(counts, ends, *refs):
-    inputs, refs = refs[:-10], refs[-10:]
-    meta_ref, shape_ref, hot_slab_ref, hot_ref, spread_ref, top_ref, slab_ref, grid_ref = inputs[:8]
-    xe_ref, xo_ref, ye_ref, yo_ref, *received = inputs[8:]
-    gvel_ref, gaff_ref, gvol_ref, gdrag_ref = refs[:4]
-    total_ref, push_slab_ref, push_ref, take_ref, pulled_ref, flat_ref = refs[4:]
-    blocks = gvol_ref.shape[0]
-    brick, size_z = gdrag_ref.shape[0], gdrag_ref.shape[1]
-    tiles = SLABS + grid_ref.shape[0]
-    saved = [shape_ref[pl.ds(k * blocks, blocks), :] for k in range(12)]
-    weight, frac = [saved[3 * k : 3 * k + 3] for k in range(3)], saved[9:]
-
-    extra = xz_additions(xe_ref, xo_ref, received[:ends], received[ends:], SLABS)
-    low, high = low_high(ye_ref[...], yo_ref[...], "gy")
-    extra[0], extra[1] = extra[0] + low, extra[1] + high
-    for tile in range(tiles):
-        if tile < SLABS:
-            total_ref[tile, pl.ds(0, ROWS), :] = slab_ref[tile] + extra[tile]
-        else:
-            more = diagonal_rows([ref[tile] for ref in received[ends:]])
-            total_ref[tile, pl.ds(0, ROWS), :] = grid_ref[tile - SLABS] + more
-        total_ref[tile, pl.ds(ROWS, 16), :] = jnp.zeros((16, LANES), F32)
-
+def node_gradients(counts, brick, size_z, tiles, totals, total_ref, push_ref, drag_ref):
     place = [lax.axis_index(axis) for axis in ("gx", "gy", "gz")]
-    edges = []
     row = iota((8, LANES), 0)
     blank = jnp.zeros((8, LANES), F32)
-    for tile in range(tiles):
-        at = tile if tile < SLABS else tile - SLABS
+    for at, (tile, total) in enumerate(zip(tiles, totals)):
+        total_ref[at, pl.ds(0, ROWS), :] = total
+        total_ref[at, pl.ds(ROWS, 16), :] = jnp.zeros((16, LANES), F32)
         lanes = pl.ds(at * LANES, LANES)
-        target_ref = push_slab_ref if tile < SLABS else push_ref
         node_x, node_y, _ = tile_nodes(tile, 8, brick)
         node_x = node_x + (place[0] * brick - 1)
         node_y = node_y + (place[1] * brick - 1)
         drags = []
         for side in range(2):
-            c = [total_ref[tile, pl.ds(32 * side + k, 8, stride=8), :] for k in range(CHANNELS)]
+            c = [total_ref[at, pl.ds(32 * side + k, 8, stride=8), :] for k in range(CHANNELS)]
             node_z = row + (4 * side - 1) + place[2] * size_z
             inside = (node_z >= 0) & (node_z < counts[2] * size_z)
             if tile < SLABS:
@@ -348,22 +324,59 @@
             inverse = 1.0 / jnp.maximum(c[0], 1.0)
             scale = jnp.where(inside, (1.0 - c[7]) * inverse, 0.0)
             high, low = split(jnp.concatenate([c[4 + a] * scale for a in range(3)] + [blank], axis=0))
-            target_ref[pl.ds(64 * side, 32), lanes] = high
-            target_ref[pl.ds(64 * side + 32, 32), lanes] = low
+            push_ref[pl.ds(64 * side, 32), lanes] = high
+            push_ref[pl.ds(64 * side + 32, 32), lanes] = low
             drags.append(
                 c[4] * (c[1] * inverse) + c[5] * (c[2] * inverse) + c[6] * (c[3] * inverse - gravity_step)
             )
-        edges.append(jnp.where(row < 7, pltpu.roll(drags[0], 7, 0), pltpu.roll(drags[1], 3, 0)))
-
-    depth = iota((size_z, brick), 0) + place[2] * size_z
+        drag_ref[at] = jnp.where(row < 7, pltpu.roll(drags[0], 7, 0), pltpu.roll(drags[1], 3, 0))
+
+
+def gather(hot, push_ref):
+    return lax.dot_general(hot, push_ref[...], (((1,), (1,)), ((), ())), preferred_element_type=F32)
+
+
+def early_kernel(counts, ends, size_z, *refs):
+    inputs, refs = refs[:-7], refs[-7:]
+    hot_slab_ref, hot_ref, slab_ref, grid_ref, xe_ref, xo_ref, *received = inputs
+    gathered_ref, drag_slab_ref, drag_ref, total_ref, push_slab_ref, push_ref, _ = refs
+    brick = 4 * grid_ref.shape[0]
+    extra = xz_additions(xe_ref, xo_ref, received[:ends], received[ends:], SLABS)
+    totals = [slab_ref[tile] + extra[tile] for tile in (2, 3)]
+    node_gradients(counts, brick, size_z, (2, 3), totals, total_ref, push_slab_ref, drag_slab_ref)
+    tiles = range(SLABS, SLABS + grid_ref.shape[0])
+    totals = [grid_ref[t - SLABS] + diagonal_rows([ref[t] for ref in received[ends:]]) for t in tiles]
+    node_gradients(counts, brick, size_z, tiles, totals, total_ref, push_ref, drag_ref)
+    gathered_ref[...] = gather(hot_slab_ref[:, pl.ds(2 * LANES, 2 * LANES)], push_slab_ref) + gather(hot_ref[...], push_ref)
+
+
+def collect_kernel(counts, ends, *refs):
+    inputs, refs = refs[:-10], refs[-10:]
+    meta_ref, shape_ref, hot_slab_ref, take_spread_ref, top_ref, gathered_ref, drag_slab_ref, drag_ref = inputs[:8]
+    slab_ref, xe_ref, xo_ref, ye_ref, yo_ref, *received = inputs[8:]
+    gvel_ref, gaff_ref, gvol_ref, gdrag_ref = refs[:4]
+    total_ref, push_ref, drag_ends_ref, take_ref, pulled_ref, flat_ref = refs[4:]
+    blocks = gvol_ref.shape[0]
+    brick, size_z = gdrag_ref.shape[0], gdrag_ref.shape[1]
+    saved = [shape_ref[pl.ds(k * blocks, blocks), :] for k in range(12)]
+    weight, frac = [saved[3 * k : 3 * k + 3] for k in range(3)], saved[9:]
+
+    extra = xz_additions(xe_ref, xo_ref, received[:ends], received[ends:], 2)
+    low, high = low_high(ye_ref[...], yo_ref[...], "gy")
+    totals = [slab_ref[0] + extra[0] + low, slab_ref[1] + extra[1] + high]
+    node_gradients(counts, brick, size_z, (0, 1), totals, total_ref, push_ref, drag_ends_ref)
+    gathered = gathered_ref[...] + gather(hot_slab_ref[:, pl.ds(0, 2 * LANES)], push_ref)
+
+    edges = [drag_ends_ref[t] for t in range(2)]
+    depth = iota((size_z, brick), 0) + lax.axis_index("gz") * size_z
     lane = iota((size_z, LANES), 1)
     for x in range(brick):
         if x == 0:
-            plane = pltpu.roll(edges[2], 96, 1)
+            plane = pltpu.roll(drag_slab_ref[0], 96, 1)
         elif x == brick - 1:
-            plane = edges[3]
+            plane = drag_slab_ref[1]
         else:
-            plane = edges[SLABS + x // 4]
+            plane = drag_ref[x // 4]
             if x % 4:
                 plane = pltpu.roll(plane, LANES - 32 * (x % 4), 1)
         at = 2 * (x + 1)
@@ -371,10 +384,6 @@
         plane = jnp.where(lane == brick - 1, edges[1][:, at : at + 1], plane)
         gdrag_ref[x] = jnp.where(depth < top_ref[pl.ds(x, 1), :], -plane[:, :brick], 0.0)
 
-    gathered = sum(
-        lax.dot_general(hot[...], push[...], (((1,), (1,)), ((), ())), preferred_element_type=F32)
-        for hot, push in ((hot_slab_ref, push_slab_ref), (hot_ref, push_ref))
-    )
     lane = iota((blocks, LANES), 1)
     low_half = lane < 64
     upper = meta_ref[1] == 1
@@ -390,7 +399,7 @@
                 value = jnp.where(low_half, lows[4 * (cx + ox) + oy], highs[4 * (cx + ox) + oy + 1])
                 take_ref[pl.ds((3 * ox + oy) * blocks, blocks), pl.ds(cx * LANES, LANES)] = value.astype(BF16)
 
-    pulled_ref[...] = jnp.dot(take_ref[...], spread_ref[...], preferred_element_type=F32)
+    pulled_ref[...] = jnp.dot(take_ref[...], take_spread_ref[...], preferred_element_type=F32)
 
     live = meta_ref[2].astype(F32)
     planar = [[live * weight[0][ox] * weight[1][oy] for oy in range(3)] for ox in range(3)]
@@ -446,7 +455,6 @@
     blocks = block_cells.shape[0]
     counts = tuple(lax.axis_size(axis) for axis in ("gx", "gy", "gz"))
     interior = brick // 4
-    smem = pl.BlockSpec(memory_space=pltpu.SMEM)
     vmem = pl.BlockSpec(memory_space=pltpu.VMEM)
 
     def f32(*shape):
@@ -455,11 +463,11 @@
     def bf16(*shape):
         return jax.ShapeDtypeStruct(shape, BF16)
 
-    def call(kernel, name, out_shape, operands, in_specs=None, scratch=(), megabytes=4, flops=0):
+    def call(kernel, name, out_shape, operands, scratch=(), megabytes=4, flops=0):
         return pl.pallas_call(
             kernel,
             out_shape=out_shape,
-            in_specs=in_specs or [vmem] * len(operands),
+            in_specs=[vmem] * len(operands),
             out_specs=(vmem,) * len(out_shape),
             scratch_shapes=scratch,
             compiler_params=pltpu.CompilerParams(vmem_limit_bytes=megabytes * 1024 * 1024),
@@ -468,7 +476,7 @@
         )(*operands)
 
     operands = (
-        block_cells, fill_counts, offsets, velocity, affine, volume.reshape(blocks, LANES), cot_velocity, cot_affine,
+        block_cells.reshape(1, blocks), fill_counts.reshape(1, 1), offsets, velocity, affine, volume.reshape(blocks, LANES), cot_velocity, cot_affine,
         baffle_top, drag.transpose(0, 2, 1),
     )
     slab = f32(ROWS, LANES)
@@ -485,7 +493,6 @@
             bf16(16 * blocks, 2 * LANES), bf16(16 * blocks, SLABS * LANES), f32(interior, size_z, LANES),
         ),
         operands + (spread,),
-        in_specs=[smem, smem] + [vmem] * 9,
         scratch=[
             pltpu.VMEM((27 * blocks, LANES), F32),
             pltpu.VMEM((18 * blocks, 21 * LANES), BF16),
@@ -531,20 +538,34 @@
     )
     yo = exchange(send_yo, counts, odd_y)
     ye = exchange(send_ye, counts, lambda x, y, z: (x, paired(y, counts[1], 0), z))
+    gathered, drag_slab, drag_rows = call(
+        functools.partial(early_kernel, counts, ends, size_z),
+        "early",
+        (f32(16 * blocks, LANES), f32(2, size_z, LANES), f32(interior, size_z, LANES)),
+        (hot_edge, hot, edge, grid, xe, xo, *xz, *layers),
+        scratch=[
+            pltpu.VMEM((interior, ROWS + 16, LANES), F32),
+            pltpu.VMEM((LANES, 2 * LANES), BF16),
+            pltpu.VMEM((LANES, interior * LANES), BF16),
+            pltpu.VMEM((8, LANES), F32),
+        ],
+        megabytes=8,
+        flops=1_000_000_000,
+    )
     grad_velocity, grad_affine, grad_volume, grad_drag = call(
         functools.partial(collect_kernel, counts, ends),
         "collect",
         (f32(3, blocks * LANES), f32(9, blocks * LANES), f32(blocks, LANES), f32(brick, size_z, brick)),
-        (meta, shape, hot_edge, hot, take, baffle_top, edge, grid, xe, xo, ye, yo, *xz, *layers),
+        (meta, shape, hot_edge, take, baffle_top, gathered, drag_slab, drag_rows, edge, xe, xo, ye, yo, *xz, *layers),
         scratch=[
-            pltpu.VMEM((SLABS + interior, ROWS + 16, LANES), F32),
-            pltpu.VMEM((LANES, SLABS * LANES), BF16),
-            pltpu.VMEM((LANES, interior * LANES), BF16),
+            pltpu.VMEM((2, ROWS + 16, LANES), F32),
+            pltpu.VMEM((LANES, 2 * LANES), BF16),
+            pltpu.VMEM((2, size_z, LANES), F32),
             pltpu.VMEM((9 * blocks, 2 * LANES), BF16),
             pltpu.VMEM((9 * blocks, 9 * LANES), F32),
             pltpu.VMEM((12 * blocks, LANES), F32),
         ],
-        megabytes=16,
+        megabytes=12,
     )
     return grad_velocity, grad_affine, grad_volume.reshape(-1), grad_drag.transpose(0, 2, 1)
 

time: 20.6 us -> 19.6 us (0.951)
  waiting for transfers between devices: 6.15 us -> 5.49 us
  Pallas kernels: 6.12 us -> 5.77 us
    ppermute x6, waiting for transfers between devices: 6.15 us -> 5.49 us  [exchange(): return lax.ppermute(array, names, links) if links else jnp.zeros_like(array)]
    pallas_call x6 -> x7, Pallas kernels: 6.12 us -> 5.77 us  [call(): pl.pallas_call(kernel, out_shape=out_shape, in_specs=[vmem] * len(operand...]
  transfers between devices with their start and end apart: 6 -> 6, of which waited for: 3 -> 3; matrix products, arithmetic and copies ran while one was open for 0% -> 0% of each run, Pallas kernels for 3% -> 6%
where the time goes in v3:
time: 19.6 us; the launch traced here: 19.4 us
  starting transfers between devices  6.69 us (34%)
  Pallas kernels  5.77 us (29%)
  waiting for transfers between devices  5.49 us (28%)
  between operations  1.46 us (7%)
    ppermute x6, starting transfers between devices, exchange(): return lax.ppermute(array, names, links) if links else jnp.zeros_like(array)  6.69 us
    pallas_call x7, Pallas kernels, call(): pl.pallas_call(kernel, out_shape=out_shape, in_specs=[vmem] * len(operand...  5.77 us
    ppermute x6, waiting for transfers between devices, exchange(): return lax.ppermute(array, names, links) if links else jnp.zeros_like(array)  5.49 us
  transfers between devices with their start and end apart: 6, of which 3 were waited for; matrix products, arithmetic and copies ran while one was open for 0% of the time, Pallas kernels for 6%

profile of v3, /device:TPU:0, one launch (start us, length us, event | category | flops | bytes accessed | tf_op | source)
XLA Modules:
  0.0 19.4 jit_solution(11819554969319564428)
XLA Ops:
  0.6 0.0 copy-start.3
  0.6 0.0 copy-start.2
  0.7 0.0 copy-start.8
  0.7 0.0 copy-start.1
  0.7 0.0 copy-start.6
  0.7 0.0 copy-start.7
  0.7 0.0 copy-start
  0.7 0.0 copy-start.5
  0.7 0.0 copy-start.4
  0.7 0.4 %spread.1 = (bf16[2688,256]{1,0:T(8,128)(2,1)S(1)}, bf16[256,1152]{1,0:T(8,128)(2,1)S(1)}) custom-call(), custom_call_target="tpu_custom_call" | custom-call | flops 20000000000 | bytes 1024 | tf_op jit(solution)/shard_map/spread/pallas_call | solution.py:467
  1.8 0.0 copy-done.3
  1.8 0.0 copy-done.2
  1.8 0.0 copy-done.8
  1.8 0.0 copy-done.1
  1.8 0.0 copy-done.6
  1.8 0.0 copy-done.7
  1.8 0.0 copy-done
  1.8 0.0 copy-done.5
  1.9 0.0 copy-done.4
  1.9 2.2 %deposit.1 = (f32[4,80,128]{2,1,0:T(8,128)S(1)}, f32[80,128]{1,0:T(8,128)S(1)}, f32[80,128]{1,0:T(8,128)S(1)}, f32[1,16,128]{2,1,0:T(8,128)S(1)}, s32[3,32,128]{...) custom-call(s32[1,32]{1,0:T(1,128)S(1)} %bitcast.10, ...), custom_call_target="tpu_custom_call" | custom-call | bytes 1024 | tf_op jit(solution)/shard_map/deposit/pallas_call | solution.py:467
  4.0 0.5 %collective-permute-start = (f32[80,128]{1,0:T(8,128)S(1)}, f32[80,128]{1,0:T(8,128)S(1)}, u32[]{:S(2)}, u32[]{:S(2)}) collective-permute-start(f32[80,128]{1,0:T(8,128)S(1)} %get-tuple-element.36), channel_id=1, source_target_pairs={{0,8},{1,9},{2,10},{3,11},{4,12},{5,13},{6,14},{7,15},{8,0},{9,1},... | collective-permute-start | bytes 122888 | tf_op jit(solution)/shard_map/ppermute | solution.py:448
  4.6 0.6 %interior.1 = (f32[8,80,128]{2,1,0:T(8,128)S(1)}, bf16[512,1024]{1,0:T(8,128)(2,1)S(1)}) custom-call(bf16[512,256]{1,0:T(8,128)(2,1)S(1)} %get-tuple-element.31.window_ref, s32[3,32,128]{2,1,0:T(8,128)S(1)} %get-tuple-element.27.meta_ref.refs_0_, f32[8,8,128]{2,1,0:T(8,128)S(1)} %get-tuple-element.32.planes_ref), custom_call_target="tpu_custom_call" | custom-call | flops 1000000000 | bytes 1024 | tf_op jit(solution)/shard_map/interior/pallas_call | solution.py:467
  5.2 0.3 %collective-permute-done.xe_ref.refs_4_.refs_1_.refs_9_ = f32[80,128]{1,0:T(8,128)S(1)} collective-permute-done((f32[80,128]{1,0:T(8,128)S(1)}, f32[80,128]{1,0:T(8,128)S(1)}, u32[]{:S(2)}, u32[]{:S(2)}) %collective-permute-start) | collective-permute-done | bytes 40992 | tf_op jit(solution)/shard_map/ppermute | solution.py:448
  5.4 0.1 pack_z.1
  5.5 2.9 %collective-permute-start.3 = (f32[12,16,128]{2,1,0:T(8,128)S(1)}, f32[12,16,128]{2,1,0:T(8,128)S(1)}, u32[]{:S(2)}, u32[]{:S(2)}) collective-permute-start(f32[12,16,128]{2,1,0:T(8,128)S(1)} %pack_z.1), channel_id=1, source_target_pairs={{0,1},{1,0},{2,3},{3,2},{4,5},{5,4},{6,7},{7,6},{8,9},{9,8},{10,11... | collective-permute-start | bytes 294920 | tf_op jit(solution)/shard_map/ppermute | solution.py:448
  8.5 1.0 %collective-permute-start.1 = (f32[80,128]{1,0:T(8,128)S(1)}, f32[80,128]{1,0:T(8,128)S(1)}, u32[]{:S(2)}, u32[]{:S(2)}) collective-permute-start(f32[80,128]{1,0:T(8,128)S(1)} %get-tuple-element.37), channel_id=1, source_target_pairs={{0,24},{1,25},{2,26},{3,27},{4,28},{5,29},{6,30},{7,31},{8,16},{9,... | collective-permute-start | bytes 122888 | tf_op jit(solution)/shard_map/ppermute | solution.py:448
  9.4 0.3 %collective-permute-start.2 = (f32[16,128]{1,0:T(8,128)S(1)}, f32[16,128]{1,0:T(8,128)S(1)}, u32[]{:S(2)}, u32[]{:S(2)}) collective-permute-start(f32[16,128]{1,0:T(8,128)S(1)} %bitcast.11), channel_id=1, source_target_pairs={{0,25},{1,24},{2,27},{3,26},{4,29},{5,28},{6,31},{7,30},{8,17},{9,... | collective-permute-start | bytes 24584 | tf_op jit(solution)/shard_map/ppermute | solution.py:448
  9.7 3.7 %collective-permute-done.2.refs_6_.refs_3_.refs_13_ = f32[16,128]{1,0:T(8,128)S(1)} collective-permute-done((f32[16,128]{1,0:T(8,128)S(1)}, f32[16,128]{1,0:T(8,128)S(1)}, u32[]{:S(2)}, u32[]{:S(2)}) %collective-permute-start.2) | collective-permute-done | bytes 8224 | tf_op jit(solution)/shard_map/ppermute | solution.py:448
  13.4 0.0 collective-permute-done.1.refs_5_.refs_2_.refs_10_
  13.4 0.0 collective-permute-done.3.refs_7_.refs_4_.refs_14_
  13.4 0.1 pack_y.1
  13.5 1.6 %collective-permute-start.4 = (f32[80,128]{1,0:T(8,128)S(1)}, f32[80,128]{1,0:T(8,128)S(1)}, u32[]{:S(2)}, u32[]{:S(2)}) collective-permute-start(f32[80,128]{1,0:T(8,128)S(1)} %get-tuple-element.42), channel_id=1, source_target_pairs={{0,2},{1,3},{2,0},{3,1},{4,6},{5,7},{6,4},{7,5},{8,10},{9,11},{10,... | collective-permute-start | bytes 122888 | tf_op jit(solution)/shard_map/ppermute | solution.py:448
  15.2 0.3 %collective-permute-start.5 = (f32[80,128]{1,0:T(8,128)S(1)}, f32[80,128]{1,0:T(8,128)S(1)}, u32[]{:S(2)}, u32[]{:S(2)}) collective-permute-start(f32[80,128]{1,0:T(8,128)S(1)} %get-tuple-element.43), channel_id=1, source_target_pairs={{0,8},{1,9},{2,4},{3,5},{4,2},{5,3},{6,14},{7,15},{8,0},{9,1},{10,... | collective-permute-start | bytes 122888 | tf_op jit(solution)/shard_map/ppermute | solution.py:448
  15.5 0.7 %early.1 = (f32[512,128]{1,0:T(8,128)S(1)}, f32[2,8,128]{2,1,0:T(8,128)S(1)}, f32[8,8,128]{2,1,0:T(8,128)S(1)}) custom-call(bf16[512,512]{1,0:T(8,128)(2,1)S(1)} %get-tuple-element.29.refs_0_.refs_2_, bf16[512,1024]{1,0:T(8,128)(2,1)S(1)} %get-tuple-element.33.refs_1_, f32[4,80,128]{2,1,0:T(8,128)S(1)} %get-tuple-element.34.slab_ref.refs_2_.refs_0_.refs_8_, ...), custom_call_target="tpu_custom_call" | custom-call | flops 1000000000 | bytes 1024 | tf_op jit(solution)/shard_map/early/pallas_call | solution.py:467
  16.2 1.5 %collective-permute-done.4.refs_11_ = f32[80,128]{1,0:T(8,128)S(1)} collective-permute-done((f32[80,128]{1,0:T(8,128)S(1)}, f32[80,128]{1,0:T(8,128)S(1)}, u32[]{:S(2)}, u32[]{:S(2)}) %collective-permute-start.4) | collective-permute-done | bytes 40992 | tf_op jit(solution)/shard_map/ppermute | solution.py:448
  17.7 0.0 collective-permute-done.5.refs_12_
  17.7 1.7 %collect.1 = (f32[3,4096]{1,0:T(4,128)}, f32[9,4096]{1,0:T(8,128)}, f32[32,128]{1,0:T(8,128)}, f32[32,8,32]{2,1,0:T(8,128)}) custom-call(s32[3,32,128]{2,1,0:T(8,128)S(1)} %get-tuple-element.27.meta_ref.refs_0_, f32[384,128]{1,0:T(8,128)S(1)} %get-tuple-element.28.refs_1_, bf16[512,512]{1,0:T(8,128)(2,1)S(1)} %get-tuple-element.29.refs_0_.refs_2_, ...), custom_call_target="tpu_custom_call" | custom-call | bytes 1024 | tf_op jit(solution)/shard_map/collect/pallas_call | solution.py:467
Async XLA Ops:
  0.6 1.1 %copy-start.3 = (s32[32,32]{1,0:T(8,128)S(1)}, s32[32,32]{1,0:T(8,128)}, u32[]{:S(2)}) copy-start(s32[32,32]{1,0:T(8,128)} %refs_4_.3) | copy-start | bytes 12292
  0.6 1.1 %copy-start.2 = (f32[32,32,8]{1,2,0:T(8,128)S(1)}, f32[32,32,8]{1,2,0:T(8,128)}, u32[]{:S(2)}) copy-start(f32[32,32,8]{1,2,0:T(8,128)} %param.19) | copy-start | bytes 98308
  0.7 1.1 %copy-start.8 = (s32[32]{0:T(128)S(1)}, s32[32]{0:T(128)}, u32[]{:S(2)}) copy-start(s32[32]{0:T(128)} %param.16) | copy-start | bytes 388
  0.7 1.1 %copy-start.1 = (f32[9,4096]{1,0:T(8,128)S(1)}, f32[9,4096]{1,0:T(8,128)}, u32[]{:S(2)}) copy-start(f32[9,4096]{1,0:T(8,128)} %refs_7_.1) | copy-start | bytes 442372
  0.7 1.1 %copy-start.6 = (f32[3,4096]{1,0:T(4,128)S(1)}, f32[3,4096]{1,0:T(4,128)}, u32[]{:S(2)}) copy-start(f32[3,4096]{1,0:T(4,128)} %refs_6_.1) | copy-start | bytes 147460
  0.7 1.1 %copy-start.7 = (f32[4096]{0:T(1024)S(1)}, f32[4096]{0:T(1024)}, u32[]{:S(2)}) copy-start(f32[4096]{0:T(1024)} %param.13) | copy-start | bytes 49156
  0.7 1.1 %copy-start = (f32[9,4096]{1,0:T(8,128)S(1)}, f32[9,4096]{1,0:T(8,128)}, u32[]{:S(2)}) copy-start(f32[9,4096]{1,0:T(8,128)} %refs_4_.2) | copy-start | bytes 442372
  0.7 1.1 %copy-start.5 = (f32[3,4096]{1,0:T(4,128)S(1)}, f32[3,4096]{1,0:T(4,128)}, u32[]{:S(2)}) copy-start(f32[3,4096]{1,0:T(4,128)} %refs_3_.1) | copy-start | bytes 147460
  0.7 1.1 %copy-start.4 = (f32[3,4096]{1,0:T(4,128)S(1)}, f32[3,4096]{1,0:T(4,128)}, u32[]{:S(2)}) copy-start(f32[3,4096]{1,0:T(4,128)} %refs_2_.1) | copy-start | bytes 147460
  4.0 1.4 %collective-permute-start = (f32[80,128]{1,0:T(8,128)S(1)}, f32[80,128]{1,0:T(8,128)S(1)}, u32[]{:S(2)}, u32[]{:S(2)}) collective-permute-start(f32[80,128]{1,0:T(8,128)S(1)} %get-tuple-element.36), channel_id=1, source_target_pairs={{0,8},{1,9},{2,10},{3,11},{4,12},{5,13},{6,14},{7,15},{8,0},{9,1},... | collective-permute-start | bytes 122888 | tf_op jit(solution)/shard_map/ppermute | solution.py:448
  5.5 7.9 %collective-permute-start.3 = (f32[12,16,128]{2,1,0:T(8,128)S(1)}, f32[12,16,128]{2,1,0:T(8,128)S(1)}, u32[]{:S(2)}, u32[]{:S(2)}) collective-permute-start(f32[12,16,128]{2,1,0:T(8,128)S(1)} %pack_z.1), channel_id=1, source_target_pairs={{0,1},{1,0},{2,3},{3,2},{4,5},{5,4},{6,7},{7,6},{8,9},{9,8},{10,11... | collective-permute-start | bytes 294920 | tf_op jit(solution)/shard_map/ppermute | solution.py:448
  8.5 5.0 %collective-permute-start.1 = (f32[80,128]{1,0:T(8,128)S(1)}, f32[80,128]{1,0:T(8,128)S(1)}, u32[]{:S(2)}, u32[]{:S(2)}) collective-permute-start(f32[80,128]{1,0:T(8,128)S(1)} %get-tuple-element.37), channel_id=1, source_target_pairs={{0,24},{1,25},{2,26},{3,27},{4,28},{5,29},{6,30},{7,31},{8,16},{9,... | collective-permute-start | bytes 122888 | tf_op jit(solution)/shard_map/ppermute | solution.py:448
  9.4 4.0 %collective-permute-start.2 = (f32[16,128]{1,0:T(8,128)S(1)}, f32[16,128]{1,0:T(8,128)S(1)}, u32[]{:S(2)}, u32[]{:S(2)}) collective-permute-start(f32[16,128]{1,0:T(8,128)S(1)} %bitcast.11), channel_id=1, source_target_pairs={{0,25},{1,24},{2,27},{3,26},{4,29},{5,28},{6,31},{7,30},{8,17},{9,... | collective-permute-start | bytes 24584 | tf_op jit(solution)/shard_map/ppermute | solution.py:448
  13.5 4.2 %collective-permute-start.4 = (f32[80,128]{1,0:T(8,128)S(1)}, f32[80,128]{1,0:T(8,128)S(1)}, u32[]{:S(2)}, u32[]{:S(2)}) collective-permute-start(f32[80,128]{1,0:T(8,128)S(1)} %get-tuple-element.42), channel_id=1, source_target_pairs={{0,2},{1,3},{2,0},{3,1},{4,6},{5,7},{6,4},{7,5},{8,10},{9,11},{10,... | collective-permute-start | bytes 122888 | tf_op jit(solution)/shard_map/ppermute | solution.py:448
  15.2 2.5 %collective-permute-start.5 = (f32[80,128]{1,0:T(8,128)S(1)}, f32[80,128]{1,0:T(8,128)S(1)}, u32[]{:S(2)}, u32[]{:S(2)}) collective-permute-start(f32[80,128]{1,0:T(8,128)S(1)} %get-tuple-element.43), channel_id=1, source_target_pairs={{0,8},{1,9},{2,4},{3,5},{4,2},{5,3},{6,14},{7,15},{8,0},{9,1},{10,... | collective-permute-start | bytes 122888 | tf_op jit(solution)/shard_map/ppermute | solution.py:448

commit v4 on v3

--- a/solution.py
+++ b/solution.py
@@ -28,11 +28,15 @@
     if tile < 2:
         x, y = lane >> 1, (lane & 1) + tile * brick
         valid = lane < 2 * (brick + 2)
+    elif tile < SLABS:
+        plane, corner = lane < 64, lane - 64
+        x = jnp.where(plane, lane >> 5, (corner & 3) >> 1) + (tile - 2) * brick
+        y = jnp.where(plane, (lane & 31) + 1, (corner >> 2) * brick + (corner & 1))
+        valid = jnp.where(plane, ((y >= 2) & (y < brick)).astype(jnp.int32), (corner < 8).astype(jnp.int32)) == 1
     else:
-        x = (lane >> 5) + ((0, brick)[tile - 2] if tile < SLABS else 4 * (tile - SLABS) + 1)
+        x = (lane >> 5) + 4 * (tile - SLABS) + 1
         y = (lane & 31) + 1
-        valid = (y >= 2) & (y < brick)
-        valid = valid & ((lane < 64) if tile < SLABS else ((x >= 2) & (x < brick)))
+        valid = (x >= 2) & (x < brick) & (y >= 2) & (y < brick)
     return x, y, valid
 
 
@@ -49,10 +53,10 @@
     return (cells >> 5) * 128 + ((cells >> 1) & 15) * 2, cells & 1
 
 
-def fill_one_hot(hot_ref, code, first_tile, brick):
+def fill_one_hot(hot_ref, code, tiles, brick):
     blocks = code.shape[0]
-    for at in range(hot_ref.shape[1] // LANES):
-        lane_code = tile_code(first_tile + at, blocks, brick) - code
+    for at, tile in enumerate(tiles):
+        lane_code = tile_code(tile, blocks, brick) - code
         for node in range(16):
             hit = lane_code == (node // 4) * 64 + node % 4
             hot_ref[pl.ds(node * blocks, blocks), pl.ds(at * LANES, LANES)] = jnp.where(hit, 1.0, 0.0).astype(BF16)
@@ -74,6 +78,10 @@
             grid_ref[tile, pl.ds(8 * z, 8), :] = piece[:, tile * LANES : (tile + 1) * LANES]
 
 
+def inner_tiles(brick):
+    return (0, 1) + tuple(range(SLABS, SLABS + brick // 4))
+
+
 def spline(frac):
     return [0.5 * (0.5 - frac) ** 2, 0.75 - frac * frac, 0.5 * (0.5 + frac) ** 2]
 
@@ -102,6 +110,12 @@
 
 def to_rows(flat_ref, first, array_ref, blocks):
     channels = array_ref.shape[0]
+    if channels > 8:
+        tiles = jnp.stack([array_ref[pl.ds(0, 8), pl.ds(b * LANES, LANES)] for b in range(blocks)])
+        flat_ref[pl.ds(first * blocks, 8 * blocks), :] = jnp.swapaxes(tiles, 0, 1).reshape(8 * blocks, LANES)
+        for b in range(blocks):
+            flat_ref[pl.ds((first + 8) * blocks + b, 1), :] = array_ref[pl.ds(8, 1), pl.ds(b * LANES, LANES)]
+        return
     for b in range(blocks):
         flat_ref[pl.ds(first * blocks + b, channels, stride=blocks), :] = array_ref[:, pl.ds(b * LANES, LANES)]
 
@@ -140,15 +154,15 @@
 def deposit_kernel(*refs):
     cells_ref, count_ref, pos_ref, vel_ref, aff_ref, vol_ref, cvel_ref, caff_ref, top_ref, drag_ref = refs[:10]
     spread_ref, refs = refs[10], refs[11:]
-    grid_ref, even_ref, odd_ref, diagonal_ref, meta_ref, shape_ref, window_ref, hot_ref, planes_ref = refs[:9]
-    flat_ref, terms_ref, sums_ref, all_ref = refs[9:]
+    grid_ref, even_ref, odd_ref, diagonal_ref, meta_ref, shape_ref, window_ref, hot_ref = refs[:8]
+    flat_ref, terms_ref, sums_ref, all_ref = refs[8:]
     blocks = vol_ref.shape[0]
     brick = drag_ref.shape[0]
     size_z = drag_ref.shape[1]
     code, upper_tile = block_columns(cells_ref)
     live_rows = iota((blocks, LANES), 0) < count_ref[...]
     meta_ref[0], meta_ref[1], meta_ref[2] = code, upper_tile, live_rows.astype(jnp.int32)
-    fill_one_hot(hot_ref, code, 0, brick)
+    fill_one_hot(hot_ref, code, (2, 3), brick)
     for first, ref in ((0, pos_ref), (3, vel_ref), (6, aff_ref), (15, cvel_ref), (18, caff_ref)):
         to_rows(flat_ref, first, ref, blocks)
 
@@ -226,28 +240,15 @@
 
     depth = iota((size_z, brick), 0) + lax.axis_index("gz") * size_z
     lane = iota((size_z, LANES), 1)
-    zero = jnp.zeros((size_z, LANES), F32)
-    ends = [zero, zero]
-    layers = []
-    for x in range(brick):
+    blank = jnp.zeros((size_z, 32), F32)
+    for side, x in enumerate((0, brick - 1)):
         layer = jnp.where(depth < top_ref[pl.ds(x, 1), :], drag_ref[x], 0.0)
-        layers.append(layer)
-        ends[0] = jnp.where(lane == 2 * (x + 1) + 1, layer[:, 0:1], ends[0])
-        ends[1] = jnp.where(lane == 2 * (x + 1), layer[:, brick - 1 : brick], ends[1])
-    blank = jnp.zeros((size_z, 32), F32)
-    planes = ends + [
-        jnp.concatenate([blank, layers[0], blank, blank], axis=1),
-        jnp.concatenate([layers[-1], blank, blank, blank], axis=1),
-    ]
-    for t in range(brick // 4):
-        planes_ref[t] = jnp.concatenate(layers[4 * t : 4 * t + 4], axis=1)
-    for tile, plane in enumerate(planes):
-        grid_ref[tile, pl.ds(8 + 7, size_z, stride=8), :] = plane
-
-    lane = iota((ROWS, LANES), 1)
-    slab = [grid_ref[t] for t in range(SLABS)]
-    low = jnp.where(lane < 64, slab[2], jnp.where(lane < 68, pltpu.roll(slab[0], 64, 1), pltpu.roll(slab[1], 68, 1)))
-    high = jnp.where(lane < 64, slab[3], jnp.where(lane < 68, slab[0], pltpu.roll(slab[1], 4, 1)))
+        plane = jnp.concatenate([blank, layer, blank, blank] if side == 0 else [layer, blank, blank, blank], axis=1)
+        plane = jnp.where(lane == 67 - 2 * side, layer[:, 0:1], plane)
+        plane = jnp.where(lane == 70 - 2 * side, layer[:, brick - 1 : brick], plane)
+        grid_ref[side, pl.ds(8 + 7, size_z, stride=8), :] = plane
+
+    low, high = grid_ref[0], grid_ref[1]
     here = is_even("gx")
     even_ref[...] = jnp.where(here, high, low)
     odd_ref[...] = jnp.where(here, low, high)
@@ -258,11 +259,26 @@
         diagonal_ref[1] = jnp.where(here, lower, upper)
 
 
-def interior_kernel(brick, window_ref, meta_ref, planes_ref, grid_ref, hot_ref, all_ref):
-    fill_one_hot(hot_ref, meta_ref[0], SLABS, brick)
+def interior_kernel(window_ref, meta_ref, top_ref, drag_ref, grid_ref, hot_ref, all_ref):
+    brick, size_z, _ = drag_ref.shape
+    fill_one_hot(hot_ref, meta_ref[0], inner_tiles(brick), brick)
     deposit_windows(grid_ref, window_ref, hot_ref, all_ref)
-    for tile in range(grid_ref.shape[0]):
-        grid_ref[tile, pl.ds(8 + 7, planes_ref.shape[1], stride=8), :] = planes_ref[tile]
+    depth = iota((size_z, brick), 0) + lax.axis_index("gz") * size_z
+    lane = iota((size_z, LANES), 1)
+    ends = [jnp.zeros((size_z, LANES), F32)] * 2
+    layers = []
+    for x in range(brick):
+        layer = jnp.where(depth < top_ref[pl.ds(x, 1), :], drag_ref[x], 0.0)
+        layers.append(layer)
+        ends[0] = jnp.where(lane == 2 * (x + 1) + 1, layer[:, 0:1], ends[0])
+        ends[1] = jnp.where(lane == 2 * (x + 1), layer[:, brick - 1 : brick], ends[1])
+    planes = ends + [jnp.concatenate(layers[4 * t : 4 * t + 4], axis=1) for t in range(brick // 4)]
+    for at, plane in enumerate(planes):
+        grid_ref[at, pl.ds(8 + 7, size_z, stride=8), :] = plane
+
+
+def own_tile(slab_ref, grid_ref, tile):
+    return grid_ref[tile] if tile < 2 else slab_ref[tile - 2] if tile < SLABS else grid_ref[tile - 2]
 
 
 def pack_z_kernel(slab_ref, grid_ref, xe_ref, even_ref, *odd_refs):
@@ -272,8 +288,8 @@
         rows = pl.ds(first, 16)
         received = xe_ref[rows, :]
         extra = x_additions(*low_high(received, jnp.zeros_like(received), "gx"))
-        ends.append([slab_ref[t, rows, :] + extra[t] for t in range(SLABS)])
-        ends[-1] += [grid_ref[t, rows, :] for t in range(grid_ref.shape[0])]
+        ends.append([own_tile(slab_ref, grid_ref, t)[first : first + 16] + extra[t] for t in range(SLABS)])
+        ends[-1] += [grid_ref[t, rows, :] for t in range(2, grid_ref.shape[0])]
     for tile, (lower, upper) in enumerate(zip(*ends)):
         even_ref[tile] = jnp.where(here, upper, lower)
         for odd_ref in odd_refs:
@@ -293,10 +309,10 @@
 
 
 def pack_y_kernel(ends, *refs):
-    slab_ref, xe_ref, xo_ref, *received = refs[:-2]
+    grid_ref, xe_ref, xo_ref, *received = refs[:-2]
     even_ref, odd_ref = refs[-2:]
     extra = xz_additions(xe_ref, xo_ref, received[:ends], received[ends:], 2)
-    lower, upper = slab_ref[0] + extra[0], slab_ref[1] + extra[1]
+    lower, upper = grid_ref[0] + extra[0], grid_ref[1] + extra[1]
     here = is_even("gy")
     even_ref[...] = jnp.where(here, upper, lower)
     odd_ref[...] = jnp.where(here, lower, upper)
@@ -318,6 +334,8 @@
             c = [total_ref[at, pl.ds(32 * side + k, 8, stride=8), :] for k in range(CHANNELS)]
             node_z = row + (4 * side - 1) + place[2] * size_z
             inside = (node_z >= 0) & (node_z < counts[2] * size_z)
+            if tile in (2, 3):
+                inside = inside & (iota((8, LANES), 1) < 64)
             if tile < SLABS:
                 inside = inside & (node_x >= 0) & (node_x < counts[0] * brick)
                 inside = inside & (node_y >= 0) & (node_y < counts[1] * brick)
@@ -340,20 +358,22 @@
     inputs, refs = refs[:-7], refs[-7:]
     hot_slab_ref, hot_ref, slab_ref, grid_ref, xe_ref, xo_ref, *received = inputs
     gathered_ref, drag_slab_ref, drag_ref, total_ref, push_slab_ref, push_ref, _ = refs
-    brick = 4 * grid_ref.shape[0]
+    brick = 4 * (grid_ref.shape[0] - 2)
     extra = xz_additions(xe_ref, xo_ref, received[:ends], received[ends:], SLABS)
-    totals = [slab_ref[tile] + extra[tile] for tile in (2, 3)]
+    totals = [slab_ref[tile - 2] + extra[tile] for tile in (2, 3)]
     node_gradients(counts, brick, size_z, (2, 3), totals, total_ref, push_slab_ref, drag_slab_ref)
-    tiles = range(SLABS, SLABS + grid_ref.shape[0])
-    totals = [grid_ref[t - SLABS] + diagonal_rows([ref[t] for ref in received[ends:]]) for t in tiles]
+    tiles = inner_tiles(brick)[2:]
+    totals = [grid_ref[t - 2] + diagonal_rows([ref[t] for ref in received[ends:]]) for t in tiles]
     node_gradients(counts, brick, size_z, tiles, totals, total_ref, push_ref, drag_ref)
-    gathered_ref[...] = gather(hot_slab_ref[:, pl.ds(2 * LANES, 2 * LANES)], push_slab_ref) + gather(hot_ref[...], push_ref)
+    gathered_ref[...] = gather(hot_slab_ref[...], push_slab_ref) + gather(
+        hot_ref[:, pl.ds(2 * LANES, push_ref.shape[1])], push_ref
+    )
 
 
 def collect_kernel(counts, ends, *refs):
     inputs, refs = refs[:-10], refs[-10:]
-    meta_ref, shape_ref, hot_slab_ref, take_spread_ref, top_ref, gathered_ref, drag_slab_ref, drag_ref = inputs[:8]
-    slab_ref, xe_ref, xo_ref, ye_ref, yo_ref, *received = inputs[8:]
+    meta_ref, shape_ref, hot_ref, take_spread_ref, top_ref, gathered_ref, drag_slab_ref, drag_ref = inputs[:8]
+    grid_ref, xe_ref, xo_ref, ye_ref, yo_ref, *received = inputs[8:]
     gvel_ref, gaff_ref, gvol_ref, gdrag_ref = refs[:4]
     total_ref, push_ref, drag_ends_ref, take_ref, pulled_ref, flat_ref = refs[4:]
     blocks = gvol_ref.shape[0]
@@ -363,9 +383,9 @@
 
     extra = xz_additions(xe_ref, xo_ref, received[:ends], received[ends:], 2)
     low, high = low_high(ye_ref[...], yo_ref[...], "gy")
-    totals = [slab_ref[0] + extra[0] + low, slab_ref[1] + extra[1] + high]
+    totals = [grid_ref[0] + extra[0] + low, grid_ref[1] + extra[1] + high]
     node_gradients(counts, brick, size_z, (0, 1), totals, total_ref, push_ref, drag_ends_ref)
-    gathered = gathered_ref[...] + gather(hot_slab_ref[:, pl.ds(0, 2 * LANES)], push_ref)
+    gathered = gathered_ref[...] + gather(hot_ref[:, pl.ds(0, 2 * LANES)], push_ref)
 
     edges = [drag_ends_ref[t] for t in range(2)]
     depth = iota((size_z, brick), 0) + lax.axis_index("gz") * size_z
@@ -484,20 +504,20 @@
     spread, take = call(
         spread_kernel, "spread", (bf16(21 * LANES, 2 * LANES), bf16(2 * LANES, 9 * LANES)), (), flops=20_000_000_000
     )
-    edge, send_xe, send_xo, send_xz, meta, shape, window, hot_edge, planes = call(
+    edge, send_xe, send_xo, send_xz, meta, shape, window, hot_edge = call(
         deposit_kernel,
         "deposit",
         (
-            f32(SLABS, ROWS, LANES), slab, slab, f32(ends, 16, LANES),
+            f32(2, ROWS, LANES), slab, slab, f32(ends, 16, LANES),
             jax.ShapeDtypeStruct((3, blocks, LANES), jnp.int32), f32(12 * blocks, LANES),
-            bf16(16 * blocks, 2 * LANES), bf16(16 * blocks, SLABS * LANES), f32(interior, size_z, LANES),
+            bf16(16 * blocks, 2 * LANES), bf16(16 * blocks, 2 * LANES),
         ),
         operands + (spread,),
         scratch=[
             pltpu.VMEM((27 * blocks, LANES), F32),
             pltpu.VMEM((18 * blocks, 21 * LANES), BF16),
             pltpu.VMEM((18 * blocks, 2 * LANES), F32),
-            pltpu.VMEM((2 * LANES, SLABS * LANES), F32),
+            pltpu.VMEM((2 * LANES, 2 * LANES), F32),
         ],
         megabytes=16,
     )
@@ -520,11 +540,11 @@
         for first in range(ends)
     ]
     grid, hot = call(
-        functools.partial(interior_kernel, brick),
+        interior_kernel,
         "interior",
-        (f32(interior, ROWS, LANES), bf16(16 * blocks, interior * LANES)),
-        (window, meta, planes),
-        scratch=[pltpu.VMEM((2 * LANES, interior * LANES), F32)],
+        (f32(2 + interior, ROWS, LANES), bf16(16 * blocks, (2 + interior) * LANES)),
+        (window, meta, *operands[-2:]),
+        scratch=[pltpu.VMEM((2 * LANES, (2 + interior) * LANES), F32)],
         megabytes=8,
         flops=1_000_000_000,
     )
@@ -534,7 +554,7 @@
         for first, array in enumerate(send_z)
     ]
     send_ye, send_yo = call(
-        functools.partial(pack_y_kernel, ends), "pack_y", (slab, slab), (edge, xe, xo, *xz, *layers)
+        functools.partial(pack_y_kernel, ends), "pack_y", (slab, slab), (grid, xe, xo, *xz, *layers)
     )
     yo = exchange(send_yo, counts, odd_y)
     ye = exchange(send_ye, counts, lambda x, y, z: (x, paired(y, counts[1], 0), z))
@@ -556,7 +576,7 @@
         functools.partial(collect_kernel, counts, ends),
         "collect",
         (f32(3, blocks * LANES), f32(9, blocks * LANES), f32(blocks, LANES), f32(brick, size_z, brick)),
-        (meta, shape, hot_edge, take, baffle_top, gathered, drag_slab, drag_rows, edge, xe, xo, ye, yo, *xz, *layers),
+        (meta, shape, hot, take, baffle_top, gathered, drag_slab, drag_rows, grid, xe, xo, ye, yo, *xz, *layers),
         scratch=[
             pltpu.VMEM((2, ROWS + 16, LANES), F32),
             pltpu.VMEM((LANES, 2 * LANES), BF16),

time: 19.6 us -> 19.2 us (0.980)
  Pallas kernels: 5.77 us -> 5.41 us
    pallas_call x7, Pallas kernels: 5.77 us -> 5.41 us  [call(): pl.pallas_call(kernel, out_shape=out_shape, in_specs=[vmem] * len(operand...]
  transfers between devices with their start and end apart: 6 -> 6, of which waited for: 3 -> 3; matrix products, arithmetic and copies ran while one was open for 0% -> 0% of each run, Pallas kernels for 6% -> 7%
where the time goes in v4:
time: 19.2 us; the launch traced here: 19 us
  starting transfers between devices  6.69 us (35%)
  waiting for transfers between devices  5.44 us (28%)
  Pallas kernels  5.41 us (28%)
  between operations  1.46 us (8%)
    ppermute x6, starting transfers between devices, exchange(): return lax.ppermute(array, names, links) if links else jnp.zeros_like(array)  6.69 us
    ppermute x6, waiting for transfers between devices, exchange(): return lax.ppermute(array, names, links) if links else jnp.zeros_like(array)  5.44 us
    pallas_call x7, Pallas kernels, call(): pl.pallas_call(kernel, out_shape=out_shape, in_specs=[vmem] * len(operand...  5.41 us
  transfers between devices with their start and end apart: 6, of which 3 were waited for; matrix products, arithmetic and copies ran while one was open for 0% of the time, Pallas kernels for 7%

profile of v4, /device:TPU:0, one launch (start us, length us, event | category | flops | bytes accessed | tf_op | source)
XLA Modules:
  0.0 19.0 jit_solution(190901985313991839)
XLA Ops:
  0.6 0.0 copy-start.3
  0.6 0.0 copy-start.2
  0.7 0.0 copy-start.8
  0.7 0.0 copy-start.1
  0.7 0.0 copy-start.6
  0.7 0.0 copy-start.7
  0.7 0.0 copy-start
  0.7 0.0 copy-start.5
  0.7 0.0 copy-start.4
  0.7 0.4 %spread.1 = (bf16[2688,256]{1,0:T(8,128)(2,1)S(1)}, bf16[256,1152]{1,0:T(8,128)(2,1)S(1)}) custom-call(), custom_call_target="tpu_custom_call" | custom-call | flops 20000000000 | bytes 1024 | tf_op jit(solution)/shard_map/spread/pallas_call | solution.py:487
  1.8 0.0 copy-done.3
  1.8 0.0 copy-done.2
  1.8 0.0 copy-done.8
  1.8 0.0 copy-done.1
  1.8 0.0 copy-done.6
  1.8 0.0 copy-done.7
  1.8 0.0 copy-done
  1.8 0.0 copy-done.5
  1.9 0.0 copy-done.4
  1.9 1.8 %deposit.1 = (f32[2,80,128]{2,1,0:T(8,128)S(1)}, f32[80,128]{1,0:T(8,128)S(1)}, f32[80,128]{1,0:T(8,128)S(1)}, f32[1,16,128]{2,1,0:T(8,128)S(1)}, s32[3,32,128]{...) custom-call(s32[1,32]{1,0:T(1,128)S(1)} %bitcast.11, ...), custom_call_target="tpu_custom_call" | custom-call | bytes 1024 | tf_op jit(solution)/shard_map/deposit/pallas_call | solution.py:487
  3.7 0.5 %collective-permute-start = (f32[80,128]{1,0:T(8,128)S(1)}, f32[80,128]{1,0:T(8,128)S(1)}, u32[]{:S(2)}, u32[]{:S(2)}) collective-permute-start(f32[80,128]{1,0:T(8,128)S(1)} %get-tuple-element.34), channel_id=1, source_target_pairs={{0,8},{1,9},{2,10},{3,11},{4,12},{5,13},{6,14},{7,15},{8,0},{9,1},... | collective-permute-start | bytes 122888 | tf_op jit(solution)/shard_map/ppermute | solution.py:468
  4.2 0.6 %interior.1 = (f32[10,80,128]{2,1,0:T(8,128)S(1)}, bf16[512,1280]{1,0:T(8,128)(2,1)S(1)}) custom-call(bf16[512,256]{1,0:T(8,128)(2,1)S(1)} %get-tuple-element.28.window_ref, s32[3,32,128]{2,1,0:T(8,128)S(1)} %get-tuple-element.26.meta_ref.refs_0_, s32[32,32]{1,0:T(8,128)S(1)} %copy-done.3, f32[32,8,32]{2,1,0:T(8,128)S(1)} %bitcast.9), custom_call_target="tpu_custom_call" | custom-call | flops 1000000000 | bytes 1024 | tf_op jit(solution)/shard_map/interior/pallas_call | solution.py:487
  4.8 0.2 %collective-permute-done.xe_ref.refs_4_.refs_1_.refs_9_ = f32[80,128]{1,0:T(8,128)S(1)} collective-permute-done((f32[80,128]{1,0:T(8,128)S(1)}, f32[80,128]{1,0:T(8,128)S(1)}, u32[]{:S(2)}, u32[]{:S(2)}) %collective-permute-start) | collective-permute-done | bytes 40992 | tf_op jit(solution)/shard_map/ppermute | solution.py:468
  5.0 0.1 pack_z.1
  5.1 2.9 %collective-permute-start.3 = (f32[12,16,128]{2,1,0:T(8,128)S(1)}, f32[12,16,128]{2,1,0:T(8,128)S(1)}, u32[]{:S(2)}, u32[]{:S(2)}) collective-permute-start(f32[12,16,128]{2,1,0:T(8,128)S(1)} %pack_z.1), channel_id=1, source_target_pairs={{0,1},{1,0},{2,3},{3,2},{4,5},{5,4},{6,7},{7,6},{8,9},{9,8},{10,11... | collective-permute-start | bytes 294920 | tf_op jit(solution)/shard_map/ppermute | solution.py:468
  8.1 1.0 %collective-permute-start.1 = (f32[80,128]{1,0:T(8,128)S(1)}, f32[80,128]{1,0:T(8,128)S(1)}, u32[]{:S(2)}, u32[]{:S(2)}) collective-permute-start(f32[80,128]{1,0:T(8,128)S(1)} %get-tuple-element.35), channel_id=1, source_target_pairs={{0,24},{1,25},{2,26},{3,27},{4,28},{5,29},{6,30},{7,31},{8,16},{9,... | collective-permute-start | bytes 122888 | tf_op jit(solution)/shard_map/ppermute | solution.py:468
  9.0 0.3 %collective-permute-start.2 = (f32[16,128]{1,0:T(8,128)S(1)}, f32[16,128]{1,0:T(8,128)S(1)}, u32[]{:S(2)}, u32[]{:S(2)}) collective-permute-start(f32[16,128]{1,0:T(8,128)S(1)} %bitcast.12), channel_id=1, source_target_pairs={{0,25},{1,24},{2,27},{3,26},{4,29},{5,28},{6,31},{7,30},{8,17},{9,... | collective-permute-start | bytes 24584 | tf_op jit(solution)/shard_map/ppermute | solution.py:468
  9.3 3.7 %collective-permute-done.2.refs_6_.refs_3_.refs_13_ = f32[16,128]{1,0:T(8,128)S(1)} collective-permute-done((f32[16,128]{1,0:T(8,128)S(1)}, f32[16,128]{1,0:T(8,128)S(1)}, u32[]{:S(2)}, u32[]{:S(2)}) %collective-permute-start.2) | collective-permute-done | bytes 8224 | tf_op jit(solution)/shard_map/ppermute | solution.py:468
  13.0 0.0 collective-permute-done.1.refs_5_.refs_2_.refs_10_
  13.0 0.0 collective-permute-done.3.refs_7_.refs_4_.refs_14_
  13.0 0.1 pack_y.1
  13.1 1.6 %collective-permute-start.4 = (f32[80,128]{1,0:T(8,128)S(1)}, f32[80,128]{1,0:T(8,128)S(1)}, u32[]{:S(2)}, u32[]{:S(2)}) collective-permute-start(f32[80,128]{1,0:T(8,128)S(1)} %get-tuple-element.40), channel_id=1, source_target_pairs={{0,2},{1,3},{2,0},{3,1},{4,6},{5,7},{6,4},{7,5},{8,10},{9,11},{10,... | collective-permute-start | bytes 122888 | tf_op jit(solution)/shard_map/ppermute | solution.py:468
  14.8 0.3 %collective-permute-start.5 = (f32[80,128]{1,0:T(8,128)S(1)}, f32[80,128]{1,0:T(8,128)S(1)}, u32[]{:S(2)}, u32[]{:S(2)}) collective-permute-start(f32[80,128]{1,0:T(8,128)S(1)} %get-tuple-element.41), channel_id=1, source_target_pairs={{0,8},{1,9},{2,4},{3,5},{4,2},{5,3},{6,14},{7,15},{8,0},{9,1},{10,... | collective-permute-start | bytes 122888 | tf_op jit(solution)/shard_map/ppermute | solution.py:468
  15.1 0.7 %early.1 = (f32[512,128]{1,0:T(8,128)S(1)}, f32[2,8,128]{2,1,0:T(8,128)S(1)}, f32[8,8,128]{2,1,0:T(8,128)S(1)}) custom-call(bf16[512,256]{1,0:T(8,128)(2,1)S(1)} %get-tuple-element.31.refs_0_, bf16[512,1280]{1,0:T(8,128)(2,1)S(1)} %get-tuple-element.29.refs_1_.refs_2_, f32[2,80,128]{2,1,0:T(8,128)S(1)} %get-tuple-element.32.slab_ref.refs_2_, ...), custom_call_target="tpu_custom_call" | custom-call | flops 1000000000 | bytes 1024 | tf_op jit(solution)/shard_map/early/pallas_call | solution.py:487
  15.8 1.5 %collective-permute-done.4.refs_11_ = f32[80,128]{1,0:T(8,128)S(1)} collective-permute-done((f32[80,128]{1,0:T(8,128)S(1)}, f32[80,128]{1,0:T(8,128)S(1)}, u32[]{:S(2)}, u32[]{:S(2)}) %collective-permute-start.4) | collective-permute-done | bytes 40992 | tf_op jit(solution)/shard_map/ppermute | solution.py:468
  17.3 0.0 collective-permute-done.5.refs_12_
  17.3 1.7 %collect.1 = (f32[3,4096]{1,0:T(4,128)}, f32[9,4096]{1,0:T(8,128)}, f32[32,128]{1,0:T(8,128)}, f32[32,8,32]{2,1,0:T(8,128)}) custom-call(s32[3,32,128]{2,1,0:T(8,128)S(1)} %get-tuple-element.26.meta_ref.refs_0_, f32[384,128]{1,0:T(8,128)S(1)} %get-tuple-element.27.refs_1_, bf16[512,1280]{1,0:T(8,128)(2,1)S(1)} %get-tuple-element.29.refs_1_.refs_2_, ...), custom_call_target="tpu_custom_call" | custom-call | bytes 1024 | tf_op jit(solution)/shard_map/collect/pallas_call | solution.py:487
Async XLA Ops:
  0.6 1.1 %copy-start.3 = (s32[32,32]{1,0:T(8,128)S(1)}, s32[32,32]{1,0:T(8,128)}, u32[]{:S(2)}) copy-start(s32[32,32]{1,0:T(8,128)} %refs_4_.3) | copy-start | bytes 12292
  0.6 1.1 %copy-start.2 = (f32[32,32,8]{1,2,0:T(8,128)S(1)}, f32[32,32,8]{1,2,0:T(8,128)}, u32[]{:S(2)}) copy-start(f32[32,32,8]{1,2,0:T(8,128)} %param.19) | copy-start | bytes 98308
  0.7 1.1 %copy-start.8 = (s32[32]{0:T(128)S(1)}, s32[32]{0:T(128)}, u32[]{:S(2)}) copy-start(s32[32]{0:T(128)} %param.16) | copy-start | bytes 388
  0.7 1.1 %copy-start.1 = (f32[9,4096]{1,0:T(8,128)S(1)}, f32[9,4096]{1,0:T(8,128)}, u32[]{:S(2)}) copy-start(f32[9,4096]{1,0:T(8,128)} %refs_7_.1) | copy-start | bytes 442372
  0.7 1.1 %copy-start.6 = (f32[3,4096]{1,0:T(4,128)S(1)}, f32[3,4096]{1,0:T(4,128)}, u32[]{:S(2)}) copy-start(f32[3,4096]{1,0:T(4,128)} %refs_6_.1) | copy-start | bytes 147460
  0.7 1.1 %copy-start.7 = (f32[4096]{0:T(1024)S(1)}, f32[4096]{0:T(1024)}, u32[]{:S(2)}) copy-start(f32[4096]{0:T(1024)} %param.13) | copy-start | bytes 49156
  0.7 1.1 %copy-start = (f32[9,4096]{1,0:T(8,128)S(1)}, f32[9,4096]{1,0:T(8,128)}, u32[]{:S(2)}) copy-start(f32[9,4096]{1,0:T(8,128)} %refs_4_.2) | copy-start | bytes 442372
  0.7 1.1 %copy-start.5 = (f32[3,4096]{1,0:T(4,128)S(1)}, f32[3,4096]{1,0:T(4,128)}, u32[]{:S(2)}) copy-start(f32[3,4096]{1,0:T(4,128)} %refs_3_.1) | copy-start | bytes 147460
  0.7 1.1 %copy-start.4 = (f32[3,4096]{1,0:T(4,128)S(1)}, f32[3,4096]{1,0:T(4,128)}, u32[]{:S(2)}) copy-start(f32[3,4096]{1,0:T(4,128)} %refs_2_.1) | copy-start | bytes 147460
  3.7 1.4 %collective-permute-start = (f32[80,128]{1,0:T(8,128)S(1)}, f32[80,128]{1,0:T(8,128)S(1)}, u32[]{:S(2)}, u32[]{:S(2)}) collective-permute-start(f32[80,128]{1,0:T(8,128)S(1)} %get-tuple-element.34), channel_id=1, source_target_pairs={{0,8},{1,9},{2,10},{3,11},{4,12},{5,13},{6,14},{7,15},{8,0},{9,1},... | collective-permute-start | bytes 122888 | tf_op jit(solution)/shard_map/ppermute | solution.py:468
  5.1 7.9 %collective-permute-start.3 = (f32[12,16,128]{2,1,0:T(8,128)S(1)}, f32[12,16,128]{2,1,0:T(8,128)S(1)}, u32[]{:S(2)}, u32[]{:S(2)}) collective-permute-start(f32[12,16,128]{2,1,0:T(8,128)S(1)} %pack_z.1), channel_id=1, source_target_pairs={{0,1},{1,0},{2,3},{3,2},{4,5},{5,4},{6,7},{7,6},{8,9},{9,8},{10,11... | collective-permute-start | bytes 294920 | tf_op jit(solution)/shard_map/ppermute | solution.py:468
  8.1 5.0 %collective-permute-start.1 = (f32[80,128]{1,0:T(8,128)S(1)}, f32[80,128]{1,0:T(8,128)S(1)}, u32[]{:S(2)}, u32[]{:S(2)}) collective-permute-start(f32[80,128]{1,0:T(8,128)S(1)} %get-tuple-element.35), channel_id=1, source_target_pairs={{0,24},{1,25},{2,26},{3,27},{4,28},{5,29},{6,30},{7,31},{8,16},{9,... | collective-permute-start | bytes 122888 | tf_op jit(solution)/shard_map/ppermute | solution.py:468
  9.0 4.0 %collective-permute-start.2 = (f32[16,128]{1,0:T(8,128)S(1)}, f32[16,128]{1,0:T(8,128)S(1)}, u32[]{:S(2)}, u32[]{:S(2)}) collective-permute-start(f32[16,128]{1,0:T(8,128)S(1)} %bitcast.12), channel_id=1, source_target_pairs={{0,25},{1,24},{2,27},{3,26},{4,29},{5,28},{6,31},{7,30},{8,17},{9,... | collective-permute-start | bytes 24584 | tf_op jit(solution)/shard_map/ppermute | solution.py:468
  13.1 4.2 %collective-permute-start.4 = (f32[80,128]{1,0:T(8,128)S(1)}, f32[80,128]{1,0:T(8,128)S(1)}, u32[]{:S(2)}, u32[]{:S(2)}) collective-permute-start(f32[80,128]{1,0:T(8,128)S(1)} %get-tuple-element.40), channel_id=1, source_target_pairs={{0,2},{1,3},{2,0},{3,1},{4,6},{5,7},{6,4},{7,5},{8,10},{9,11},{10,... | collective-permute-start | bytes 122888 | tf_op jit(solution)/shard_map/ppermute | solution.py:468
  14.8 2.5 %collective-permute-start.5 = (f32[80,128]{1,0:T(8,128)S(1)}, f32[80,128]{1,0:T(8,128)S(1)}, u32[]{:S(2)}, u32[]{:S(2)}) collective-permute-start(f32[80,128]{1,0:T(8,128)S(1)} %get-tuple-element.41), channel_id=1, source_target_pairs={{0,8},{1,9},{2,4},{3,5},{4,2},{5,3},{6,14},{7,15},{8,0},{9,1},{10,... | collective-permute-start | bytes 122888 | tf_op jit(solution)/shard_map/ppermute | solution.py:468

commit v5 on v4

--- a/solution.py
+++ b/solution.py
@@ -53,10 +53,12 @@
     return (cells >> 5) * 128 + ((cells >> 1) & 15) * 2, cells & 1
 
 
-def fill_one_hot(hot_ref, code, tiles, brick):
+def fill_one_hot(hot_ref, code, tiles, brick, masks=(None,)):
     blocks = code.shape[0]
-    for at, tile in enumerate(tiles):
+    for at, (mask, tile) in enumerate((mask, tile) for mask in masks for tile in tiles):
         lane_code = tile_code(tile, blocks, brick) - code
+        if mask is not None:
+            lane_code = jnp.where(mask, lane_code, -1)
         for node in range(16):
             hit = lane_code == (node // 4) * 64 + node % 4
             hot_ref[pl.ds(node * blocks, blocks), pl.ds(at * LANES, LANES)] = jnp.where(hit, 1.0, 0.0).astype(BF16)
@@ -122,6 +124,13 @@
 
 def from_rows(array_ref, flat_ref, first, blocks):
     channels = array_ref.shape[0]
+    if channels > 8:
+        tiles = flat_ref[pl.ds(first * blocks, 8 * blocks), :].reshape(8, blocks, LANES)
+        tiles = jnp.swapaxes(tiles, 0, 1)
+        for b in range(blocks):
+            array_ref[pl.ds(0, 8), pl.ds(b * LANES, LANES)] = tiles[b]
+            array_ref[pl.ds(8, 1), pl.ds(b * LANES, LANES)] = flat_ref[pl.ds((first + 8) * blocks + b, 1), :]
+        return
     for b in range(blocks):
         array_ref[:, pl.ds(b * LANES, LANES)] = flat_ref[pl.ds(first * blocks + b, channels, stride=blocks), :]
 
@@ -309,16 +318,17 @@
 
 
 def pack_y_kernel(ends, *refs):
-    grid_ref, xe_ref, xo_ref, *received = refs[:-2]
-    even_ref, odd_ref = refs[-2:]
+    grid_ref, xe_ref, xo_ref, *received = refs[:-3]
+    even_ref, odd_ref, sums_ref = refs[-3:]
     extra = xz_additions(xe_ref, xo_ref, received[:ends], received[ends:], 2)
     lower, upper = grid_ref[0] + extra[0], grid_ref[1] + extra[1]
+    sums_ref[0], sums_ref[1] = lower, upper
     here = is_even("gy")
     even_ref[...] = jnp.where(here, upper, lower)
     odd_ref[...] = jnp.where(here, lower, upper)
 
 
-def node_gradients(counts, brick, size_z, tiles, totals, total_ref, push_ref, drag_ref):
+def node_gradients(counts, brick, size_z, tiles, totals, total_ref, push_ref, drag_ref, apart=0):
     place = [lax.axis_index(axis) for axis in ("gx", "gy", "gz")]
     row = iota((8, LANES), 0)
     blank = jnp.zeros((8, LANES), F32)
@@ -342,8 +352,11 @@
             inverse = 1.0 / jnp.maximum(c[0], 1.0)
             scale = jnp.where(inside, (1.0 - c[7]) * inverse, 0.0)
             high, low = split(jnp.concatenate([c[4 + a] * scale for a in range(3)] + [blank], axis=0))
-            push_ref[pl.ds(64 * side, 32), lanes] = high
-            push_ref[pl.ds(64 * side + 32, 32), lanes] = low
+            if apart:
+                lanes = pl.ds((apart * side + at) * LANES, LANES)
+            for first in (0, 64) if apart else (64 * side,):
+                push_ref[pl.ds(first, 32), lanes] = high
+                push_ref[pl.ds(first + 32, 32), lanes] = low
             drags.append(
                 c[4] * (c[1] * inverse) + c[5] * (c[2] * inverse) + c[6] * (c[3] * inverse - gravity_step)
             )
@@ -356,8 +369,8 @@
 
 def early_kernel(counts, ends, size_z, *refs):
     inputs, refs = refs[:-7], refs[-7:]
-    hot_slab_ref, hot_ref, slab_ref, grid_ref, xe_ref, xo_ref, *received = inputs
-    gathered_ref, drag_slab_ref, drag_ref, total_ref, push_slab_ref, push_ref, _ = refs
+    meta_ref, hot_slab_ref, hot_ref, slab_ref, grid_ref, xe_ref, xo_ref, *received = inputs
+    gathered_ref, drag_slab_ref, drag_ref, masked_ref, total_ref, push_slab_ref, push_ref = refs
     brick = 4 * (grid_ref.shape[0] - 2)
     extra = xz_additions(xe_ref, xo_ref, received[:ends], received[ends:], SLABS)
     totals = [slab_ref[tile - 2] + extra[tile] for tile in (2, 3)]
@@ -365,15 +378,22 @@
     tiles = inner_tiles(brick)[2:]
     totals = [grid_ref[t - 2] + diagonal_rows([ref[t] for ref in received[ends:]]) for t in tiles]
     node_gradients(counts, brick, size_z, tiles, totals, total_ref, push_ref, drag_ref)
-    gathered_ref[...] = gather(hot_slab_ref[...], push_slab_ref) + gather(
+    gathered = gather(hot_slab_ref[...], push_slab_ref) + gather(
         hot_ref[:, pl.ds(2 * LANES, push_ref.shape[1])], push_ref
     )
-
-
-def collect_kernel(counts, ends, *refs):
+    upper = meta_ref[1] == 1
+    blocks = upper.shape[0]
+    keep = (iota((blocks, LANES), 1) < 64) != upper
+    for node in range(16):
+        value = gathered[node * blocks : (node + 1) * blocks]
+        gathered_ref[pl.ds(node * blocks, blocks), :] = jnp.where(keep, value, pltpu.roll(value, 64, 1))
+    fill_one_hot(masked_ref, meta_ref[0], (0, 1), brick, (jnp.logical_not(upper), upper))
+
+
+def collect_kernel(counts, *refs):
     inputs, refs = refs[:-10], refs[-10:]
-    meta_ref, shape_ref, hot_ref, take_spread_ref, top_ref, gathered_ref, drag_slab_ref, drag_ref = inputs[:8]
-    grid_ref, xe_ref, xo_ref, ye_ref, yo_ref, *received = inputs[8:]
+    meta_ref, shape_ref, masked_ref, take_spread_ref, top_ref, gathered_ref, drag_slab_ref, drag_ref = inputs[:8]
+    near_ref, ye_ref, yo_ref = inputs[8:]
     gvel_ref, gaff_ref, gvol_ref, gdrag_ref = refs[:4]
     total_ref, push_ref, drag_ends_ref, take_ref, pulled_ref, flat_ref = refs[4:]
     blocks = gvol_ref.shape[0]
@@ -381,11 +401,10 @@
     saved = [shape_ref[pl.ds(k * blocks, blocks), :] for k in range(12)]
     weight, frac = [saved[3 * k : 3 * k + 3] for k in range(3)], saved[9:]
 
-    extra = xz_additions(xe_ref, xo_ref, received[:ends], received[ends:], 2)
     low, high = low_high(ye_ref[...], yo_ref[...], "gy")
-    totals = [grid_ref[0] + extra[0] + low, grid_ref[1] + extra[1] + high]
-    node_gradients(counts, brick, size_z, (0, 1), totals, total_ref, push_ref, drag_ends_ref)
-    gathered = gathered_ref[...] + gather(hot_ref[:, pl.ds(0, 2 * LANES)], push_ref)
+    totals = [near_ref[0] + low, near_ref[1] + high]
+    node_gradients(counts, brick, size_z, (0, 1), totals, total_ref, push_ref, drag_ends_ref, 2)
+    gathered = gathered_ref[...] + gather(masked_ref[...], push_ref)
 
     edges = [drag_ends_ref[t] for t in range(2)]
     depth = iota((size_z, brick), 0) + lax.axis_index("gz") * size_z
@@ -406,17 +425,11 @@
 
     lane = iota((blocks, LANES), 1)
     low_half = lane < 64
-    upper = meta_ref[1] == 1
-    lows, highs = [], []
-    for node in range(16):
-        value = gathered[node * blocks : (node + 1) * blocks]
-        rolled = pltpu.roll(value, 64, 1)
-        lows.append(jnp.where(upper, rolled, value))
-        highs.append(jnp.where(upper, value, rolled))
+    nodes = [gathered[node * blocks : (node + 1) * blocks] for node in range(16)]
     for ox in range(3):
         for oy in range(3):
             for cx in range(2):
-                value = jnp.where(low_half, lows[4 * (cx + ox) + oy], highs[4 * (cx + ox) + oy + 1])
+                value = jnp.where(low_half, nodes[4 * (cx + ox) + oy], nodes[4 * (cx + ox) + oy + 1])
                 take_ref[pl.ds((3 * ox + oy) * blocks, blocks), pl.ds(cx * LANES, LANES)] = value.astype(BF16)
 
     pulled_ref[...] = jnp.dot(take_ref[...], take_spread_ref[...], preferred_element_type=F32)
@@ -553,33 +566,35 @@
         exchange(array, counts, lambda x, y, z: (x, y, paired(z, counts[2], first)))
         for first, array in enumerate(send_z)
     ]
-    send_ye, send_yo = call(
-        functools.partial(pack_y_kernel, ends), "pack_y", (slab, slab), (grid, xe, xo, *xz, *layers)
+    send_ye, send_yo, near_y = call(
+        functools.partial(pack_y_kernel, ends), "pack_y", (slab, slab, f32(2, ROWS, LANES)), (grid, xe, xo, *xz, *layers)
     )
     yo = exchange(send_yo, counts, odd_y)
     ye = exchange(send_ye, counts, lambda x, y, z: (x, paired(y, counts[1], 0), z))
-    gathered, drag_slab, drag_rows = call(
+    gathered, drag_slab, drag_rows, masked = call(
         functools.partial(early_kernel, counts, ends, size_z),
         "early",
-        (f32(16 * blocks, LANES), f32(2, size_z, LANES), f32(interior, size_z, LANES)),
-        (hot_edge, hot, edge, grid, xe, xo, *xz, *layers),
+        (
+            f32(16 * blocks, LANES), f32(2, size_z, LANES), f32(interior, size_z, LANES),
+            bf16(16 * blocks, 4 * LANES),
+        ),
+        (meta, hot_edge, hot, edge, grid, xe, xo, *xz, *layers),
         scratch=[
             pltpu.VMEM((interior, ROWS + 16, LANES), F32),
             pltpu.VMEM((LANES, 2 * LANES), BF16),
             pltpu.VMEM((LANES, interior * LANES), BF16),
-            pltpu.VMEM((8, LANES), F32),
         ],
         megabytes=8,
         flops=1_000_000_000,
     )
     grad_velocity, grad_affine, grad_volume, grad_drag = call(
-        functools.partial(collect_kernel, counts, ends),
+        functools.partial(collect_kernel, counts),
         "collect",
         (f32(3, blocks * LANES), f32(9, blocks * LANES), f32(blocks, LANES), f32(brick, size_z, brick)),
-        (meta, shape, hot, take, baffle_top, gathered, drag_slab, drag_rows, grid, xe, xo, ye, yo, *xz, *layers),
+        (meta, shape, masked, take, baffle_top, gathered, drag_slab, drag_rows, near_y, ye, yo),
         scratch=[
             pltpu.VMEM((2, ROWS + 16, LANES), F32),
-            pltpu.VMEM((LANES, 2 * LANES), BF16),
+            pltpu.VMEM((LANES, 4 * LANES), BF16),
             pltpu.VMEM((2, size_z, LANES), F32),
             pltpu.VMEM((9 * blocks, 2 * LANES), BF16),
             pltpu.VMEM((9 * blocks, 9 * LANES), F32),

time: 19.2 us -> 19 us (0.990)
  no operation moved by 1% of the time
where the time goes in v5:
time: 19 us; the launch traced here: 18.9 us
  starting transfers between devices  6.69 us (35%)
  waiting for transfers between devices  5.34 us (28%)
  Pallas kernels  5.32 us (28%)
  between operations  1.47 us (8%)
    ppermute x6, starting transfers between devices, exchange(): return lax.ppermute(array, names, links) if links else jnp.zeros_like(array)  6.69 us
    ppermute x6, waiting for transfers between devices, exchange(): return lax.ppermute(array, names, links) if links else jnp.zeros_like(array)  5.34 us
    pallas_call x7, Pallas kernels, call(): pl.pallas_call(kernel, out_shape=out_shape, in_specs=[vmem] * len(operand...  5.32 us
  transfers between devices with their start and end apart: 6, of which 3 were waited for; matrix products, arithmetic and copies ran while one was open for 0% of the time, Pallas kernels for 7%

profile of v5, /device:TPU:0, one launch (start us, length us, event | category | flops | bytes accessed | tf_op | source)
XLA Modules:
  0.0 18.9 jit_solution(5730311878099833156)
XLA Ops:
  0.6 0.0 copy-start.3
  0.6 0.0 copy-start.2
  0.7 0.0 copy-start.8
  0.7 0.0 copy-start.1
  0.7 0.0 copy-start.6
  0.7 0.0 copy-start.7
  0.7 0.0 copy-start
  0.7 0.0 copy-start.5
  0.7 0.0 copy-start.4
  0.7 0.4 %spread.1 = (bf16[2688,256]{1,0:T(8,128)(2,1)S(1)}, bf16[256,1152]{1,0:T(8,128)(2,1)S(1)}) custom-call(), custom_call_target="tpu_custom_call" | custom-call | flops 20000000000 | bytes 1024 | tf_op jit(solution)/shard_map/spread/pallas_call | solution.py:500
  1.8 0.0 copy-done.3
  1.8 0.0 copy-done.2
  1.8 0.0 copy-done.8
  1.8 0.0 copy-done.1
  1.8 0.0 copy-done.6
  1.8 0.0 copy-done.7
  1.8 0.0 copy-done
  1.8 0.0 copy-done.5
  1.9 0.0 copy-done.4
  1.9 1.8 %deposit.1 = (f32[2,80,128]{2,1,0:T(8,128)S(1)}, f32[80,128]{1,0:T(8,128)S(1)}, f32[80,128]{1,0:T(8,128)S(1)}, f32[1,16,128]{2,1,0:T(8,128)S(1)}, s32[3,32,128]{...) custom-call(s32[1,32]{1,0:T(1,128)S(1)} %bitcast.11, ...), custom_call_target="tpu_custom_call" | custom-call | bytes 1024 | tf_op jit(solution)/shard_map/deposit/pallas_call | solution.py:500
  3.7 0.5 %collective-permute-start = (f32[80,128]{1,0:T(8,128)S(1)}, f32[80,128]{1,0:T(8,128)S(1)}, u32[]{:S(2)}, u32[]{:S(2)}) collective-permute-start(f32[80,128]{1,0:T(8,128)S(1)} %get-tuple-element.35), channel_id=1, source_target_pairs={{0,8},{1,9},{2,10},{3,11},{4,12},{5,13},{6,14},{7,15},{8,0},{9,1},... | collective-permute-start | bytes 122888 | tf_op jit(solution)/shard_map/ppermute | solution.py:481
  4.2 0.6 %interior.1 = (f32[10,80,128]{2,1,0:T(8,128)S(1)}, bf16[512,1280]{1,0:T(8,128)(2,1)S(1)}) custom-call(bf16[512,256]{1,0:T(8,128)(2,1)S(1)} %get-tuple-element.31.window_ref, s32[3,32,128]{2,1,0:T(8,128)S(1)} %get-tuple-element.28.meta_ref.refs_0_, s32[32,32]{1,0:T(8,128)S(1)} %copy-done.3, f32[32,8,32]{2,1,0:T(8,128)S(1)} %bitcast.9), custom_call_target="tpu_custom_call" | custom-call | flops 1000000000 | bytes 1024 | tf_op jit(solution)/shard_map/interior/pallas_call | solution.py:500
  4.8 0.2 %collective-permute-done.xe_ref.refs_5_.refs_1_ = f32[80,128]{1,0:T(8,128)S(1)} collective-permute-done((f32[80,128]{1,0:T(8,128)S(1)}, f32[80,128]{1,0:T(8,128)S(1)}, u32[]{:S(2)}, u32[]{:S(2)}) %collective-permute-start) | collective-permute-done | bytes 40992 | tf_op jit(solution)/shard_map/ppermute | solution.py:481
  5.0 0.1 pack_z.1
  5.1 2.9 %collective-permute-start.3 = (f32[12,16,128]{2,1,0:T(8,128)S(1)}, f32[12,16,128]{2,1,0:T(8,128)S(1)}, u32[]{:S(2)}, u32[]{:S(2)}) collective-permute-start(f32[12,16,128]{2,1,0:T(8,128)S(1)} %pack_z.1), channel_id=1, source_target_pairs={{0,1},{1,0},{2,3},{3,2},{4,5},{5,4},{6,7},{7,6},{8,9},{9,8},{10,11... | collective-permute-start | bytes 294920 | tf_op jit(solution)/shard_map/ppermute | solution.py:481
  8.1 1.0 %collective-permute-start.1 = (f32[80,128]{1,0:T(8,128)S(1)}, f32[80,128]{1,0:T(8,128)S(1)}, u32[]{:S(2)}, u32[]{:S(2)}) collective-permute-start(f32[80,128]{1,0:T(8,128)S(1)} %get-tuple-element.36), channel_id=1, source_target_pairs={{0,24},{1,25},{2,26},{3,27},{4,28},{5,29},{6,30},{7,31},{8,16},{9,... | collective-permute-start | bytes 122888 | tf_op jit(solution)/shard_map/ppermute | solution.py:481
  9.0 0.3 %collective-permute-start.2 = (f32[16,128]{1,0:T(8,128)S(1)}, f32[16,128]{1,0:T(8,128)S(1)}, u32[]{:S(2)}, u32[]{:S(2)}) collective-permute-start(f32[16,128]{1,0:T(8,128)S(1)} %bitcast.12), channel_id=1, source_target_pairs={{0,25},{1,24},{2,27},{3,26},{4,29},{5,28},{6,31},{7,30},{8,17},{9,... | collective-permute-start | bytes 24584 | tf_op jit(solution)/shard_map/ppermute | solution.py:481
  9.3 3.7 %collective-permute-done.2.refs_7_.refs_3_ = f32[16,128]{1,0:T(8,128)S(1)} collective-permute-done((f32[16,128]{1,0:T(8,128)S(1)}, f32[16,128]{1,0:T(8,128)S(1)}, u32[]{:S(2)}, u32[]{:S(2)}) %collective-permute-start.2) | collective-permute-done | bytes 8224 | tf_op jit(solution)/shard_map/ppermute | solution.py:481
  13.0 0.0 collective-permute-done.1.refs_6_.refs_2_
  13.0 0.0 collective-permute-done.3.refs_8_.refs_4_
  13.0 0.1 pack_y.1
  13.1 1.6 %collective-permute-start.4 = (f32[80,128]{1,0:T(8,128)S(1)}, f32[80,128]{1,0:T(8,128)S(1)}, u32[]{:S(2)}, u32[]{:S(2)}) collective-permute-start(f32[80,128]{1,0:T(8,128)S(1)} %get-tuple-element.44), channel_id=1, source_target_pairs={{0,2},{1,3},{2,0},{3,1},{4,6},{5,7},{6,4},{7,5},{8,10},{9,11},{10,... | collective-permute-start | bytes 122888 | tf_op jit(solution)/shard_map/ppermute | solution.py:481
  14.8 0.3 %collective-permute-start.5 = (f32[80,128]{1,0:T(8,128)S(1)}, f32[80,128]{1,0:T(8,128)S(1)}, u32[]{:S(2)}, u32[]{:S(2)}) collective-permute-start(f32[80,128]{1,0:T(8,128)S(1)} %get-tuple-element.45), channel_id=1, source_target_pairs={{0,8},{1,9},{2,4},{3,5},{4,2},{5,3},{6,14},{7,15},{8,0},{9,1},{10,... | collective-permute-start | bytes 122888 | tf_op jit(solution)/shard_map/ppermute | solution.py:481
  15.1 0.8 %early.1 = (f32[512,128]{1,0:T(8,128)S(1)}, f32[2,8,128]{2,1,0:T(8,128)S(1)}, f32[8,8,128]{2,1,0:T(8,128)S(1)}, bf16[512,512]{1,0:T(8,128)(2,1)S(1)}) custom-call(s32[3,32,128]{2,1,0:T(8,128)S(1)} %get-tuple-element.28.meta_ref.refs_0_, bf16[512,256]{1,0:T(8,128)(2,1)S(1)} %get-tuple-element.30.refs_1_, bf16[512,1280]{1,0:T(8,128)(2,1)S(1)} %get-tuple-element.32.refs_2_, ...), custom_call_target="tpu_custom_call" | custom-call | flops 1000000000 | bytes 1024 | tf_op jit(solution)/shard_map/early/pallas_call | solution.py:500
  15.9 1.4 %collective-permute-done.4.refs_9_ = f32[80,128]{1,0:T(8,128)S(1)} collective-permute-done((f32[80,128]{1,0:T(8,128)S(1)}, f32[80,128]{1,0:T(8,128)S(1)}, u32[]{:S(2)}, u32[]{:S(2)}) %collective-permute-start.4) | collective-permute-done | bytes 40992 | tf_op jit(solution)/shard_map/ppermute | solution.py:481
  17.3 0.0 collective-permute-done.5.refs_10_
  17.3 1.5 %collect.1 = (f32[3,4096]{1,0:T(4,128)}, f32[9,4096]{1,0:T(8,128)}, f32[32,128]{1,0:T(8,128)}, f32[32,8,32]{2,1,0:T(8,128)}) custom-call(s32[3,32,128]{2,1,0:T(8,128)S(1)} %get-tuple-element.28.meta_ref.refs_0_, f32[384,128]{1,0:T(8,128)S(1)} %get-tuple-element.29.refs_1_, bf16[512,512]{1,0:T(8,128)(2,1)S(1)} %get-tuple-element.38.refs_2_, ...), custom_call_target="tpu_custom_call" | custom-call | bytes 1024 | tf_op jit(solution)/shard_map/collect/pallas_call | solution.py:500
Async XLA Ops:
  0.6 1.1 %copy-start.3 = (s32[32,32]{1,0:T(8,128)S(1)}, s32[32,32]{1,0:T(8,128)}, u32[]{:S(2)}) copy-start(s32[32,32]{1,0:T(8,128)} %refs_4_.3) | copy-start | bytes 12292
  0.6 1.1 %copy-start.2 = (f32[32,32,8]{1,2,0:T(8,128)S(1)}, f32[32,32,8]{1,2,0:T(8,128)}, u32[]{:S(2)}) copy-start(f32[32,32,8]{1,2,0:T(8,128)} %param.19) | copy-start | bytes 98308
  0.7 1.1 %copy-start.8 = (s32[32]{0:T(128)S(1)}, s32[32]{0:T(128)}, u32[]{:S(2)}) copy-start(s32[32]{0:T(128)} %param.16) | copy-start | bytes 388
  0.7 1.1 %copy-start.1 = (f32[9,4096]{1,0:T(8,128)S(1)}, f32[9,4096]{1,0:T(8,128)}, u32[]{:S(2)}) copy-start(f32[9,4096]{1,0:T(8,128)} %refs_7_.1) | copy-start | bytes 442372
  0.7 1.1 %copy-start.6 = (f32[3,4096]{1,0:T(4,128)S(1)}, f32[3,4096]{1,0:T(4,128)}, u32[]{:S(2)}) copy-start(f32[3,4096]{1,0:T(4,128)} %refs_6_.1) | copy-start | bytes 147460
  0.7 1.1 %copy-start.7 = (f32[4096]{0:T(1024)S(1)}, f32[4096]{0:T(1024)}, u32[]{:S(2)}) copy-start(f32[4096]{0:T(1024)} %param.13) | copy-start | bytes 49156
  0.7 1.1 %copy-start = (f32[9,4096]{1,0:T(8,128)S(1)}, f32[9,4096]{1,0:T(8,128)}, u32[]{:S(2)}) copy-start(f32[9,4096]{1,0:T(8,128)} %refs_4_.2) | copy-start | bytes 442372
  0.7 1.1 %copy-start.5 = (f32[3,4096]{1,0:T(4,128)S(1)}, f32[3,4096]{1,0:T(4,128)}, u32[]{:S(2)}) copy-start(f32[3,4096]{1,0:T(4,128)} %refs_3_.1) | copy-start | bytes 147460
  0.7 1.1 %copy-start.4 = (f32[3,4096]{1,0:T(4,128)S(1)}, f32[3,4096]{1,0:T(4,128)}, u32[]{:S(2)}) copy-start(f32[3,4096]{1,0:T(4,128)} %refs_2_.1) | copy-start | bytes 147460
  3.7 1.4 %collective-permute-start = (f32[80,128]{1,0:T(8,128)S(1)}, f32[80,128]{1,0:T(8,128)S(1)}, u32[]{:S(2)}, u32[]{:S(2)}) collective-permute-start(f32[80,128]{1,0:T(8,128)S(1)} %get-tuple-element.35), channel_id=1, source_target_pairs={{0,8},{1,9},{2,10},{3,11},{4,12},{5,13},{6,14},{7,15},{8,0},{9,1},... | collective-permute-start | bytes 122888 | tf_op jit(solution)/shard_map/ppermute | solution.py:481
  5.1 7.9 %collective-permute-start.3 = (f32[12,16,128]{2,1,0:T(8,128)S(1)}, f32[12,16,128]{2,1,0:T(8,128)S(1)}, u32[]{:S(2)}, u32[]{:S(2)}) collective-permute-start(f32[12,16,128]{2,1,0:T(8,128)S(1)} %pack_z.1), channel_id=1, source_target_pairs={{0,1},{1,0},{2,3},{3,2},{4,5},{5,4},{6,7},{7,6},{8,9},{9,8},{10,11... | collective-permute-start | bytes 294920 | tf_op jit(solution)/shard_map/ppermute | solution.py:481
  8.1 5.0 %collective-permute-start.1 = (f32[80,128]{1,0:T(8,128)S(1)}, f32[80,128]{1,0:T(8,128)S(1)}, u32[]{:S(2)}, u32[]{:S(2)}) collective-permute-start(f32[80,128]{1,0:T(8,128)S(1)} %get-tuple-element.36), channel_id=1, source_target_pairs={{0,24},{1,25},{2,26},{3,27},{4,28},{5,29},{6,30},{7,31},{8,16},{9,... | collective-permute-start | bytes 122888 | tf_op jit(solution)/shard_map/ppermute | solution.py:481
  9.0 4.0 %collective-permute-start.2 = (f32[16,128]{1,0:T(8,128)S(1)}, f32[16,128]{1,0:T(8,128)S(1)}, u32[]{:S(2)}, u32[]{:S(2)}) collective-permute-start(f32[16,128]{1,0:T(8,128)S(1)} %bitcast.12), channel_id=1, source_target_pairs={{0,25},{1,24},{2,27},{3,26},{4,29},{5,28},{6,31},{7,30},{8,17},{9,... | collective-permute-start | bytes 24584 | tf_op jit(solution)/shard_map/ppermute | solution.py:481
  13.1 4.2 %collective-permute-start.4 = (f32[80,128]{1,0:T(8,128)S(1)}, f32[80,128]{1,0:T(8,128)S(1)}, u32[]{:S(2)}, u32[]{:S(2)}) collective-permute-start(f32[80,128]{1,0:T(8,128)S(1)} %get-tuple-element.44), channel_id=1, source_target_pairs={{0,2},{1,3},{2,0},{3,1},{4,6},{5,7},{6,4},{7,5},{8,10},{9,11},{10,... | collective-permute-start | bytes 122888 | tf_op jit(solution)/shard_map/ppermute | solution.py:481
  14.8 2.5 %collective-permute-start.5 = (f32[80,128]{1,0:T(8,128)S(1)}, f32[80,128]{1,0:T(8,128)S(1)}, u32[]{:S(2)}, u32[]{:S(2)}) collective-permute-start(f32[80,128]{1,0:T(8,128)S(1)} %get-tuple-element.45), channel_id=1, source_target_pairs={{0,8},{1,9},{2,4},{3,5},{4,2},{5,3},{6,14},{7,15},{8,0},{9,1},{10,... | collective-permute-start | bytes 122888 | tf_op jit(solution)/shard_map/ppermute | solution.py:481

commit v6 on v5

--- a/solution.py
+++ b/solution.py
@@ -259,7 +259,8 @@
 
     low, high = grid_ref[0], grid_ref[1]
     here = is_even("gx")
-    even_ref[...] = jnp.where(here, high, low)
+    even_ref[pl.ds(0, ROWS), :] = jnp.where(here, high, low)
+    even_ref[pl.ds(ROWS, even_ref.shape[0] - ROWS), :] = jnp.zeros((even_ref.shape[0] - ROWS, LANES), F32)
     odd_ref[...] = jnp.where(here, low, high)
     here = is_even("gz")
     lower, upper = odd_ref[pl.ds(0, 16), :], odd_ref[pl.ds(ROWS - 16, 16), :]
@@ -286,6 +287,20 @@
         grid_ref[at, pl.ds(8 + 7, size_z, stride=8), :] = plane
 
 
+def join_columns(near_y, near_x):
+    lane = iota(near_y.shape, 1)
+    near_x = jnp.where(lane < 98, pltpu.roll(near_x, 67, 1), pltpu.roll(near_x, 65, 1))
+    return jnp.where(lane < 68, near_y, near_x)
+
+
+def joined_columns(joined, near_x):
+    lane = iota(joined.shape, 1)
+    if not near_x:
+        return jnp.where(lane < 68, joined, 0.0)
+    first, second = (lane >= 1) & (lane <= 30), (lane >= 33) & (lane <= 62)
+    return jnp.where(first, pltpu.roll(joined, 61, 1), jnp.where(second, pltpu.roll(joined, 63, 1), 0.0))
+
+
 def own_tile(slab_ref, grid_ref, tile):
     return grid_ref[tile] if tile < 2 else slab_ref[tile - 2] if tile < SLABS else grid_ref[tile - 2]
 
@@ -297,7 +312,8 @@
         rows = pl.ds(first, 16)
         received = xe_ref[rows, :]
         extra = x_additions(*low_high(received, jnp.zeros_like(received), "gx"))
-        ends.append([own_tile(slab_ref, grid_ref, t)[first : first + 16] + extra[t] for t in range(SLABS)])
+        tiles = [own_tile(slab_ref, grid_ref, t)[first : first + 16] + extra[t] for t in range(SLABS)]
+        ends.append([join_columns(tiles[t], tiles[t + 2]) for t in range(2)])
         ends[-1] += [grid_ref[t, rows, :] for t in range(2, grid_ref.shape[0])]
     for tile, (lower, upper) in enumerate(zip(*ends)):
         even_ref[tile] = jnp.where(here, upper, lower)
@@ -311,10 +327,15 @@
     return [lower, upper, jnp.where(planar, low, 0.0), jnp.where(planar, high, 0.0)]
 
 
+def keep_kernel(received_ref, kept_ref):
+    kept_ref[...] = received_ref[...]
+
+
 def xz_additions(xe_ref, xo_ref, diagonals, layers, tiles):
     odd = xo_ref[...] + diagonal_rows([ref[...] for ref in diagonals])
-    extra = x_additions(*low_high(xe_ref[...], odd, "gx"))
-    return [extra[t] + diagonal_rows([ref[t] for ref in layers]) for t in range(tiles)]
+    extra = x_additions(*low_high(xe_ref[pl.ds(0, ROWS), :], odd, "gx"))
+    joined = [diagonal_rows([ref[t] for ref in layers]) for t in range(2)]
+    return [extra[t] + joined_columns(joined[t % 2], t >= 2) for t in range(tiles)]
 
 
 def pack_y_kernel(ends, *refs):
@@ -376,7 +397,7 @@
     totals = [slab_ref[tile - 2] + extra[tile] for tile in (2, 3)]
     node_gradients(counts, brick, size_z, (2, 3), totals, total_ref, push_slab_ref, drag_slab_ref)
     tiles = inner_tiles(brick)[2:]
-    totals = [grid_ref[t - 2] + diagonal_rows([ref[t] for ref in received[ends:]]) for t in tiles]
+    totals = [grid_ref[t - 2] + diagonal_rows([ref[t - 2] for ref in received[ends:]]) for t in tiles]
     node_gradients(counts, brick, size_z, tiles, totals, total_ref, push_ref, drag_ref)
     gathered = gather(hot_slab_ref[...], push_slab_ref) + gather(
         hot_ref[:, pl.ds(2 * LANES, push_ref.shape[1])], push_ref
@@ -521,7 +542,7 @@
         deposit_kernel,
         "deposit",
         (
-            f32(2, ROWS, LANES), slab, slab, f32(ends, 16, LANES),
+            f32(2, ROWS, LANES), f32(256, LANES), slab, f32(ends, 16, LANES),
             jax.ShapeDtypeStruct((3, blocks, LANES), jnp.int32), f32(12 * blocks, LANES),
             bf16(16 * blocks, 2 * LANES), bf16(16 * blocks, 2 * LANES),
         ),
@@ -538,18 +559,22 @@
     def even_x(x):
         return paired(x, counts[0], 0)
 
-    def odd_x(x):
+    def odd_x(x, y, z):
         partner = paired(x, counts[0], 1)
-        return counts[0] - 1 - x if partner is None and counts[0] % 2 == 0 else partner
+        return (x, y, paired(z, counts[2], 0)) if partner is None else (partner, y, z)
+
+    def odd_xz(x, y, z, first):
+        partner = paired(x, counts[0], 1)
+        return x if partner is None else partner, y, paired(z, counts[2], first)
 
     def odd_y(x, y, z):
         partner = paired(y, counts[1], 1)
         return (even_x(x), y, z) if partner is None else (x, partner, z)
 
     xe = exchange(send_xe, counts, lambda x, y, z: (even_x(x), y, z))
-    xo = exchange(send_xo, counts, lambda x, y, z: (odd_x(x), y, z))
+    xo = exchange(send_xo, counts, odd_x)
     xz = [
-        exchange(send_xz[first], counts, lambda x, y, z: (odd_x(x), y, paired(z, counts[2], first)))
+        exchange(send_xz[first], counts, lambda x, y, z: odd_xz(x, y, z, first))
         for first in range(ends)
     ]
     grid, hot = call(
@@ -561,7 +586,8 @@
         megabytes=8,
         flops=1_000_000_000,
     )
-    send_z = call(pack_z_kernel, "pack_z", (f32(SLABS + interior, 16, LANES),) * ends, (edge, grid, xe))
+    (xo,) = call(keep_kernel, "keep", (slab,), (xo,), flops=700_000_000)
+    send_z = call(pack_z_kernel, "pack_z", (f32(2 + interior, 16, LANES),) * ends, (edge, grid, xe))
     layers = [
         exchange(array, counts, lambda x, y, z: (x, y, paired(z, counts[2], first)))
         for first, array in enumerate(send_z)

time: 19 us -> 18.2 us (0.958)
  waiting for transfers between devices: 5.34 us -> 3.9 us
  starting transfers between devices: 6.69 us -> 7.34 us
    ppermute x6, waiting for transfers between devices: 5.34 us -> 3.9 us  [exchange(): return lax.ppermute(array, names, links) if links else jnp.zeros_like(array)]
    ppermute x6, starting transfers between devices: 6.69 us -> 7.34 us  [exchange(): return lax.ppermute(array, names, links) if links else jnp.zeros_like(array)]
    pallas_call x7 -> x8, Pallas kernels: 5.32 us -> 5.35 us  [call(): pl.pallas_call(kernel, out_shape=out_shape, in_specs=[vmem] * len(operand...]
  transfers between devices with their start and end apart: 6 -> 6, of which waited for: 3 -> 2; matrix products, arithmetic and copies ran while one was open for 0% -> 0% of each run, Pallas kernels for 7% -> 8%
where the time goes in v6:
time: 18.2 us; the launch traced here: 18.1 us
  starting transfers between devices  7.34 us (40%)
  Pallas kernels  5.35 us (29%)
  waiting for transfers between devices  3.9 us (21%)
  between operations  1.47 us (8%)
    ppermute x6, starting transfers between devices, exchange(): return lax.ppermute(array, names, links) if links else jnp.zeros_like(array)  7.34 us
    pallas_call x8, Pallas kernels, call(): pl.pallas_call(kernel, out_shape=out_shape, in_specs=[vmem] * len(operand...  5.35 us
    ppermute x6, waiting for transfers between devices, exchange(): return lax.ppermute(array, names, links) if links else jnp.zeros_like(array)  3.9 us
  transfers between devices with their start and end apart: 6, of which 2 were waited for; matrix products, arithmetic and copies ran while one was open for 0% of the time, Pallas kernels for 8%

profile of v6, /device:TPU:0, one launch (start us, length us, event | category | flops | bytes accessed | tf_op | source)
XLA Modules:
  0.0 18.1 jit_solution(16810905824755851972)
XLA Ops:
  0.6 0.0 copy-start.3
  0.6 0.0 copy-start.2
  0.7 0.0 copy-start.8
  0.7 0.0 copy-start.1
  0.7 0.0 copy-start.6
  0.7 0.0 copy-start.7
  0.7 0.0 copy-start
  0.7 0.0 copy-start.5
  0.7 0.0 copy-start.4
  0.7 0.4 %spread.1 = (bf16[2688,256]{1,0:T(8,128)(2,1)S(1)}, bf16[256,1152]{1,0:T(8,128)(2,1)S(1)}) custom-call(), custom_call_target="tpu_custom_call" | custom-call | flops 20000000000 | bytes 1024 | tf_op jit(solution)/shard_map/spread/pallas_call | solution.py:521
  1.8 0.0 copy-done.3
  1.8 0.0 copy-done.2
  1.8 0.0 copy-done.8
  1.8 0.0 copy-done.1
  1.8 0.0 copy-done.6
  1.8 0.0 copy-done.7
  1.8 0.0 copy-done
  1.8 0.0 copy-done.5
  1.9 0.0 copy-done.4
  1.9 1.8 %deposit.1 = (f32[2,80,128]{2,1,0:T(8,128)S(1)}, f32[256,128]{1,0:T(8,128)S(1)}, f32[80,128]{1,0:T(8,128)S(1)}, f32[1,16,128]{2,1,0:T(8,128)S(1)}, s32[3,32,128]...) custom-call(s32[1,32]{1,0:T(1,128)S(1)} %bitcast.11, ...), custom_call_target="tpu_custom_call" | custom-call | bytes 1024 | tf_op jit(solution)/shard_map/deposit/pallas_call | solution.py:521
  3.6 0.5 %collective-permute-start = (f32[256,128]{1,0:T(8,128)S(1)}, f32[256,128]{1,0:T(8,128)S(1)}, u32[]{:S(2)}, u32[]{:S(2)}) collective-permute-start(f32[256,128]{1,0:T(8,128)S(1)} %get-tuple-element.35), channel_id=1, source_target_pairs={{0,8},{1,9},{2,10},{3,11},{4,12},{5,13},{6,14},{7,15},{8,0},{9,1},... | collective-permute-start | bytes 393224 | tf_op jit(solution)/shard_map/ppermute | solution.py:502
  4.2 2.6 %collective-permute-start.1 = (f32[80,128]{1,0:T(8,128)S(1)}, f32[80,128]{1,0:T(8,128)S(1)}, u32[]{:S(2)}, u32[]{:S(2)}) collective-permute-start(f32[80,128]{1,0:T(8,128)S(1)} %get-tuple-element.36), channel_id=1, source_target_pairs={{0,1},{1,0},{2,3},{3,2},{4,5},{5,4},{6,7},{7,6},{8,16},{9,17},{10,... | collective-permute-start | bytes 122888 | tf_op jit(solution)/shard_map/ppermute | solution.py:502
  6.8 0.6 %interior.1 = (f32[10,80,128]{2,1,0:T(8,128)S(1)}, bf16[512,1280]{1,0:T(8,128)(2,1)S(1)}) custom-call(bf16[512,256]{1,0:T(8,128)(2,1)S(1)} %get-tuple-element.31.window_ref, s32[3,32,128]{2,1,0:T(8,128)S(1)} %get-tuple-element.28.meta_ref.refs_0_, s32[32,32]{1,0:T(8,128)S(1)} %copy-done.3, f32[32,8,32]{2,1,0:T(8,128)S(1)} %bitcast.9), custom_call_target="tpu_custom_call" | custom-call | flops 1000000000 | bytes 1024 | tf_op jit(solution)/shard_map/interior/pallas_call | solution.py:521
  7.4 0.0 collective-permute-done.xe_ref.refs_5_.refs_1_
  7.4 0.1 pack_z.1
  7.5 0.7 %collective-permute-start.3 = (f32[10,16,128]{2,1,0:T(8,128)S(1)}, f32[10,16,128]{2,1,0:T(8,128)S(1)}, u32[]{:S(2)}, u32[]{:S(2)}) collective-permute-start(f32[10,16,128]{2,1,0:T(8,128)S(1)} %pack_z.1), channel_id=1, source_target_pairs={{0,1},{1,0},{2,3},{3,2},{4,5},{5,4},{6,7},{7,6},{8,9},{9,8},{10,11... | collective-permute-start | bytes 245768 | tf_op jit(solution)/shard_map/ppermute | solution.py:502
  8.2 1.4 %collective-permute-start.2 = (f32[16,128]{1,0:T(8,128)S(1)}, f32[16,128]{1,0:T(8,128)S(1)}, u32[]{:S(2)}, u32[]{:S(2)}) collective-permute-start(f32[16,128]{1,0:T(8,128)S(1)} %bitcast.12), channel_id=1, source_target_pairs={{0,1},{1,0},{2,3},{3,2},{4,5},{5,4},{6,7},{7,6},{8,17},{9,16},{10,... | collective-permute-start | bytes 24584 | tf_op jit(solution)/shard_map/ppermute | solution.py:502
  9.6 0.0 collective-permute-done.1.received_ref
  9.6 2.5 %collective-permute-done.2.refs_7_.refs_3_ = f32[16,128]{1,0:T(8,128)S(1)} collective-permute-done((f32[16,128]{1,0:T(8,128)S(1)}, f32[16,128]{1,0:T(8,128)S(1)}, u32[]{:S(2)}, u32[]{:S(2)}) %collective-permute-start.2) | collective-permute-done | bytes 8224 | tf_op jit(solution)/shard_map/ppermute | solution.py:502
  12.1 0.0 collective-permute-done.3.refs_8_.refs_4_
  12.1 0.1 pack_y.1
  12.2 1.6 %collective-permute-start.4 = (f32[80,128]{1,0:T(8,128)S(1)}, f32[80,128]{1,0:T(8,128)S(1)}, u32[]{:S(2)}, u32[]{:S(2)}) collective-permute-start(f32[80,128]{1,0:T(8,128)S(1)} %get-tuple-element.44), channel_id=1, source_target_pairs={{0,2},{1,3},{2,0},{3,1},{4,6},{5,7},{6,4},{7,5},{8,10},{9,11},{10,... | collective-permute-start | bytes 122888 | tf_op jit(solution)/shard_map/ppermute | solution.py:502
  13.9 0.5 %collective-permute-start.5 = (f32[80,128]{1,0:T(8,128)S(1)}, f32[80,128]{1,0:T(8,128)S(1)}, u32[]{:S(2)}, u32[]{:S(2)}) collective-permute-start(f32[80,128]{1,0:T(8,128)S(1)} %get-tuple-element.45), channel_id=1, source_target_pairs={{0,8},{1,9},{2,4},{3,5},{4,2},{5,3},{6,14},{7,15},{8,0},{9,1},{10,... | collective-permute-start | bytes 122888 | tf_op jit(solution)/shard_map/ppermute | solution.py:502
  14.4 0.8 %early.1 = (f32[512,128]{1,0:T(8,128)S(1)}, f32[2,8,128]{2,1,0:T(8,128)S(1)}, f32[8,8,128]{2,1,0:T(8,128)S(1)}, bf16[512,512]{1,0:T(8,128)(2,1)S(1)}) custom-call(s32[3,32,128]{2,1,0:T(8,128)S(1)} %get-tuple-element.28.meta_ref.refs_0_, bf16[512,256]{1,0:T(8,128)(2,1)S(1)} %get-tuple-element.30.refs_1_, bf16[512,1280]{1,0:T(8,128)(2,1)S(1)} %get-tuple-element.32.refs_2_, ...), custom_call_target="tpu_custom_call" | custom-call | flops 1000000000 | bytes 1024 | tf_op jit(solution)/shard_map/early/pallas_call | solution.py:521
  15.2 1.4 %collective-permute-done.4.refs_9_ = f32[80,128]{1,0:T(8,128)S(1)} collective-permute-done((f32[80,128]{1,0:T(8,128)S(1)}, f32[80,128]{1,0:T(8,128)S(1)}, u32[]{:S(2)}, u32[]{:S(2)}) %collective-permute-start.4) | collective-permute-done | bytes 40992 | tf_op jit(solution)/shard_map/ppermute | solution.py:502
  16.5 0.0 collective-permute-done.5.refs_10_
  16.6 1.5 %collect.1 = (f32[3,4096]{1,0:T(4,128)}, f32[9,4096]{1,0:T(8,128)}, f32[32,128]{1,0:T(8,128)}, f32[32,8,32]{2,1,0:T(8,128)}) custom-call(s32[3,32,128]{2,1,0:T(8,128)S(1)} %get-tuple-element.28.meta_ref.refs_0_, f32[384,128]{1,0:T(8,128)S(1)} %get-tuple-element.29.refs_1_, bf16[512,512]{1,0:T(8,128)(2,1)S(1)} %get-tuple-element.38.refs_2_, ...), custom_call_target="tpu_custom_call" | custom-call | bytes 1024 | tf_op jit(solution)/shard_map/collect/pallas_call | solution.py:521
  (1 shorter events, 0.0 us)
Async XLA Ops:
  0.6 1.1 %copy-start.3 = (s32[32,32]{1,0:T(8,128)S(1)}, s32[32,32]{1,0:T(8,128)}, u32[]{:S(2)}) copy-start(s32[32,32]{1,0:T(8,128)} %refs_4_.3) | copy-start | bytes 12292
  0.6 1.1 %copy-start.2 = (f32[32,32,8]{1,2,0:T(8,128)S(1)}, f32[32,32,8]{1,2,0:T(8,128)}, u32[]{:S(2)}) copy-start(f32[32,32,8]{1,2,0:T(8,128)} %param.19) | copy-start | bytes 98308
  0.7 1.1 %copy-start.8 = (s32[32]{0:T(128)S(1)}, s32[32]{0:T(128)}, u32[]{:S(2)}) copy-start(s32[32]{0:T(128)} %param.16) | copy-start | bytes 388
  0.7 1.1 %copy-start.1 = (f32[9,4096]{1,0:T(8,128)S(1)}, f32[9,4096]{1,0:T(8,128)}, u32[]{:S(2)}) copy-start(f32[9,4096]{1,0:T(8,128)} %refs_7_.1) | copy-start | bytes 442372
  0.7 1.1 %copy-start.6 = (f32[3,4096]{1,0:T(4,128)S(1)}, f32[3,4096]{1,0:T(4,128)}, u32[]{:S(2)}) copy-start(f32[3,4096]{1,0:T(4,128)} %refs_6_.1) | copy-start | bytes 147460
  0.7 1.1 %copy-start.7 = (f32[4096]{0:T(1024)S(1)}, f32[4096]{0:T(1024)}, u32[]{:S(2)}) copy-start(f32[4096]{0:T(1024)} %param.13) | copy-start | bytes 49156
  0.7 1.1 %copy-start = (f32[9,4096]{1,0:T(8,128)S(1)}, f32[9,4096]{1,0:T(8,128)}, u32[]{:S(2)}) copy-start(f32[9,4096]{1,0:T(8,128)} %refs_4_.2) | copy-start | bytes 442372
  0.7 1.1 %copy-start.5 = (f32[3,4096]{1,0:T(4,128)S(1)}, f32[3,4096]{1,0:T(4,128)}, u32[]{:S(2)}) copy-start(f32[3,4096]{1,0:T(4,128)} %refs_3_.1) | copy-start | bytes 147460
  0.7 1.1 %copy-start.4 = (f32[3,4096]{1,0:T(4,128)S(1)}, f32[3,4096]{1,0:T(4,128)}, u32[]{:S(2)}) copy-start(f32[3,4096]{1,0:T(4,128)} %refs_2_.1) | copy-start | bytes 147460
  3.6 3.8 %collective-permute-start = (f32[256,128]{1,0:T(8,128)S(1)}, f32[256,128]{1,0:T(8,128)S(1)}, u32[]{:S(2)}, u32[]{:S(2)}) collective-permute-start(f32[256,128]{1,0:T(8,128)S(1)} %get-tuple-element.35), channel_id=1, source_target_pairs={{0,8},{1,9},{2,10},{3,11},{4,12},{5,13},{6,14},{7,15},{8,0},{9,1},... | collective-permute-start | bytes 393224 | tf_op jit(solution)/shard_map/ppermute | solution.py:502
  4.2 5.5 %collective-permute-start.1 = (f32[80,128]{1,0:T(8,128)S(1)}, f32[80,128]{1,0:T(8,128)S(1)}, u32[]{:S(2)}, u32[]{:S(2)}) collective-permute-start(f32[80,128]{1,0:T(8,128)S(1)} %get-tuple-element.36), channel_id=1, source_target_pairs={{0,1},{1,0},{2,3},{3,2},{4,5},{5,4},{6,7},{7,6},{8,16},{9,17},{10,... | collective-permute-start | bytes 122888 | tf_op jit(solution)/shard_map/ppermute | solution.py:502
  7.5 4.6 %collective-permute-start.3 = (f32[10,16,128]{2,1,0:T(8,128)S(1)}, f32[10,16,128]{2,1,0:T(8,128)S(1)}, u32[]{:S(2)}, u32[]{:S(2)}) collective-permute-start(f32[10,16,128]{2,1,0:T(8,128)S(1)} %pack_z.1), channel_id=1, source_target_pairs={{0,1},{1,0},{2,3},{3,2},{4,5},{5,4},{6,7},{7,6},{8,9},{9,8},{10,11... | collective-permute-start | bytes 245768 | tf_op jit(solution)/shard_map/ppermute | solution.py:502
  8.2 3.9 %collective-permute-start.2 = (f32[16,128]{1,0:T(8,128)S(1)}, f32[16,128]{1,0:T(8,128)S(1)}, u32[]{:S(2)}, u32[]{:S(2)}) collective-permute-start(f32[16,128]{1,0:T(8,128)S(1)} %bitcast.12), channel_id=1, source_target_pairs={{0,1},{1,0},{2,3},{3,2},{4,5},{5,4},{6,7},{7,6},{8,17},{9,16},{10,... | collective-permute-start | bytes 24584 | tf_op jit(solution)/shard_map/ppermute | solution.py:502
  12.2 4.3 %collective-permute-start.4 = (f32[80,128]{1,0:T(8,128)S(1)}, f32[80,128]{1,0:T(8,128)S(1)}, u32[]{:S(2)}, u32[]{:S(2)}) collective-permute-start(f32[80,128]{1,0:T(8,128)S(1)} %get-tuple-element.44), channel_id=1, source_target_pairs={{0,2},{1,3},{2,0},{3,1},{4,6},{5,7},{6,4},{7,5},{8,10},{9,11},{10,... | collective-permute-start | bytes 122888 | tf_op jit(solution)/shard_map/ppermute | solution.py:502
  13.9 2.7 %collective-permute-start.5 = (f32[80,128]{1,0:T(8,128)S(1)}, f32[80,128]{1,0:T(8,128)S(1)}, u32[]{:S(2)}, u32[]{:S(2)}) collective-permute-start(f32[80,128]{1,0:T(8,128)S(1)} %get-tuple-element.45), channel_id=1, source_target_pairs={{0,8},{1,9},{2,4},{3,5},{4,2},{5,3},{6,14},{7,15},{8,0},{9,1},{10,... | collective-permute-start | bytes 122888 | tf_op jit(solution)/shard_map/ppermute | solution.py:502

commit v7 on v6

--- a/solution.py
+++ b/solution.py
@@ -108,6 +108,28 @@
     even = ends[0]
     low, high = low_high(even, ends[1] if len(ends) > 1 else jnp.zeros_like(even), "gz")
     return jnp.concatenate([low, jnp.zeros((ROWS - 32, LANES), F32), high], axis=0)
+
+
+def pack_layers(tiles):
+    row = iota((8, LANES), 0)
+    firsts = [jnp.where(row == 7, pltpu.roll(mine, 7, 0), theirs) for theirs, mine in tiles]
+    pairs = [
+        jnp.where(row < 4, pltpu.roll(odd[1], 4, 0), even[1]) for even, odd in zip(tiles[0::2], tiles[1::2])
+    ]
+    return firsts + pairs
+
+
+def layer_rows(refs, tile):
+    row = iota((8, LANES), 0)
+    planes = []
+    for ref in refs:
+        first, pair = ref[tile], ref[2 * ref.shape[0] // 3 + tile // 2]
+        half = pltpu.roll(pair, 4, 0) if tile % 2 else pair
+        own = jnp.where(row < 7, first, 0.0)
+        halo = jnp.where(row >= 4, half, jnp.where(row == 0, pltpu.roll(first, 1, 0), 0.0))
+        planes.append(jnp.concatenate([own, halo], axis=0))
+    low, high = low_high(planes[0], planes[1] if len(planes) > 1 else jnp.zeros_like(planes[0]), "gz")
+    return jnp.concatenate([low[8:], low[:8], jnp.zeros((ROWS - 32, LANES), F32), high], axis=0)
 
 
 def to_rows(flat_ref, first, array_ref, blocks):
@@ -315,10 +337,14 @@
         tiles = [own_tile(slab_ref, grid_ref, t)[first : first + 16] + extra[t] for t in range(SLABS)]
         ends.append([join_columns(tiles[t], tiles[t + 2]) for t in range(2)])
         ends[-1] += [grid_ref[t, rows, :] for t in range(2, grid_ref.shape[0])]
-    for tile, (lower, upper) in enumerate(zip(*ends)):
-        even_ref[tile] = jnp.where(here, upper, lower)
-        for odd_ref in odd_refs:
-            odd_ref[tile] = jnp.where(here, lower, upper)
+    for up, refs in ((here, (even_ref,)), (jnp.logical_not(here), odd_refs)):
+        for ref in refs:
+            tiles = [
+                (jnp.where(up, upper[8:], lower[:8]), jnp.where(up, upper[:8], lower[8:]))
+                for lower, upper in zip(*ends)
+            ]
+            for at, rows in enumerate(pack_layers(tiles)):
+                ref[at] = rows
 
 
 def x_additions(low, high):
@@ -334,7 +360,7 @@
 def xz_additions(xe_ref, xo_ref, diagonals, layers, tiles):
     odd = xo_ref[...] + diagonal_rows([ref[...] for ref in diagonals])
     extra = x_additions(*low_high(xe_ref[pl.ds(0, ROWS), :], odd, "gx"))
-    joined = [diagonal_rows([ref[t] for ref in layers]) for t in range(2)]
+    joined = [layer_rows(layers, t) for t in range(2)]
     return [extra[t] + joined_columns(joined[t % 2], t >= 2) for t in range(tiles)]
 
 
@@ -397,7 +423,7 @@
     totals = [slab_ref[tile - 2] + extra[tile] for tile in (2, 3)]
     node_gradients(counts, brick, size_z, (2, 3), totals, total_ref, push_slab_ref, drag_slab_ref)
     tiles = inner_tiles(brick)[2:]
-    totals = [grid_ref[t - 2] + diagonal_rows([ref[t - 2] for ref in received[ends:]]) for t in tiles]
+    totals = [grid_ref[t - 2] + layer_rows(received[ends:], t - 2) for t in tiles]
     node_gradients(counts, brick, size_z, tiles, totals, total_ref, push_ref, drag_ref)
     gathered = gather(hot_slab_ref[...], push_slab_ref) + gather(
         hot_ref[:, pl.ds(2 * LANES, push_ref.shape[1])], push_ref
@@ -542,7 +568,7 @@
         deposit_kernel,
         "deposit",
         (
-            f32(2, ROWS, LANES), f32(256, LANES), slab, f32(ends, 16, LANES),
+            f32(2, ROWS, LANES), f32(192, LANES), slab, f32(ends, 16, LANES),
             jax.ShapeDtypeStruct((3, blocks, LANES), jnp.int32), f32(12 * blocks, LANES),
             bf16(16 * blocks, 2 * LANES), bf16(16 * blocks, 2 * LANES),
         ),
@@ -586,8 +612,8 @@
         megabytes=8,
         flops=1_000_000_000,
     )
-    (xo,) = call(keep_kernel, "keep", (slab,), (xo,), flops=700_000_000)
-    send_z = call(pack_z_kernel, "pack_z", (f32(2 + interior, 16, LANES),) * ends, (edge, grid, xe))
+    (xo,) = call(keep_kernel, "keep", (slab,), (xo,), flops=400_000_000)
+    send_z = call(pack_z_kernel, "pack_z", (f32(3 * (2 + interior) // 2, 8, LANES),) * ends, (edge, grid, xe))
     layers = [
         exchange(array, counts, lambda x, y, z: (x, y, paired(z, counts[2], first)))
         for first, array in enumerate(send_z)

time: 18.2 us -> 18.2 us (level)
  waiting for transfers between devices: 3.9 us -> 3.63 us
  starting transfers between devices: 7.34 us -> 7.56 us
    ppermute x6, waiting for transfers between devices: 3.9 us -> 3.63 us  [exchange(): return lax.ppermute(array, names, links) if links else jnp.zeros_like(array)]
    ppermute x6, starting transfers between devices: 7.34 us -> 7.56 us  [exchange(): return lax.ppermute(array, names, links) if links else jnp.zeros_like(array)]
where the time goes in v7:
time: 18.2 us; the launch traced here: 18.1 us
  starting transfers between devices  7.56 us (42%)
  Pallas kernels  5.36 us (29%)
  waiting for transfers between devices  3.63 us (20%)
  between operations  1.48 us (8%)
    ppermute x6, starting transfers between devices, exchange(): return lax.ppermute(array, names, links) if links else jnp.zeros_like(array)  7.56 us
    pallas_call x8, Pallas kernels, call(): pl.pallas_call(kernel, out_shape=out_shape, in_specs=[vmem] * len(operand...  5.36 us
    ppermute x6, waiting for transfers between devices, exchange(): return lax.ppermute(array, names, links) if links else jnp.zeros_like(array)  3.63 us
  transfers between devices with their start and end apart: 6, of which 2 were waited for; matrix products, arithmetic and copies ran while one was open for 0% of the time, Pallas kernels for 8%

profile of v7, /device:TPU:0, one launch (start us, length us, event | category | flops | bytes accessed | tf_op | source)
XLA Modules:
  0.0 18.1 jit_solution(11318390914490996062)
XLA Ops:
  0.6 0.0 copy-start.3
  0.6 0.0 copy-start.2
  0.7 0.0 copy-start.8
  0.7 0.0 copy-start.1
  0.7 0.0 copy-start.6
  0.7 0.0 copy-start.7
  0.7 0.0 copy-start
  0.7 0.0 copy-start.5
  0.7 0.0 copy-start.4
  0.7 0.4 %spread.1 = (bf16[2688,256]{1,0:T(8,128)(2,1)S(1)}, bf16[256,1152]{1,0:T(8,128)(2,1)S(1)}) custom-call(), custom_call_target="tpu_custom_call" | custom-call | flops 20000000000 | bytes 1024 | tf_op jit(solution)/shard_map/spread/pallas_call | solution.py:547
  1.8 0.0 copy-done.3
  1.8 0.0 copy-done.2
  1.8 0.0 copy-done.8
  1.8 0.0 copy-done.1
  1.8 0.0 copy-done.6
  1.8 0.0 copy-done.7
  1.8 0.0 copy-done
  1.8 0.0 copy-done.5
  1.9 0.0 copy-done.4
  1.9 1.8 %deposit.1 = (f32[2,80,128]{2,1,0:T(8,128)S(1)}, f32[192,128]{1,0:T(8,128)S(1)}, f32[80,128]{1,0:T(8,128)S(1)}, f32[1,16,128]{2,1,0:T(8,128)S(1)}, s32[3,32,128]...) custom-call(s32[1,32]{1,0:T(1,128)S(1)} %bitcast.11, ...), custom_call_target="tpu_custom_call" | custom-call | bytes 1024 | tf_op jit(solution)/shard_map/deposit/pallas_call | solution.py:547
  3.6 0.5 %collective-permute-start = (f32[192,128]{1,0:T(8,128)S(1)}, f32[192,128]{1,0:T(8,128)S(1)}, u32[]{:S(2)}, u32[]{:S(2)}) collective-permute-start(f32[192,128]{1,0:T(8,128)S(1)} %get-tuple-element.35), channel_id=1, source_target_pairs={{0,8},{1,9},{2,10},{3,11},{4,12},{5,13},{6,14},{7,15},{8,0},{9,1},... | collective-permute-start | bytes 294920 | tf_op jit(solution)/shard_map/ppermute | solution.py:528
  4.2 2.6 %collective-permute-start.1 = (f32[80,128]{1,0:T(8,128)S(1)}, f32[80,128]{1,0:T(8,128)S(1)}, u32[]{:S(2)}, u32[]{:S(2)}) collective-permute-start(f32[80,128]{1,0:T(8,128)S(1)} %get-tuple-element.36), channel_id=1, source_target_pairs={{0,1},{1,0},{2,3},{3,2},{4,5},{5,4},{6,7},{7,6},{8,16},{9,17},{10,... | collective-permute-start | bytes 122888 | tf_op jit(solution)/shard_map/ppermute | solution.py:528
  6.8 0.6 %interior.1 = (f32[10,80,128]{2,1,0:T(8,128)S(1)}, bf16[512,1280]{1,0:T(8,128)(2,1)S(1)}) custom-call(bf16[512,256]{1,0:T(8,128)(2,1)S(1)} %get-tuple-element.31.window_ref, s32[3,32,128]{2,1,0:T(8,128)S(1)} %get-tuple-element.28.meta_ref.refs_0_, s32[32,32]{1,0:T(8,128)S(1)} %copy-done.3, f32[32,8,32]{2,1,0:T(8,128)S(1)} %bitcast.9), custom_call_target="tpu_custom_call" | custom-call | flops 1000000000 | bytes 1024 | tf_op jit(solution)/shard_map/interior/pallas_call | solution.py:547
  7.4 0.0 collective-permute-done.xe_ref.refs_5_.refs_1_
  7.4 0.1 pack_z.1
  7.5 0.6 %collective-permute-start.3 = (f32[15,8,128]{2,1,0:T(8,128)S(1)}, f32[15,8,128]{2,1,0:T(8,128)S(1)}, u32[]{:S(2)}, u32[]{:S(2)}) collective-permute-start(f32[15,8,128]{2,1,0:T(8,128)S(1)} %pack_z.1), channel_id=1, source_target_pairs={{0,1},{1,0},{2,3},{3,2},{4,5},{5,4},{6,7},{7,6},{8,9},{9,8},{10,11... | collective-permute-start | bytes 184328 | tf_op jit(solution)/shard_map/ppermute | solution.py:528
  8.2 1.5 %collective-permute-start.2 = (f32[16,128]{1,0:T(8,128)S(1)}, f32[16,128]{1,0:T(8,128)S(1)}, u32[]{:S(2)}, u32[]{:S(2)}) collective-permute-start(f32[16,128]{1,0:T(8,128)S(1)} %bitcast.12), channel_id=1, source_target_pairs={{0,1},{1,0},{2,3},{3,2},{4,5},{5,4},{6,7},{7,6},{8,17},{9,16},{10,... | collective-permute-start | bytes 24584 | tf_op jit(solution)/shard_map/ppermute | solution.py:528
  9.6 0.0 collective-permute-done.1.received_ref
  9.6 2.3 %collective-permute-done.2.refs_7_.refs_3_ = f32[16,128]{1,0:T(8,128)S(1)} collective-permute-done((f32[16,128]{1,0:T(8,128)S(1)}, f32[16,128]{1,0:T(8,128)S(1)}, u32[]{:S(2)}, u32[]{:S(2)}) %collective-permute-start.2) | collective-permute-done | bytes 8224 | tf_op jit(solution)/shard_map/ppermute | solution.py:528
  11.9 0.0 collective-permute-done.3.refs_8_.refs_4_
  11.9 0.1 pack_y.1
  12.0 1.6 %collective-permute-start.4 = (f32[80,128]{1,0:T(8,128)S(1)}, f32[80,128]{1,0:T(8,128)S(1)}, u32[]{:S(2)}, u32[]{:S(2)}) collective-permute-start(f32[80,128]{1,0:T(8,128)S(1)} %get-tuple-element.44), channel_id=1, source_target_pairs={{0,2},{1,3},{2,0},{3,1},{4,6},{5,7},{6,4},{7,5},{8,10},{9,11},{10,... | collective-permute-start | bytes 122888 | tf_op jit(solution)/shard_map/ppermute | solution.py:528
  13.7 0.7 %collective-permute-start.5 = (f32[80,128]{1,0:T(8,128)S(1)}, f32[80,128]{1,0:T(8,128)S(1)}, u32[]{:S(2)}, u32[]{:S(2)}) collective-permute-start(f32[80,128]{1,0:T(8,128)S(1)} %get-tuple-element.45), channel_id=1, source_target_pairs={{0,8},{1,9},{2,4},{3,5},{4,2},{5,3},{6,14},{7,15},{8,0},{9,1},{10,... | collective-permute-start | bytes 122888 | tf_op jit(solution)/shard_map/ppermute | solution.py:528
  14.4 0.8 %early.1 = (f32[512,128]{1,0:T(8,128)S(1)}, f32[2,8,128]{2,1,0:T(8,128)S(1)}, f32[8,8,128]{2,1,0:T(8,128)S(1)}, bf16[512,512]{1,0:T(8,128)(2,1)S(1)}) custom-call(s32[3,32,128]{2,1,0:T(8,128)S(1)} %get-tuple-element.28.meta_ref.refs_0_, bf16[512,256]{1,0:T(8,128)(2,1)S(1)} %get-tuple-element.30.refs_1_, bf16[512,1280]{1,0:T(8,128)(2,1)S(1)} %get-tuple-element.32.refs_2_, ...), custom_call_target="tpu_custom_call" | custom-call | flops 1000000000 | bytes 1024 | tf_op jit(solution)/shard_map/early/pallas_call | solution.py:547
  15.2 1.3 %collective-permute-done.4.refs_9_ = f32[80,128]{1,0:T(8,128)S(1)} collective-permute-done((f32[80,128]{1,0:T(8,128)S(1)}, f32[80,128]{1,0:T(8,128)S(1)}, u32[]{:S(2)}, u32[]{:S(2)}) %collective-permute-start.4) | collective-permute-done | bytes 40992 | tf_op jit(solution)/shard_map/ppermute | solution.py:528
  16.5 0.0 collective-permute-done.5.refs_10_
  16.5 1.5 %collect.1 = (f32[3,4096]{1,0:T(4,128)}, f32[9,4096]{1,0:T(8,128)}, f32[32,128]{1,0:T(8,128)}, f32[32,8,32]{2,1,0:T(8,128)}) custom-call(s32[3,32,128]{2,1,0:T(8,128)S(1)} %get-tuple-element.28.meta_ref.refs_0_, f32[384,128]{1,0:T(8,128)S(1)} %get-tuple-element.29.refs_1_, bf16[512,512]{1,0:T(8,128)(2,1)S(1)} %get-tuple-element.38.refs_2_, ...), custom_call_target="tpu_custom_call" | custom-call | bytes 1024 | tf_op jit(solution)/shard_map/collect/pallas_call | solution.py:547
  (1 shorter events, 0.0 us)
Async XLA Ops:
  0.6 1.1 %copy-start.3 = (s32[32,32]{1,0:T(8,128)S(1)}, s32[32,32]{1,0:T(8,128)}, u32[]{:S(2)}) copy-start(s32[32,32]{1,0:T(8,128)} %refs_4_.3) | copy-start | bytes 12292
  0.6 1.1 %copy-start.2 = (f32[32,32,8]{1,2,0:T(8,128)S(1)}, f32[32,32,8]{1,2,0:T(8,128)}, u32[]{:S(2)}) copy-start(f32[32,32,8]{1,2,0:T(8,128)} %param.19) | copy-start | bytes 98308
  0.7 1.1 %copy-start.8 = (s32[32]{0:T(128)S(1)}, s32[32]{0:T(128)}, u32[]{:S(2)}) copy-start(s32[32]{0:T(128)} %param.16) | copy-start | bytes 388
  0.7 1.1 %copy-start.1 = (f32[9,4096]{1,0:T(8,128)S(1)}, f32[9,4096]{1,0:T(8,128)}, u32[]{:S(2)}) copy-start(f32[9,4096]{1,0:T(8,128)} %refs_7_.1) | copy-start | bytes 442372
  0.7 1.1 %copy-start.6 = (f32[3,4096]{1,0:T(4,128)S(1)}, f32[3,4096]{1,0:T(4,128)}, u32[]{:S(2)}) copy-start(f32[3,4096]{1,0:T(4,128)} %refs_6_.1) | copy-start | bytes 147460
  0.7 1.1 %copy-start.7 = (f32[4096]{0:T(1024)S(1)}, f32[4096]{0:T(1024)}, u32[]{:S(2)}) copy-start(f32[4096]{0:T(1024)} %param.13) | copy-start | bytes 49156
  0.7 1.1 %copy-start = (f32[9,4096]{1,0:T(8,128)S(1)}, f32[9,4096]{1,0:T(8,128)}, u32[]{:S(2)}) copy-start(f32[9,4096]{1,0:T(8,128)} %refs_4_.2) | copy-start | bytes 442372
  0.7 1.1 %copy-start.5 = (f32[3,4096]{1,0:T(4,128)S(1)}, f32[3,4096]{1,0:T(4,128)}, u32[]{:S(2)}) copy-start(f32[3,4096]{1,0:T(4,128)} %refs_3_.1) | copy-start | bytes 147460
  0.7 1.1 %copy-start.4 = (f32[3,4096]{1,0:T(4,128)S(1)}, f32[3,4096]{1,0:T(4,128)}, u32[]{:S(2)}) copy-start(f32[3,4096]{1,0:T(4,128)} %refs_2_.1) | copy-start | bytes 147460
  3.6 3.7 %collective-permute-start = (f32[192,128]{1,0:T(8,128)S(1)}, f32[192,128]{1,0:T(8,128)S(1)}, u32[]{:S(2)}, u32[]{:S(2)}) collective-permute-start(f32[192,128]{1,0:T(8,128)S(1)} %get-tuple-element.35), channel_id=1, source_target_pairs={{0,8},{1,9},{2,10},{3,11},{4,12},{5,13},{6,14},{7,15},{8,0},{9,1},... | collective-permute-start | bytes 294920 | tf_op jit(solution)/shard_map/ppermute | solution.py:528
  4.2 5.5 %collective-permute-start.1 = (f32[80,128]{1,0:T(8,128)S(1)}, f32[80,128]{1,0:T(8,128)S(1)}, u32[]{:S(2)}, u32[]{:S(2)}) collective-permute-start(f32[80,128]{1,0:T(8,128)S(1)} %get-tuple-element.36), channel_id=1, source_target_pairs={{0,1},{1,0},{2,3},{3,2},{4,5},{5,4},{6,7},{7,6},{8,16},{9,17},{10,... | collective-permute-start | bytes 122888 | tf_op jit(solution)/shard_map/ppermute | solution.py:528
  7.5 4.4 %collective-permute-start.3 = (f32[15,8,128]{2,1,0:T(8,128)S(1)}, f32[15,8,128]{2,1,0:T(8,128)S(1)}, u32[]{:S(2)}, u32[]{:S(2)}) collective-permute-start(f32[15,8,128]{2,1,0:T(8,128)S(1)} %pack_z.1), channel_id=1, source_target_pairs={{0,1},{1,0},{2,3},{3,2},{4,5},{5,4},{6,7},{7,6},{8,9},{9,8},{10,11... | collective-permute-start | bytes 184328 | tf_op jit(solution)/shard_map/ppermute | solution.py:528
  8.2 3.7 %collective-permute-start.2 = (f32[16,128]{1,0:T(8,128)S(1)}, f32[16,128]{1,0:T(8,128)S(1)}, u32[]{:S(2)}, u32[]{:S(2)}) collective-permute-start(f32[16,128]{1,0:T(8,128)S(1)} %bitcast.12), channel_id=1, source_target_pairs={{0,1},{1,0},{2,3},{3,2},{4,5},{5,4},{6,7},{7,6},{8,17},{9,16},{10,... | collective-permute-start | bytes 24584 | tf_op jit(solution)/shard_map/ppermute | solution.py:528
  12.0 4.5 %collective-permute-start.4 = (f32[80,128]{1,0:T(8,128)S(1)}, f32[80,128]{1,0:T(8,128)S(1)}, u32[]{:S(2)}, u32[]{:S(2)}) collective-permute-start(f32[80,128]{1,0:T(8,128)S(1)} %get-tuple-element.44), channel_id=1, source_target_pairs={{0,2},{1,3},{2,0},{3,1},{4,6},{5,7},{6,4},{7,5},{8,10},{9,11},{10,... | collective-permute-start | bytes 122888 | tf_op jit(solution)/shard_map/ppermute | solution.py:528
  13.7 2.8 %collective-permute-start.5 = (f32[80,128]{1,0:T(8,128)S(1)}, f32[80,128]{1,0:T(8,128)S(1)}, u32[]{:S(2)}, u32[]{:S(2)}) collective-permute-start(f32[80,128]{1,0:T(8,128)S(1)} %get-tuple-element.45), channel_id=1, source_target_pairs={{0,8},{1,9},{2,4},{3,5},{4,2},{5,3},{6,14},{7,15},{8,0},{9,1},{10,... | collective-permute-start | bytes 122888 | tf_op jit(solution)/shard_map/ppermute | solution.py:528

commit v8 on v7

--- a/solution.py
+++ b/solution.py
@@ -632,7 +632,7 @@
         ),
         (meta, hot_edge, hot, edge, grid, xe, xo, *xz, *layers),
         scratch=[
-            pltpu.VMEM((interior, ROWS + 16, LANES), F32),
+            pltpu.VMEM((interior, ROWS + 24, LANES), F32),
             pltpu.VMEM((LANES, 2 * LANES), BF16),
             pltpu.VMEM((LANES, interior * LANES), BF16),
         ],
@@ -645,7 +645,7 @@
         (f32(3, blocks * LANES), f32(9, blocks * LANES), f32(blocks, LANES), f32(brick, size_z, brick)),
         (meta, shape, masked, take, baffle_top, gathered, drag_slab, drag_rows, near_y, ye, yo),
         scratch=[
-            pltpu.VMEM((2, ROWS + 16, LANES), F32),
+            pltpu.VMEM((2, ROWS + 24, LANES), F32),
             pltpu.VMEM((LANES, 4 * LANES), BF16),
             pltpu.VMEM((2, size_z, LANES), F32),
             pltpu.VMEM((9 * blocks, 2 * LANES), BF16),

time: 18.2 us -> 18.2 us (level)
  no operation moved by 1% of the time
where the time goes in v8:
time: 18.2 us; the launch traced here: 18.1 us
  starting transfers between devices  7.56 us (42%)
  Pallas kernels  5.36 us (29%)
  waiting for transfers between devices  3.63 us (20%)
  between operations  1.48 us (8%)
    ppermute x6, starting transfers between devices, exchange(): return lax.ppermute(array, names, links) if links else jnp.zeros_like(array)  7.56 us
    pallas_call x8, Pallas kernels, call(): pl.pallas_call(kernel, out_shape=out_shape, in_specs=[vmem] * len(operand...  5.36 us
    ppermute x6, waiting for transfers between devices, exchange(): return lax.ppermute(array, names, links) if links else jnp.zeros_like(array)  3.63 us
  transfers between devices with their start and end apart: 6, of which 2 were waited for; matrix products, arithmetic and copies ran while one was open for 0% of the time, Pallas kernels for 8%

profile of v8, /device:TPU:0, one launch (start us, length us, event | category | flops | bytes accessed | tf_op | source)
XLA Modules:
  0.0 18.1 jit_solution(16849393332682043274)
XLA Ops:
  0.6 0.0 copy-start.3
  0.6 0.0 copy-start.2
  0.7 0.0 copy-start.8
  0.7 0.0 copy-start.1
  0.7 0.0 copy-start.6
  0.7 0.0 copy-start.7
  0.7 0.0 copy-start
  0.7 0.0 copy-start.5
  0.7 0.0 copy-start.4
  0.7 0.4 %spread.1 = (bf16[2688,256]{1,0:T(8,128)(2,1)S(1)}, bf16[256,1152]{1,0:T(8,128)(2,1)S(1)}) custom-call(), custom_call_target="tpu_custom_call" | custom-call | flops 20000000000 | bytes 1024 | tf_op jit(solution)/shard_map/spread/pallas_call | solution.py:547
  1.8 0.0 copy-done.3
  1.8 0.0 copy-done.2
  1.8 0.0 copy-done.8
  1.8 0.0 copy-done.1
  1.8 0.0 copy-done.6
  1.8 0.0 copy-done.7
  1.8 0.0 copy-done
  1.8 0.0 copy-done.5
  1.9 0.0 copy-done.4
  1.9 1.8 %deposit.1 = (f32[2,80,128]{2,1,0:T(8,128)S(1)}, f32[192,128]{1,0:T(8,128)S(1)}, f32[80,128]{1,0:T(8,128)S(1)}, f32[1,16,128]{2,1,0:T(8,128)S(1)}, s32[3,32,128]...) custom-call(s32[1,32]{1,0:T(1,128)S(1)} %bitcast.11, ...), custom_call_target="tpu_custom_call" | custom-call | bytes 1024 | tf_op jit(solution)/shard_map/deposit/pallas_call | solution.py:547
  3.6 0.5 %collective-permute-start = (f32[192,128]{1,0:T(8,128)S(1)}, f32[192,128]{1,0:T(8,128)S(1)}, u32[]{:S(2)}, u32[]{:S(2)}) collective-permute-start(f32[192,128]{1,0:T(8,128)S(1)} %get-tuple-element.35), channel_id=1, source_target_pairs={{0,8},{1,9},{2,10},{3,11},{4,12},{5,13},{6,14},{7,15},{8,0},{9,1},... | collective-permute-start | bytes 294920 | tf_op jit(solution)/shard_map/ppermute | solution.py:528
  4.2 2.6 %collective-permute-start.1 = (f32[80,128]{1,0:T(8,128)S(1)}, f32[80,128]{1,0:T(8,128)S(1)}, u32[]{:S(2)}, u32[]{:S(2)}) collective-permute-start(f32[80,128]{1,0:T(8,128)S(1)} %get-tuple-element.36), channel_id=1, source_target_pairs={{0,1},{1,0},{2,3},{3,2},{4,5},{5,4},{6,7},{7,6},{8,16},{9,17},{10,... | collective-permute-start | bytes 122888 | tf_op jit(solution)/shard_map/ppermute | solution.py:528
  6.8 0.6 %interior.1 = (f32[10,80,128]{2,1,0:T(8,128)S(1)}, bf16[512,1280]{1,0:T(8,128)(2,1)S(1)}) custom-call(bf16[512,256]{1,0:T(8,128)(2,1)S(1)} %get-tuple-element.31.window_ref, s32[3,32,128]{2,1,0:T(8,128)S(1)} %get-tuple-element.28.meta_ref.refs_0_, s32[32,32]{1,0:T(8,128)S(1)} %copy-done.3, f32[32,8,32]{2,1,0:T(8,128)S(1)} %bitcast.9), custom_call_target="tpu_custom_call" | custom-call | flops 1000000000 | bytes 1024 | tf_op jit(solution)/shard_map/interior/pallas_call | solution.py:547
  7.4 0.0 collective-permute-done.xe_ref.refs_5_.refs_1_
  7.4 0.1 pack_z.1
  7.5 0.6 %collective-permute-start.3 = (f32[15,8,128]{2,1,0:T(8,128)S(1)}, f32[15,8,128]{2,1,0:T(8,128)S(1)}, u32[]{:S(2)}, u32[]{:S(2)}) collective-permute-start(f32[15,8,128]{2,1,0:T(8,128)S(1)} %pack_z.1), channel_id=1, source_target_pairs={{0,1},{1,0},{2,3},{3,2},{4,5},{5,4},{6,7},{7,6},{8,9},{9,8},{10,11... | collective-permute-start | bytes 184328 | tf_op jit(solution)/shard_map/ppermute | solution.py:528
  8.2 1.5 %collective-permute-start.2 = (f32[16,128]{1,0:T(8,128)S(1)}, f32[16,128]{1,0:T(8,128)S(1)}, u32[]{:S(2)}, u32[]{:S(2)}) collective-permute-start(f32[16,128]{1,0:T(8,128)S(1)} %bitcast.12), channel_id=1, source_target_pairs={{0,1},{1,0},{2,3},{3,2},{4,5},{5,4},{6,7},{7,6},{8,17},{9,16},{10,... | collective-permute-start | bytes 24584 | tf_op jit(solution)/shard_map/ppermute | solution.py:528
  9.6 0.0 collective-permute-done.1.received_ref
  9.6 2.3 %collective-permute-done.2.refs_7_.refs_3_ = f32[16,128]{1,0:T(8,128)S(1)} collective-permute-done((f32[16,128]{1,0:T(8,128)S(1)}, f32[16,128]{1,0:T(8,128)S(1)}, u32[]{:S(2)}, u32[]{:S(2)}) %collective-permute-start.2) | collective-permute-done | bytes 8224 | tf_op jit(solution)/shard_map/ppermute | solution.py:528
  11.9 0.0 collective-permute-done.3.refs_8_.refs_4_
  11.9 0.1 pack_y.1
  12.0 1.6 %collective-permute-start.4 = (f32[80,128]{1,0:T(8,128)S(1)}, f32[80,128]{1,0:T(8,128)S(1)}, u32[]{:S(2)}, u32[]{:S(2)}) collective-permute-start(f32[80,128]{1,0:T(8,128)S(1)} %get-tuple-element.44), channel_id=1, source_target_pairs={{0,2},{1,3},{2,0},{3,1},{4,6},{5,7},{6,4},{7,5},{8,10},{9,11},{10,... | collective-permute-start | bytes 122888 | tf_op jit(solution)/shard_map/ppermute | solution.py:528
  13.7 0.7 %collective-permute-start.5 = (f32[80,128]{1,0:T(8,128)S(1)}, f32[80,128]{1,0:T(8,128)S(1)}, u32[]{:S(2)}, u32[]{:S(2)}) collective-permute-start(f32[80,128]{1,0:T(8,128)S(1)} %get-tuple-element.45), channel_id=1, source_target_pairs={{0,8},{1,9},{2,4},{3,5},{4,2},{5,3},{6,14},{7,15},{8,0},{9,1},{10,... | collective-permute-start | bytes 122888 | tf_op jit(solution)/shard_map/ppermute | solution.py:528
  14.4 0.8 %early.1 = (f32[512,128]{1,0:T(8,128)S(1)}, f32[2,8,128]{2,1,0:T(8,128)S(1)}, f32[8,8,128]{2,1,0:T(8,128)S(1)}, bf16[512,512]{1,0:T(8,128)(2,1)S(1)}) custom-call(s32[3,32,128]{2,1,0:T(8,128)S(1)} %get-tuple-element.28.meta_ref.refs_0_, bf16[512,256]{1,0:T(8,128)(2,1)S(1)} %get-tuple-element.30.refs_1_, bf16[512,1280]{1,0:T(8,128)(2,1)S(1)} %get-tuple-element.32.refs_2_, ...), custom_call_target="tpu_custom_call" | custom-call | flops 1000000000 | bytes 1024 | tf_op jit(solution)/shard_map/early/pallas_call | solution.py:547
  15.2 1.3 %collective-permute-done.4.refs_9_ = f32[80,128]{1,0:T(8,128)S(1)} collective-permute-done((f32[80,128]{1,0:T(8,128)S(1)}, f32[80,128]{1,0:T(8,128)S(1)}, u32[]{:S(2)}, u32[]{:S(2)}) %collective-permute-start.4) | collective-permute-done | bytes 40992 | tf_op jit(solution)/shard_map/ppermute | solution.py:528
  16.5 0.0 collective-permute-done.5.refs_10_
  16.5 1.6 %collect.1 = (f32[3,4096]{1,0:T(4,128)}, f32[9,4096]{1,0:T(8,128)}, f32[32,128]{1,0:T(8,128)}, f32[32,8,32]{2,1,0:T(8,128)}) custom-call(s32[3,32,128]{2,1,0:T(8,128)S(1)} %get-tuple-element.28.meta_ref.refs_0_, f32[384,128]{1,0:T(8,128)S(1)} %get-tuple-element.29.refs_1_, bf16[512,512]{1,0:T(8,128)(2,1)S(1)} %get-tuple-element.38.refs_2_, ...), custom_call_target="tpu_custom_call" | custom-call | bytes 1024 | tf_op jit(solution)/shard_map/collect/pallas_call | solution.py:547
  (1 shorter events, 0.0 us)
Async XLA Ops:
  0.6 1.1 %copy-start.3 = (s32[32,32]{1,0:T(8,128)S(1)}, s32[32,32]{1,0:T(8,128)}, u32[]{:S(2)}) copy-start(s32[32,32]{1,0:T(8,128)} %refs_4_.3) | copy-start | bytes 12292
  0.6 1.1 %copy-start.2 = (f32[32,32,8]{1,2,0:T(8,128)S(1)}, f32[32,32,8]{1,2,0:T(8,128)}, u32[]{:S(2)}) copy-start(f32[32,32,8]{1,2,0:T(8,128)} %param.19) | copy-start | bytes 98308
  0.7 1.1 %copy-start.8 = (s32[32]{0:T(128)S(1)}, s32[32]{0:T(128)}, u32[]{:S(2)}) copy-start(s32[32]{0:T(128)} %param.16) | copy-start | bytes 388
  0.7 1.1 %copy-start.1 = (f32[9,4096]{1,0:T(8,128)S(1)}, f32[9,4096]{1,0:T(8,128)}, u32[]{:S(2)}) copy-start(f32[9,4096]{1,0:T(8,128)} %refs_7_.1) | copy-start | bytes 442372
  0.7 1.1 %copy-start.6 = (f32[3,4096]{1,0:T(4,128)S(1)}, f32[3,4096]{1,0:T(4,128)}, u32[]{:S(2)}) copy-start(f32[3,4096]{1,0:T(4,128)} %refs_6_.1) | copy-start | bytes 147460
  0.7 1.1 %copy-start.7 = (f32[4096]{0:T(1024)S(1)}, f32[4096]{0:T(1024)}, u32[]{:S(2)}) copy-start(f32[4096]{0:T(1024)} %param.13) | copy-start | bytes 49156
  0.7 1.1 %copy-start = (f32[9,4096]{1,0:T(8,128)S(1)}, f32[9,4096]{1,0:T(8,128)}, u32[]{:S(2)}) copy-start(f32[9,4096]{1,0:T(8,128)} %refs_4_.2) | copy-start | bytes 442372
  0.7 1.1 %copy-start.5 = (f32[3,4096]{1,0:T(4,128)S(1)}, f32[3,4096]{1,0:T(4,128)}, u32[]{:S(2)}) copy-start(f32[3,4096]{1,0:T(4,128)} %refs_3_.1) | copy-start | bytes 147460
  0.7 1.1 %copy-start.4 = (f32[3,4096]{1,0:T(4,128)S(1)}, f32[3,4096]{1,0:T(4,128)}, u32[]{:S(2)}) copy-start(f32[3,4096]{1,0:T(4,128)} %refs_2_.1) | copy-start | bytes 147460
  3.6 3.7 %collective-permute-start = (f32[192,128]{1,0:T(8,128)S(1)}, f32[192,128]{1,0:T(8,128)S(1)}, u32[]{:S(2)}, u32[]{:S(2)}) collective-permute-start(f32[192,128]{1,0:T(8,128)S(1)} %get-tuple-element.35), channel_id=1, source_target_pairs={{0,8},{1,9},{2,10},{3,11},{4,12},{5,13},{6,14},{7,15},{8,0},{9,1},... | collective-permute-start | bytes 294920 | tf_op jit(solution)/shard_map/ppermute | solution.py:528
  4.2 5.5 %collective-permute-start.1 = (f32[80,128]{1,0:T(8,128)S(1)}, f32[80,128]{1,0:T(8,128)S(1)}, u32[]{:S(2)}, u32[]{:S(2)}) collective-permute-start(f32[80,128]{1,0:T(8,128)S(1)} %get-tuple-element.36), channel_id=1, source_target_pairs={{0,1},{1,0},{2,3},{3,2},{4,5},{5,4},{6,7},{7,6},{8,16},{9,17},{10,... | collective-permute-start | bytes 122888 | tf_op jit(solution)/shard_map/ppermute | solution.py:528
  7.5 4.4 %collective-permute-start.3 = (f32[15,8,128]{2,1,0:T(8,128)S(1)}, f32[15,8,128]{2,1,0:T(8,128)S(1)}, u32[]{:S(2)}, u32[]{:S(2)}) collective-permute-start(f32[15,8,128]{2,1,0:T(8,128)S(1)} %pack_z.1), channel_id=1, source_target_pairs={{0,1},{1,0},{2,3},{3,2},{4,5},{5,4},{6,7},{7,6},{8,9},{9,8},{10,11... | collective-permute-start | bytes 184328 | tf_op jit(solution)/shard_map/ppermute | solution.py:528
  8.2 3.7 %collective-permute-start.2 = (f32[16,128]{1,0:T(8,128)S(1)}, f32[16,128]{1,0:T(8,128)S(1)}, u32[]{:S(2)}, u32[]{:S(2)}) collective-permute-start(f32[16,128]{1,0:T(8,128)S(1)} %bitcast.12), channel_id=1, source_target_pairs={{0,1},{1,0},{2,3},{3,2},{4,5},{5,4},{6,7},{7,6},{8,17},{9,16},{10,... | collective-permute-start | bytes 24584 | tf_op jit(solution)/shard_map/ppermute | solution.py:528
  12.0 4.5 %collective-permute-start.4 = (f32[80,128]{1,0:T(8,128)S(1)}, f32[80,128]{1,0:T(8,128)S(1)}, u32[]{:S(2)}, u32[]{:S(2)}) collective-permute-start(f32[80,128]{1,0:T(8,128)S(1)} %get-tuple-element.44), channel_id=1, source_target_pairs={{0,2},{1,3},{2,0},{3,1},{4,6},{5,7},{6,4},{7,5},{8,10},{9,11},{10,... | collective-permute-start | bytes 122888 | tf_op jit(solution)/shard_map/ppermute | solution.py:528
  13.7 2.8 %collective-permute-start.5 = (f32[80,128]{1,0:T(8,128)S(1)}, f32[80,128]{1,0:T(8,128)S(1)}, u32[]{:S(2)}, u32[]{:S(2)}) collective-permute-start(f32[80,128]{1,0:T(8,128)S(1)} %get-tuple-element.45), channel_id=1, source_target_pairs={{0,8},{1,9},{2,4},{3,5},{4,2},{5,3},{6,14},{7,15},{8,0},{9,1},{10,... | collective-permute-start | bytes 122888 | tf_op jit(solution)/shard_map/ppermute | solution.py:528

commit v9 on v8

--- a/solution.py
+++ b/solution.py
@@ -166,13 +166,7 @@
     return lower, upper
 
 
-def spread_kernel(spread_ref, take_ref):
-    particle = iota((LANES, 2 * LANES), 0)
-    shift = iota((LANES, 2 * LANES), 1) - ((particle >> 5) * 64 + ((particle >> 3) & 3) * 8)
-    for c in range(7):
-        for oz in range(3):
-            hit = shift == oz * 8 + c
-            spread_ref[pl.ds((3 * c + oz) * LANES, LANES), :] = jnp.where(hit, 1.0, 0.0).astype(BF16)
+def fill_take(take_ref):
     key = iota((2 * LANES, LANES), 0)
     particle = iota((2 * LANES, LANES), 1)
     shift = jnp.where((key >> 6) == (particle >> 5), (key & 31) - ((particle >> 3) & 3), -64)
@@ -180,6 +174,15 @@
         for oz in range(3):
             hit = shift == 8 * a + oz
             take_ref[:, pl.ds((3 * a + oz) * LANES, LANES)] = jnp.where(hit, 1.0, 0.0).astype(BF16)
+
+
+def spread_kernel(spread_ref):
+    particle = iota((LANES, 2 * LANES), 0)
+    shift = iota((LANES, 2 * LANES), 1) - ((particle >> 5) * 64 + ((particle >> 3) & 3) * 8)
+    for c in range(7):
+        for oz in range(3):
+            hit = shift == oz * 8 + c
+            spread_ref[pl.ds((3 * c + oz) * LANES, LANES), :] = jnp.where(hit, 1.0, 0.0).astype(BF16)
 
 
 def deposit_kernel(*refs):
@@ -415,9 +418,10 @@
 
 
 def early_kernel(counts, ends, size_z, *refs):
-    inputs, refs = refs[:-7], refs[-7:]
+    inputs, refs = refs[:-8], refs[-8:]
     meta_ref, hot_slab_ref, hot_ref, slab_ref, grid_ref, xe_ref, xo_ref, *received = inputs
-    gathered_ref, drag_slab_ref, drag_ref, masked_ref, total_ref, push_slab_ref, push_ref = refs
+    gathered_ref, drag_slab_ref, drag_ref, masked_ref, take_ref, total_ref, push_slab_ref, push_ref = refs
+    fill_take(take_ref)
     brick = 4 * (grid_ref.shape[0] - 2)
     extra = xz_additions(xe_ref, xo_ref, received[:ends], received[ends:], SLABS)
     totals = [slab_ref[tile - 2] + extra[tile] for tile in (2, 3)]
@@ -561,9 +565,7 @@
     )
     slab = f32(ROWS, LANES)
     ends = 2 if counts[2] > 2 else 1
-    spread, take = call(
-        spread_kernel, "spread", (bf16(21 * LANES, 2 * LANES), bf16(2 * LANES, 9 * LANES)), (), flops=20_000_000_000
-    )
+    (spread,) = call(spread_kernel, "spread", (bf16(21 * LANES, 2 * LANES),), (), flops=20_000_000_000)
     edge, send_xe, send_xo, send_xz, meta, shape, window, hot_edge = call(
         deposit_kernel,
         "deposit",
@@ -623,12 +625,12 @@
     )
     yo = exchange(send_yo, counts, odd_y)
     ye = exchange(send_ye, counts, lambda x, y, z: (x, paired(y, counts[1], 0), z))
-    gathered, drag_slab, drag_rows, masked = call(
+    gathered, drag_slab, drag_rows, masked, take = call(
         functools.partial(early_kernel, counts, ends, size_z),
         "early",
         (
             f32(16 * blocks, LANES), f32(2, size_z, LANES), f32(interior, size_z, LANES),
-            bf16(16 * blocks, 4 * LANES),
+            bf16(16 * blocks, 4 * LANES), bf16(2 * LANES, 9 * LANES),
         ),
         (meta, hot_edge, hot, edge, grid, xe, xo, *xz, *layers),
         scratch=[

time: 18.2 us -> 18.2 us (level)
  waiting for transfers between devices: 3.63 us -> 3.43 us
    ppermute x6, waiting for transfers between devices: 3.63 us -> 3.43 us  [exchange(): return lax.ppermute(array, names, links) if links else jnp.zeros_like(array)]
  transfers between devices with their start and end apart: 6 -> 6, of which waited for: 2 -> 2; matrix products, arithmetic and copies ran while one was open for 0% -> 0% of each run, Pallas kernels for 8% -> 10%
where the time goes in v9:
time: 18.2 us; the launch traced here: 18 us
  starting transfers between devices  7.56 us (42%)
  Pallas kernels  5.41 us (30%)
  waiting for transfers between devices  3.43 us (19%)
  between operations  1.48 us (8%)
    ppermute x6, starting transfers between devices, exchange(): return lax.ppermute(array, names, links) if links else jnp.zeros_like(array)  7.56 us
    pallas_call x8, Pallas kernels, call(): pl.pallas_call(kernel, out_shape=out_shape, in_specs=[vmem] * len(operand...  5.41 us
    ppermute x6, waiting for transfers between devices, exchange(): return lax.ppermute(array, names, links) if links else jnp.zeros_like(array)  3.43 us
  transfers between devices with their start and end apart: 6, of which 2 were waited for; matrix products, arithmetic and copies ran while one was open for 0% of the time, Pallas kernels for 10%

profile of v9, /device:TPU:0, one launch (start us, length us, event | category | flops | bytes accessed | tf_op | source)
XLA Modules:
  0.0 18.0 jit_solution(17431757934968243823)
XLA Ops:
  0.6 0.0 copy-start.3
  0.6 0.0 copy-start.2
  0.7 0.0 copy-start.8
  0.7 0.0 copy-start.1
  0.7 0.0 copy-start.6
  0.7 0.0 copy-start.7
  0.7 0.0 copy-start
  0.7 0.0 copy-start.5
  0.7 0.0 copy-start.4
  0.7 0.2 %spread.1.refs_10_ = bf16[2688,256]{1,0:T(8,128)(2,1)S(1)} custom-call(), custom_call_target="tpu_custom_call" | custom-call | flops 20000000000 | bytes 1024 | tf_op jit(solution)/shard_map/spread/pallas_call | solution.py:551
  1.7 0.0 copy-done.3
  1.7 0.0 copy-done.2
  1.7 0.0 copy-done.8
  1.7 0.0 copy-done.1
  1.7 0.0 copy-done.6
  1.7 0.0 copy-done.7
  1.7 0.1 copy-done
  1.8 0.0 copy-done.5
  1.8 0.0 copy-done.4
  1.8 1.8 %deposit.1 = (f32[2,80,128]{2,1,0:T(8,128)S(1)}, f32[192,128]{1,0:T(8,128)S(1)}, f32[80,128]{1,0:T(8,128)S(1)}, f32[1,16,128]{2,1,0:T(8,128)S(1)}, s32[3,32,128]...) custom-call(s32[1,32]{1,0:T(1,128)S(1)} %bitcast.11, ...), custom_call_target="tpu_custom_call" | custom-call | bytes 1024 | tf_op jit(solution)/shard_map/deposit/pallas_call | solution.py:551
  3.6 0.5 %collective-permute-start = (f32[192,128]{1,0:T(8,128)S(1)}, f32[192,128]{1,0:T(8,128)S(1)}, u32[]{:S(2)}, u32[]{:S(2)}) collective-permute-start(f32[192,128]{1,0:T(8,128)S(1)} %get-tuple-element.33), channel_id=1, source_target_pairs={{0,8},{1,9},{2,10},{3,11},{4,12},{5,13},{6,14},{7,15},{8,0},{9,1},... | collective-permute-start | bytes 294920 | tf_op jit(solution)/shard_map/ppermute | solution.py:532
  4.1 2.6 %collective-permute-start.1 = (f32[80,128]{1,0:T(8,128)S(1)}, f32[80,128]{1,0:T(8,128)S(1)}, u32[]{:S(2)}, u32[]{:S(2)}) collective-permute-start(f32[80,128]{1,0:T(8,128)S(1)} %get-tuple-element.34), channel_id=1, source_target_pairs={{0,1},{1,0},{2,3},{3,2},{4,5},{5,4},{6,7},{7,6},{8,16},{9,17},{10,... | collective-permute-start | bytes 122888 | tf_op jit(solution)/shard_map/ppermute | solution.py:532
  6.7 0.6 %interior.1 = (f32[10,80,128]{2,1,0:T(8,128)S(1)}, bf16[512,1280]{1,0:T(8,128)(2,1)S(1)}) custom-call(bf16[512,256]{1,0:T(8,128)(2,1)S(1)} %get-tuple-element.29.window_ref, s32[3,32,128]{2,1,0:T(8,128)S(1)} %get-tuple-element.26.meta_ref.refs_0_, s32[32,32]{1,0:T(8,128)S(1)} %copy-done.3, f32[32,8,32]{2,1,0:T(8,128)S(1)} %bitcast.9), custom_call_target="tpu_custom_call" | custom-call | flops 1000000000 | bytes 1024 | tf_op jit(solution)/shard_map/interior/pallas_call | solution.py:551
  7.4 0.0 collective-permute-done.xe_ref.refs_5_.refs_1_
  7.4 0.1 pack_z.1
  7.5 0.6 %collective-permute-start.3 = (f32[15,8,128]{2,1,0:T(8,128)S(1)}, f32[15,8,128]{2,1,0:T(8,128)S(1)}, u32[]{:S(2)}, u32[]{:S(2)}) collective-permute-start(f32[15,8,128]{2,1,0:T(8,128)S(1)} %pack_z.1), channel_id=1, source_target_pairs={{0,1},{1,0},{2,3},{3,2},{4,5},{5,4},{6,7},{7,6},{8,9},{9,8},{10,11... | collective-permute-start | bytes 184328 | tf_op jit(solution)/shard_map/ppermute | solution.py:532
  8.1 1.5 %collective-permute-start.2 = (f32[16,128]{1,0:T(8,128)S(1)}, f32[16,128]{1,0:T(8,128)S(1)}, u32[]{:S(2)}, u32[]{:S(2)}) collective-permute-start(f32[16,128]{1,0:T(8,128)S(1)} %bitcast.12), channel_id=1, source_target_pairs={{0,1},{1,0},{2,3},{3,2},{4,5},{5,4},{6,7},{7,6},{8,17},{9,16},{10,... | collective-permute-start | bytes 24584 | tf_op jit(solution)/shard_map/ppermute | solution.py:532
  9.6 0.0 collective-permute-done.1.received_ref
  9.6 2.3 %collective-permute-done.2.refs_7_.refs_3_ = f32[16,128]{1,0:T(8,128)S(1)} collective-permute-done((f32[16,128]{1,0:T(8,128)S(1)}, f32[16,128]{1,0:T(8,128)S(1)}, u32[]{:S(2)}, u32[]{:S(2)}) %collective-permute-start.2) | collective-permute-done | bytes 8224 | tf_op jit(solution)/shard_map/ppermute | solution.py:532
  11.9 0.0 collective-permute-done.3.refs_8_.refs_4_
  11.9 0.1 pack_y.1
  12.0 1.6 %collective-permute-start.4 = (f32[80,128]{1,0:T(8,128)S(1)}, f32[80,128]{1,0:T(8,128)S(1)}, u32[]{:S(2)}, u32[]{:S(2)}) collective-permute-start(f32[80,128]{1,0:T(8,128)S(1)} %get-tuple-element.42), channel_id=1, source_target_pairs={{0,2},{1,3},{2,0},{3,1},{4,6},{5,7},{6,4},{7,5},{8,10},{9,11},{10,... | collective-permute-start | bytes 122888 | tf_op jit(solution)/shard_map/ppermute | solution.py:532
  13.6 0.7 %collective-permute-start.5 = (f32[80,128]{1,0:T(8,128)S(1)}, f32[80,128]{1,0:T(8,128)S(1)}, u32[]{:S(2)}, u32[]{:S(2)}) collective-permute-start(f32[80,128]{1,0:T(8,128)S(1)} %get-tuple-element.43), channel_id=1, source_target_pairs={{0,8},{1,9},{2,4},{3,5},{4,2},{5,3},{6,14},{7,15},{8,0},{9,1},{10,... | collective-permute-start | bytes 122888 | tf_op jit(solution)/shard_map/ppermute | solution.py:532
  14.3 1.0 %early.1 = (f32[512,128]{1,0:T(8,128)S(1)}, f32[2,8,128]{2,1,0:T(8,128)S(1)}, f32[8,8,128]{2,1,0:T(8,128)S(1)}, bf16[512,512]{1,0:T(8,128)(2,1)S(1)}, bf16[256,1152]{1,0:T(8,128)(2,1)S(1)}) custom-call(s32[3,32,128]{2,1,0:T(8,128)S(1)} %get-tuple-element.26.meta_ref.refs_0_, bf16[512,256]{1,0:T(8,128)(2,1)S(1)} %get-tuple-element.28.refs_1_, ...), custom_call_target="tpu_custom_call" | custom-call | flops 1000000000 | bytes 1024 | tf_op jit(solution)/shard_map/early/pallas_call | solution.py:551
  15.3 1.1 %collective-permute-done.4.refs_9_ = f32[80,128]{1,0:T(8,128)S(1)} collective-permute-done((f32[80,128]{1,0:T(8,128)S(1)}, f32[80,128]{1,0:T(8,128)S(1)}, u32[]{:S(2)}, u32[]{:S(2)}) %collective-permute-start.4) | collective-permute-done | bytes 40992 | tf_op jit(solution)/shard_map/ppermute | solution.py:532
  16.5 0.0 collective-permute-done.5.refs_10_
  16.5 1.6 %collect.1 = (f32[3,4096]{1,0:T(4,128)}, f32[9,4096]{1,0:T(8,128)}, f32[32,128]{1,0:T(8,128)}, f32[32,8,32]{2,1,0:T(8,128)}) custom-call(s32[3,32,128]{2,1,0:T(8,128)S(1)} %get-tuple-element.26.meta_ref.refs_0_, f32[384,128]{1,0:T(8,128)S(1)} %get-tuple-element.27.refs_1_, bf16[512,512]{1,0:T(8,128)(2,1)S(1)} %get-tuple-element.36.refs_2_, ...), custom_call_target="tpu_custom_call" | custom-call | bytes 1024 | tf_op jit(solution)/shard_map/collect/pallas_call | solution.py:551
  (1 shorter events, 0.0 us)
Async XLA Ops:
  0.6 1.0 %copy-start.3 = (s32[32,32]{1,0:T(8,128)S(1)}, s32[32,32]{1,0:T(8,128)}, u32[]{:S(2)}) copy-start(s32[32,32]{1,0:T(8,128)} %refs_4_.3) | copy-start | bytes 12292
  0.6 1.0 %copy-start.2 = (f32[32,32,8]{1,2,0:T(8,128)S(1)}, f32[32,32,8]{1,2,0:T(8,128)}, u32[]{:S(2)}) copy-start(f32[32,32,8]{1,2,0:T(8,128)} %param.19) | copy-start | bytes 98308
  0.7 1.0 %copy-start.8 = (s32[32]{0:T(128)S(1)}, s32[32]{0:T(128)}, u32[]{:S(2)}) copy-start(s32[32]{0:T(128)} %param.16) | copy-start | bytes 388
  0.7 1.0 %copy-start.1 = (f32[9,4096]{1,0:T(8,128)S(1)}, f32[9,4096]{1,0:T(8,128)}, u32[]{:S(2)}) copy-start(f32[9,4096]{1,0:T(8,128)} %refs_7_.1) | copy-start | bytes 442372
  0.7 1.0 %copy-start.6 = (f32[3,4096]{1,0:T(4,128)S(1)}, f32[3,4096]{1,0:T(4,128)}, u32[]{:S(2)}) copy-start(f32[3,4096]{1,0:T(4,128)} %refs_6_.1) | copy-start | bytes 147460
  0.7 1.0 %copy-start.7 = (f32[4096]{0:T(1024)S(1)}, f32[4096]{0:T(1024)}, u32[]{:S(2)}) copy-start(f32[4096]{0:T(1024)} %param.13) | copy-start | bytes 49156
  0.7 1.1 %copy-start = (f32[9,4096]{1,0:T(8,128)S(1)}, f32[9,4096]{1,0:T(8,128)}, u32[]{:S(2)}) copy-start(f32[9,4096]{1,0:T(8,128)} %refs_4_.2) | copy-start | bytes 442372
  0.7 1.1 %copy-start.5 = (f32[3,4096]{1,0:T(4,128)S(1)}, f32[3,4096]{1,0:T(4,128)}, u32[]{:S(2)}) copy-start(f32[3,4096]{1,0:T(4,128)} %refs_3_.1) | copy-start | bytes 147460
  0.7 1.1 %copy-start.4 = (f32[3,4096]{1,0:T(4,128)S(1)}, f32[3,4096]{1,0:T(4,128)}, u32[]{:S(2)}) copy-start(f32[3,4096]{1,0:T(4,128)} %refs_2_.1) | copy-start | bytes 147460
  3.6 3.8 %collective-permute-start = (f32[192,128]{1,0:T(8,128)S(1)}, f32[192,128]{1,0:T(8,128)S(1)}, u32[]{:S(2)}, u32[]{:S(2)}) collective-permute-start(f32[192,128]{1,0:T(8,128)S(1)} %get-tuple-element.33), channel_id=1, source_target_pairs={{0,8},{1,9},{2,10},{3,11},{4,12},{5,13},{6,14},{7,15},{8,0},{9,1},... | collective-permute-start | bytes 294920 | tf_op jit(solution)/shard_map/ppermute | solution.py:532
  4.1 5.5 %collective-permute-start.1 = (f32[80,128]{1,0:T(8,128)S(1)}, f32[80,128]{1,0:T(8,128)S(1)}, u32[]{:S(2)}, u32[]{:S(2)}) collective-permute-start(f32[80,128]{1,0:T(8,128)S(1)} %get-tuple-element.34), channel_id=1, source_target_pairs={{0,1},{1,0},{2,3},{3,2},{4,5},{5,4},{6,7},{7,6},{8,16},{9,17},{10,... | collective-permute-start | bytes 122888 | tf_op jit(solution)/shard_map/ppermute | solution.py:532
  7.5 4.4 %collective-permute-start.3 = (f32[15,8,128]{2,1,0:T(8,128)S(1)}, f32[15,8,128]{2,1,0:T(8,128)S(1)}, u32[]{:S(2)}, u32[]{:S(2)}) collective-permute-start(f32[15,8,128]{2,1,0:T(8,128)S(1)} %pack_z.1), channel_id=1, source_target_pairs={{0,1},{1,0},{2,3},{3,2},{4,5},{5,4},{6,7},{7,6},{8,9},{9,8},{10,11... | collective-permute-start | bytes 184328 | tf_op jit(solution)/shard_map/ppermute | solution.py:532
  8.1 3.7 %collective-permute-start.2 = (f32[16,128]{1,0:T(8,128)S(1)}, f32[16,128]{1,0:T(8,128)S(1)}, u32[]{:S(2)}, u32[]{:S(2)}) collective-permute-start(f32[16,128]{1,0:T(8,128)S(1)} %bitcast.12), channel_id=1, source_target_pairs={{0,1},{1,0},{2,3},{3,2},{4,5},{5,4},{6,7},{7,6},{8,17},{9,16},{10,... | collective-permute-start | bytes 24584 | tf_op jit(solution)/shard_map/ppermute | solution.py:532
  12.0 4.5 %collective-permute-start.4 = (f32[80,128]{1,0:T(8,128)S(1)}, f32[80,128]{1,0:T(8,128)S(1)}, u32[]{:S(2)}, u32[]{:S(2)}) collective-permute-start(f32[80,128]{1,0:T(8,128)S(1)} %get-tuple-element.42), channel_id=1, source_target_pairs={{0,2},{1,3},{2,0},{3,1},{4,6},{5,7},{6,4},{7,5},{8,10},{9,11},{10,... | collective-permute-start | bytes 122888 | tf_op jit(solution)/shard_map/ppermute | solution.py:532
  13.6 2.8 %collective-permute-start.5 = (f32[80,128]{1,0:T(8,128)S(1)}, f32[80,128]{1,0:T(8,128)S(1)}, u32[]{:S(2)}, u32[]{:S(2)}) collective-permute-start(f32[80,128]{1,0:T(8,128)S(1)} %get-tuple-element.43), channel_id=1, source_target_pairs={{0,8},{1,9},{2,4},{3,5},{4,2},{5,3},{6,14},{7,15},{8,0},{9,1},{10,... | collective-permute-start | bytes 122888 | tf_op jit(solution)/shard_map/ppermute | solution.py:532
